TPU v7x, 32 devices: a whole 2x2x4 slice. The times are simulated.
32 devices in a mesh: blk: 4 (over y, core), dp: 8 (over z, x).
Axes of the slice: x: 2, y: 2, z: 4, core: 2. Of those that a mesh axis runs over, the one named last changes fastest.
Arguments:
- tokens: bfloat16 [8, 1024, 384], P('dp', 'blk'), may hold values from -6 to 6
- lengths: int32 [8], P('dp'), may hold values from 512 to 1024, as said below
- query_weight: bfloat16 [384, 384], replicated, may hold values from -0.3125 to 0.3125
- query_bias: bfloat16 [384], replicated, may hold values from -1.5 to 1.5
- key_weight: bfloat16 [384, 384], replicated, may hold values from -0.3125 to 0.3125
- key_bias: bfloat16 [384], replicated, may hold values from -1.5 to 1.5
- value_weight: bfloat16 [384, 384], replicated, may hold values from -0.3125 to 0.3125
- value_bias: bfloat16 [384], replicated, may hold values from -1.5 to 1.5
- output_weight: bfloat16 [384, 384], replicated, may hold values from -2.5 to 2.5
- output_bias: bfloat16 [384], replicated, may hold values from -1.5 to 1.5
- first_gain: bfloat16 [384], replicated, may hold values from 0.5 to 1.5
- first_bias: bfloat16 [384], replicated, may hold values from -1.5 to 1.5
- inner_weight: bfloat16 [384, 1536], replicated, may hold values from -0.3125 to 0.3125
- inner_bias: bfloat16 [1536], replicated, may hold values from -1.5 to 1.5
- outer_weight: bfloat16 [1536, 384], replicated, may hold values from -0.15625 to 0.15625
- outer_bias: bfloat16 [384], replicated, may hold values from -1.5 to 1.5
- second_gain: bfloat16 [384], replicated, may hold values from 0.5 to 1.5
- second_bias: bfloat16 [384], replicated, may hold values from -1.5 to 1.5
- relative_table: bfloat16 [512, 384], replicated, may hold values from -6 to 6
- cotangent: bfloat16 [8, 1024, 384], P('dp', 'blk'), may hold values from -18 to 18
Outputs:
- layer_out: float32 [8, 1024, 384], P('dp', 'blk')
- grad_tokens: float32 [8, 1024, 384], P('dp', 'blk')
- grad_query_weight: float32 [384, 384], replicated
- grad_query_bias: float32 [384], replicated
- grad_key_weight: float32 [384, 384], replicated
- grad_key_bias: float32 [384], replicated
- grad_value_weight: float32 [384, 384], replicated
- grad_value_bias: float32 [384], replicated
- grad_output_weight: float32 [384, 384], replicated
- grad_output_bias: float32 [384], replicated
- grad_first_gain: float32 [384], replicated
- grad_first_bias: float32 [384], replicated
- grad_inner_weight: float32 [384, 1536], replicated
- grad_inner_bias: float32 [1536], replicated
- grad_outer_weight: float32 [1536, 384], replicated
- grad_outer_bias: float32 [384], replicated
- grad_second_gain: float32 [384], replicated
- grad_second_bias: float32 [384], replicated
- grad_relative_table: float32 [512, 384], replicated
Inputs may be any that keep to these rules, and one draw needn't show every extreme that they name: `lengths`: one sequence uses all 1024 positions and one uses 1024 // 2.
All inputs are finite; a program needn't handle non-finite values.
Results may differ from a plain program's by a relative error of at most 0.04.
Values may be sent and summed in bfloat16 or wider, within the bound.
No kernel may reach another device: no remote copies, remote signals or barrier semaphores. Data moves between devices by JAX's collectives and lax.ppermute only.
A program may use at most 320 MiB of HBM per device.

v0:
```python
import math

import jax
import jax.numpy as jnp
from jax import lax
from jax.experimental import pallas as pl
from jax.experimental.pallas import tpu as pltpu
from jax.sharding import PartitionSpec as P

HEADS = 6
BF = jnp.bfloat16
F32 = jnp.float32
LOG2E = math.log2(math.e)
EPS = 1e-07
MIB = 1024 * 1024
EARLY_ROWS = 3584
LATE_ROWS = 1792


def nn(left, right):
    return lax.dot_general(left, right, (((1,), (0,)), ((), ())), preferred_element_type=F32)


def nt(left, right):
    return lax.dot_general(left, right, (((1,), (1,)), ((), ())), preferred_element_type=F32)


def tn(left, right):
    return lax.dot_general(left, right, (((0,), (0,)), ((), ())), preferred_element_type=F32)


def tt(left, right):
    return lax.dot_general(left, right, (((0,), (1,)), ((), ())), preferred_element_type=F32)


def lanes(shape):
    return lax.broadcasted_iota(jnp.int32, shape, len(shape) - 1)


def of_head(values, head):
    inside = (lanes(values.shape) // 64) == head
    return jnp.where(inside, values, jnp.zeros_like(values))


def stacked(values):
    return jnp.concatenate([of_head(values, 0), of_head(values, 1)], axis=0)


def abreast(values):
    rows = values.shape[0] // 2
    return jnp.concatenate([values[:rows], values[rows:]], axis=1)


def pair_columns(pair):
    if isinstance(pair, int):
        return slice(pair * 128, (pair + 1) * 128)
    return pl.ds(pl.multiple_of(pair * 128, 128), 128)


def wide(column, width):
    return jnp.broadcast_to(column, (column.shape[0], width))


def reversal(size):
    rows = lax.broadcasted_iota(jnp.int32, (size, size), 0)
    cols = lax.broadcasted_iota(jnp.int32, (size, size), 1)
    return jnp.where(rows + cols == size - 1, 1.0, 0.0).astype(BF)


def placed(block, size, own, core, far, diagonal):
    even = block % 2 == 0
    core_at = pl.multiple_of(jnp.where(even, 2 * size, 0), size)
    diagonal_at = pl.multiple_of(jnp.where(even, 0, 2 * size), size)
    return (size, own), (3 * size, far), (core_at, core), (diagonal_at, diagonal)


def rolled_window(source, shift):
    half = source.shape[0] // 2
    upper = pltpu.roll(source[:half, half:], shift, 1, stride=1, stride_axis=0)[:, half:]
    lower = pltpu.roll(source[half:, : 3 * half], shift, 1, stride=1, stride_axis=0)[:, half:]
    return jnp.concatenate([upper, lower], axis=0)


def own_terms(block, s_ref, own_rows, own_table, shift):
    size = own_rows.shape[0] // 2
    rel = own_table.shape[0]
    scores = nt(own_rows, own_table)
    last, first = scores[:, rel - 1 : rel], scores[:, 0:1]
    source = jnp.concatenate([scores, wide(last, size), wide(first, size)], axis=1)
    for side in range(2):
        rows = slice(side * size, (side + 1) * size)
        s_ref[rows, : 3 * size] = pltpu.roll(source[rows], shift, 1, stride=1, stride_axis=0)[:, : 3 * size]
    s_ref[:, 3 * size :] = wide(jnp.where(block < 2, last, first), size)


def other_terms(block, s_ref, others, tables, shift, slots):
    size = s_ref.shape[0] // 2
    rel = tables.shape[0] // 2

    def both(start, rows):
        return jnp.concatenate([tables[start : start + rows], tables[rel + start : rel + start + rows]], axis=0)

    def near(slot):
        if slot == 1:
            product = nt(others(slot), tables)
            parts = [product[:, :rel], product[:, rel:]]
        else:
            product = nt(others(slot), both(size if slot == 0 else 0, size))
            parts = [product[:, :size], product[:, size:]]
        if slot == 0:
            parts = [jnp.concatenate([part, wide(part[:, size - 1 : size], size)], axis=1) for part in parts]
        elif slot == 2:
            parts = [jnp.concatenate([wide(part[:, 0:1], size), part], axis=1) for part in parts]
        return [rolled_window(part, shift).T for part in parts]

    def constant(slot):
        rows = others(slot)
        top = nt(both(0, 16), rows)
        bottom = nt(both(rel - 16, 16), rows)
        return [
            s_ref[side * size : (side + 1) * size, 3 * size :]
            + jnp.where(block < 2, top[16 * side : 16 * side + 1], bottom[16 * side + 15 : 16 * side + 16])
            for side in range(2)
        ]

    for slot in slots:
        span = slice(slot * size, (slot + 1) * size)
        terms = near(slot) if slot < 3 else None
        fixed = constant(slot) if slot != 1 else None
        past = block == (0 if slot == 0 else 3)
        for side in range(2):
            rows = slice(side * size, (side + 1) * size)
            if slot == 1:
                s_ref[rows, span] += terms[side]
            elif slot == 3:
                s_ref[rows, span] = fixed[side]
            else:
                s_ref[rows, span] = jnp.where(past, fixed[side], s_ref[rows, span] + terms[side])


def extend_table(ext_ref, table_ref):
    rel = table_ref.shape[0]
    half = rel // 2
    width = table_ref.shape[1]
    ext_ref[0:rel, :] = table_ref[...]
    ext_ref[rel : rel + half, :] = jnp.broadcast_to(table_ref[rel - 1 : rel, :], (half, width))
    ext_ref[rel + half : 2 * rel, :] = jnp.broadcast_to(table_ref[0:1, :], (half, width))


def unskewed(block, wall_ref, grad_rows, shift):
    size = grad_rows.shape[0]
    before, own, after, far = (grad_rows[:, k * size : (k + 1) * size] for k in range(4))
    none = jnp.zeros_like(own)
    no_before, no_after = block == 0, block == 3
    near = jnp.concatenate(
        [jnp.where(no_before, none, before), own, jnp.where(no_after, none, after), none], axis=1
    )
    rolled = pltpu.roll(near, shift, 1, stride=1, stride_axis=0)
    far = far + jnp.where(no_before, before, jnp.where(no_after, after, none))
    wall_ref[:, : 2 * size] = rolled[:, : 2 * size]
    wall_ref[:, 2 * size : 3 * size] = rolled[:, 2 * size : 3 * size] + jnp.where(block < 2, far, none)
    wall_ref[:, 3 * size :] = rolled[:, 3 * size :] + jnp.where(block < 2, none, far)


def table_grad(sums, scale):
    rel = sums.shape[1] // 2
    half = rel // 2
    over = jnp.sum(sums[:, rel : rel + half], axis=1, keepdims=True)
    under = jnp.sum(sums[:, rel + half :], axis=1, keepdims=True)
    at = lanes((sums.shape[0], rel))
    folded = sums[:, :rel] + jnp.where(at == rel - 1, over, 0.0) + jnp.where(at == 0, under, 0.0)
    return folded * scale


def as_row(vector_ref):
    return vector_ref[...].astype(F32).reshape(1, -1)


def affine(values, weight_ref, bias_ref):
    return nn(values, weight_ref[...]) + as_row(bias_ref)


def norm_forward(values):
    center = values - jnp.mean(values, axis=-1, keepdims=True)
    spread = jnp.mean(center * center, axis=-1, keepdims=True)
    rate = lax.rsqrt(spread + EPS)
    return center * rate, rate


def norm_backward(grad_hat, hat, rate):
    mean_grad = jnp.mean(grad_hat, axis=-1, keepdims=True)
    mean_along = jnp.mean(grad_hat * hat, axis=-1, keepdims=True)
    return rate * (grad_hat - mean_grad - hat * mean_along)


def column_sum(values):
    return jnp.sum(values.astype(F32), axis=0, keepdims=True)


def slab_copy(source, target, sems, k):
    return pltpu.make_async_copy(source.at[k], target.at[k], sems.at[k])


def first_kernel(
    block_ref, relative, query_weight, key_weight, query_bias, key_bias, own, value_weight,
    value_bias, *rest,
):
    rel_query_store, rel_key_store, terms_out, query_ref, key_ref, terms_ref, sems = rest
    block = block_ref[0]
    relative, query_weight, key_weight, query_bias, key_bias = ready(
        relative, query_weight, key_weight, query_bias, key_bias
    )
    rel_query_out, rel_key_out = rel_query_store.ref, rel_key_store.ref
    rel_query_out[...] = affine(relative[...], query_weight, query_bias).astype(BF)
    rel_key_out[...] = affine(
        nn(reversal(relative.shape[0]), relative[...]).astype(BF), key_weight, key_bias
    ).astype(BF)
    (own,) = ready(own)
    size = own.shape[0]
    query_ref[...] = affine(own[...], query_weight, query_bias).astype(BF)
    key_ref[...] = affine(own[...], key_weight, key_bias).astype(BF)

    def pair_step(pair, carry):
        columns = pair_columns(pair)
        s_ref = terms_ref.at[pair]
        query_own = stacked(query_ref[:, columns])
        own_terms(block, s_ref, query_own, rel_key_out[:, columns], 1)
        other_terms(block, s_ref, lambda slot: key_ref[:, columns], stacked(rel_query_out[:, columns]), 0, (1,))
        s_ref[:, size : 2 * size] += nt(query_own, key_ref[:, columns])
        slab_copy(terms_ref, terms_out, sems, pair).start()
        return carry

    lax.fori_loop(0, HEADS // 2, pair_step, 0)
    for pair in range(HEADS // 2):
        slab_copy(terms_ref, terms_out, sems, pair).wait()


def forward_kernel(
    block_ref, length_ref, place_ref, own, core, far, diagonal, rel_query, rel_key, *rest
):
    (
        terms, query_weight, key_weight, query_bias, key_bias, value_weight, value_bias, output_weight,
        output_bias, first_gain, first_bias, inner_weight, inner_bias, outer_weight, outer_bias, second_gain,
        second_bias, cotangent,
        layer_store, first_store, chances_store, sent_store, stats_store, query_store, key_store, value_store,
        early_send_low, early_send_high, early_keep,
        x_all, s_ref, mixture_ref, log_ref, active_ref, slope_ref, grads_out, terms_ref, sums_ref, small_ref, bias_ref, sems,
    ) = rest
    block = block_ref[0]
    length = length_ref[0]
    size, model_width = layer_store.shape
    head_dim = model_width // HEADS
    factor = LOG2E / math.sqrt(3.0 * head_dim)
    query_out, key_out, value_out = query_store.ref, key_store.ref, value_store.ref
    chances_out, sent_out = chances_store.ref, sent_store.ref
    for pair in range(HEADS // 2):
        slab_copy(terms, terms_ref, sems, pair).start()
    own, core, far, diagonal, rel_query_out = ready(own, core, far, diagonal, rel_query)
    query_weight, key_weight, query_bias, key_bias = ready(query_weight, key_weight, query_bias, key_bias)
    value_weight, value_bias = ready(value_weight, value_bias)
    for at, rows in placed(block, size, own, core, far, diagonal):
        x_all[pl.ds(at, size), :] = rows[...]
    query_out[...] = affine(x_all[...], query_weight, query_bias).astype(BF)
    key_out[...] = affine(x_all[...], key_weight, key_bias).astype(BF)
    value_out[...] = affine(x_all[...], value_weight, value_bias).astype(BF)
    step = lanes((1, 4 * size))
    position = ((block + 3 + step // size) % 4) * size + step % size
    mask_row = jnp.where(position < length, 0.0, -1e30)
    stat_lane = lanes((size, 128))
    log_ref[...] = jnp.zeros_like(log_ref)

    def pair_step(pair, carry):
        columns = pair_columns(pair)
        query_own = stacked(query_out[size : 2 * size, columns])
        slab_copy(terms, terms_ref, sems, pair).wait()
        s_ref[...] = terms_ref[pair]
        other_terms(
            block,
            s_ref,
            lambda slot: key_out[slot * size : (slot + 1) * size, columns],
            stacked(rel_query_out[:, columns]),
            0,
            (0, 2, 3),
        )
        before = s_ref[:, :size] + nt(query_own, key_out[:size, columns])
        s_ref[:, :size] = before * factor + mask_row[:, :size]
        s_ref[:, size : 2 * size] = s_ref[:, size : 2 * size] * factor + mask_row[:, size : 2 * size]
        after = s_ref[:, 2 * size :] + nt(query_own, key_out[2 * size :, columns])
        s_ref[:, 2 * size :] = after * factor + mask_row[:, 2 * size :]
        top = jnp.max(s_ref[...], axis=1, keepdims=True)
        raised = jnp.exp2(s_ref[...] - top)
        s_ref[...] = raised
        row_sum = jnp.sum(raised, axis=1, keepdims=True)
        chances = (s_ref[...] * (1.0 / row_sum)).astype(BF)
        chances_out[pair] = chances
        log_total = top + jnp.log2(row_sum)
        for side in range(2):
            log_ref[...] = jnp.where(
                stat_lane % 8 == 2 * pair + side, log_total[side * size : (side + 1) * size], log_ref[...]
            )
        total = nn(abreast(chances), stacked(value_out[:, columns]))
        mixture_ref[:, columns] = total
        return carry

    lax.fori_loop(0, HEADS // 2, pair_step, 0)

    (
        output_weight, output_bias, first_gain, first_bias, inner_weight, inner_bias, outer_weight, outer_bias,
        second_gain, second_bias, cotangent,
    ) = ready(
        output_weight, output_bias, first_gain, first_bias, inner_weight, inner_bias, outer_weight, outer_bias,
        second_gain, second_bias, cotangent,
    )
    inner_width = inner_weight.shape[1]
    chunks = inner_width // model_width
    mixture_low = mixture_ref[...].astype(BF)
    first_sum = own[...].astype(F32) + affine(mixture_low, output_weight, output_bias)
    first_hat, first_rate = norm_forward(first_sum)
    normed = (first_hat * as_row(first_gain) + as_row(first_bias)).astype(BF)
    root_half = math.sqrt(0.5)
    density = 1.0 / math.sqrt(2.0 * math.pi)

    sums_ref[...] = normed.astype(F32) + as_row(outer_bias)
    bias_ref[...] = as_row(inner_bias)

    def chunk_span(chunk):
        return pl.ds(chunk * model_width, model_width)

    def ahead(chunk, carry):
        span = chunk_span(chunk)
        inner_pre = nn(normed, inner_weight[:, span]) + bias_ref[:, span]
        below = 0.5 + 0.5 * lax.erf(inner_pre * root_half)
        slope_ref[:, span] = below + inner_pre * density * jnp.exp(-0.5 * inner_pre * inner_pre)
        active = (inner_pre * below).astype(BF)
        active_ref[:, span] = active
        sums_ref[...] += nn(active, outer_weight[span, :])
        return carry

    for chunk in range(chunks):
        ahead(chunk, 0)
    second_sum = sums_ref[...]
    second_hat, second_rate = norm_forward(second_sum)
    gain = as_row(second_gain)
    layer_store.ref[...] = second_hat * gain + as_row(second_bias)
    layer_store.push()
    cot = cotangent[...].astype(F32)
    grad_second = norm_backward(cot * gain, second_hat, second_rate)
    grad_outer = grad_second.astype(BF)
    outer_at, inner_at, output_at, small_at = 0, inner_width, 2 * inner_width, 2 * inner_width + model_width
    grads_out[small_at + 16 :, :] = jnp.zeros((grads_out.shape[0] - small_at - 16, model_width), BF)
    small_ref[...] = jnp.zeros_like(small_ref)
    for k, values in enumerate((column_sum(grad_outer), column_sum(cot * second_hat), column_sum(cot))):
        small_ref[k : k + 1, :] = values
    sums_ref[...] = grad_second
    outer_turned, normed_turned = grad_outer.T, normed.T

    def back(chunk, carry):
        span = chunk_span(chunk)
        at = outer_at + chunk * model_width
        grads_out[pl.ds(at, model_width), :] = nn(outer_turned, active_ref[:, span]).astype(BF)
        grad_inner = (nt(grad_outer, outer_weight[span, :]) * slope_ref[:, span]).astype(BF)
        small_ref[pl.ds(3 + chunk, 1), :] = column_sum(grad_inner)
        at = inner_at + chunk * model_width
        grads_out[pl.ds(at, model_width), :] = nn(normed_turned, grad_inner).astype(BF)
        sums_ref[...] += nt(grad_inner, inner_weight[:, span])
        return carry

    for chunk in range(chunks):
        back(chunk, 0)
    grad_normed = sums_ref[...].astype(BF).astype(F32)
    grad_first = norm_backward(grad_normed * as_row(first_gain), first_hat, first_rate)
    first_store.ref[...] = grad_first
    first_store.push()
    grad_branch = grad_first.astype(BF)
    grads_out[output_at : output_at + model_width, :] = tn(mixture_low, grad_branch).astype(BF)
    for k, values in enumerate(
        (column_sum(grad_normed * first_hat), column_sum(grad_normed), column_sum(grad_branch))
    ):
        small_ref[3 + chunks + k : 4 + chunks + k, :] = values
    grads_out[small_at : small_at + 16, :] = small_ref[...].astype(BF)
    push_halves(block % 2, place_ref[0], grads_out, (early_send_low, early_send_high), early_keep)
    grad_mixture = nt(grad_branch, output_weight[...]).astype(BF)
    sent_out[:size, :] = grad_mixture
    along = grad_mixture.astype(F32) * mixture_ref[...]
    stats = log_ref[...]
    for head in range(HEADS):
        columns = slice((head // 2) * 128, (head // 2 + 1) * 128)
        delta = jnp.sum(of_head(along[:, columns], head % 2), axis=1, keepdims=True)
        stats = jnp.where((stat_lane < 16) & (stat_lane % 8 == head), delta, stats)
    stats_store.ref[...] = stats
    upper = stats.astype(BF).astype(F32)
    parts = jnp.where((stat_lane // 8) % 2 == 0, upper, stats - upper).T[:32, :]
    sent_out[size:, :size] = parts.astype(BF)
    sent_out[size:, size:] = jnp.zeros((32, model_width - size), BF)
    sent_store.push()


def position_backward(block, grad_scores, flip, other_pair, ext_pair, own_rows_back, wall_ref, shift):
    size = flip.shape[0]
    full = grad_scores.shape[1]
    grad_back = nn(flip, abreast(grad_scores)).astype(BF)
    for side in range(2):
        unskewed(block, wall_ref.at[pl.ds(side * size, size)], grad_back[:, side * full : (side + 1) * full], shift)
    row_grad = nn(grad_back, stacked(other_pair)) + nn(abreast(wall_ref[...]), stacked(ext_pair))
    return row_grad, tn(stacked(own_rows_back), wall_ref[...])


def query_kernel(
    block_ref, rel_key, query_all, sent, stats, value_all, key_all, chances_load,
    query_store, rel_key_grad_store,
    ext_ref, wall_ref, back_ref, rows_ref,
):
    block = block_ref[0]
    size, model_width = query_store.shape
    scale = 1.0 / math.sqrt(3.0 * (model_width // HEADS))
    flip = reversal(size)
    chances = chances_load.buffer
    rel_key, query_all, sent, stats, value_all, key_all = ready(rel_key, query_all, sent, stats, value_all, key_all)
    extend_table(ext_ref, rel_key)
    back_ref[...] = nn(flip, query_all[size : 2 * size, :]).astype(BF)
    stat_lane = lanes((size, 128))

    def pair_step(pair, carry):
        columns = pair_columns(pair)
        delta = jnp.concatenate(
            [
                jnp.sum(jnp.where(stat_lane == head, stats[...], 0.0), axis=1, keepdims=True)
                for head in (2 * pair, 2 * pair + 1)
            ],
            axis=0,
        )
        grad_chances = nt(stacked(sent[:size, columns]), value_all[:, columns])
        grad_scores = (chances[pair].astype(F32) * (grad_chances - delta)).astype(BF)
        row_grad, table = position_backward(
            block, grad_scores, flip, key_all[:, columns], ext_ref[:, columns], back_ref[:, columns], wall_ref, 3 * size
        )
        rows_ref[:, columns] = (row_grad * scale).astype(BF)
        rel_key_grad_store.ref[columns, :] = table_grad(table, scale)
        return carry

    lax.fori_loop(0, HEADS // 2, pair_step, 0)
    query_store.ref[...] = nn(flip, rows_ref[...]).astype(BF)


def key_kernel(
    block_ref, length_ref, place_ref, rel_query, key_all, rel_key, query_all, value_all,
    sent_own, sent_core, sent_far, sent_diagonal,
    own, relative, grad_query, grad_rel_key, query_weight, key_weight, value_weight, grad_first,
    tokens_store, late_send_low, late_send_high, late_keep,
    grads_out, key_rows_ref, value_rows_ref, rel_grad_ref,
    sent_ref, s_ref, grad_ref, ext_ref, wall_ref, back_ref, stat_ref,
):
    block = block_ref[0]
    length = length_ref[0]
    size, model_width = key_rows_ref.shape
    scale = 1.0 / math.sqrt(3.0 * (model_width // HEADS))
    factor = LOG2E * scale
    flip = reversal(size)
    rel_query, key_all, rel_key, query_all, value_all = ready(rel_query, key_all, rel_key, query_all, value_all)
    extend_table(ext_ref, rel_query)
    back_ref[...] = nn(flip, key_all[size : 2 * size, :]).astype(BF)
    for at, rows in placed(block, size, *ready(sent_own, sent_core, sent_far, sent_diagonal)):
        sent_ref[pl.ds(at, size), :] = rows[:size, :]
        parts = rows[size:, :size].astype(F32)
        stat_ref[0:8, pl.ds(at, size)] = parts[0:8, :] + parts[8:16, :]
        stat_ref[8:16, pl.ds(at, size)] = parts[16:24, :] + parts[24:32, :]
    position = block * size + lax.broadcasted_iota(jnp.int32, (size, 1), 0)
    mask_column = jnp.where(position < length, 0.0, -1e30)

    def pair_step(pair, carry):
        columns = pair_columns(pair)
        key_pair = stacked(key_all[size : 2 * size, columns])
        own_terms(block, s_ref, key_pair, rel_query[:, columns], 0)
        other_terms(
            block,
            s_ref,
            lambda slot: query_all[slot * size : (slot + 1) * size, columns],
            stacked(rel_key[:, columns]),
            1,
            range(4),
        )
        content = nt(key_pair, query_all[:, columns])
        for side in range(2):
            rows = slice(side * size, (side + 1) * size)
            less = mask_column - stat_ref[pl.ds(8 + 2 * pair + side, 1), :]
            s_ref[rows, :] = jnp.exp2((s_ref[rows, :] + content[rows]) * factor + less)
        value_grad = nn(abreast(s_ref[...].astype(BF)), stacked(sent_ref[:, columns]))
        grad_chances = nt(stacked(value_all[size : 2 * size, columns]), sent_ref[:, columns])
        for side in range(2):
            rows = slice(side * size, (side + 1) * size)
            delta = stat_ref[pl.ds(2 * pair + side, 1), :]
            grad_ref[rows, :] = (s_ref[rows, :] * (grad_chances[rows] - delta)).astype(BF)
        row_grad, table = position_backward(
            block, grad_ref[...], flip, query_all[:, columns], ext_ref[:, columns], back_ref[:, columns], wall_ref,
            3 * size + 1,
        )
        key_rows_ref[:, columns] = (row_grad * scale).astype(BF)
        value_rows_ref[:, columns] = value_grad.astype(BF)
        rel_grad_ref[columns, :] = table_grad(table, scale)
        return carry

    lax.fori_loop(0, HEADS // 2, pair_step, 0)
    own, relative, grad_query, grad_rel_key = ready(own, relative, grad_query, grad_rel_key)
    rel = relative.shape[0]
    grad_key = nn(flip, key_rows_ref[...]).astype(BF)
    grad_value = value_rows_ref[...]
    rel_query_grad = rel_grad_ref[...]
    rel_key_grad = grad_rel_key[...]
    query_low = rel_query_grad.astype(BF)
    key_low = nn(rel_key_grad.astype(BF), reversal(rel)).astype(BF)
    tokens = own[...]
    table = relative[...]
    grads_out[0:model_width, :] = (tn(tokens, grad_query[...]) + tt(table, query_low)).astype(BF)
    grads_out[model_width : 2 * model_width, :] = (tn(tokens, grad_key) + tt(table, key_low)).astype(BF)
    grads_out[2 * model_width : 3 * model_width, :] = tn(tokens, grad_value).astype(BF)
    table_at = 3 * model_width
    query_weight, key_weight, value_weight, grad_first = ready(query_weight, key_weight, value_weight, grad_first)
    grads_out[table_at : table_at + rel, :] = (
        tt(query_low, query_weight[...]) + tt(key_low, key_weight[...])
    ).astype(BF)
    small_at = table_at + rel
    grads_out[small_at + 16 :, :] = jnp.zeros((grads_out.shape[0] - small_at - 16, model_width), BF)
    ones = jnp.ones((8, rel), BF)

    def lane_sums(values):
        high = values.astype(BF)
        low = (values - high.astype(F32)).astype(BF)
        return (nt(ones, high) + nt(ones, low))[0:1, :]

    small = [
        column_sum(grad_query[...]) + lane_sums(rel_query_grad),
        column_sum(grad_key) + lane_sums(rel_key_grad),
        column_sum(grad_value),
        jnp.zeros((13, model_width), F32),
    ]
    grads_out[small_at : small_at + 16, :] = jnp.concatenate(small, axis=0).astype(BF)
    push_halves(block % 2, place_ref[0], grads_out, (late_send_low, late_send_high), late_keep)
    tokens_store.ref[...] = (
        nt(grad_query[...], query_weight[...])
        + nt(grad_key, key_weight[...])
        + nt(grad_value, value_weight[...])
        + grad_first[...]
    )


class Load:
    def __init__(self, source, buffer, sem):
        self.copy, self.buffer, self.waiting = pltpu.make_async_copy(source, buffer, sem), buffer, True
        self.copy.start()

    def ready(self):
        if self.waiting:
            self.copy.wait()
        self.waiting = False
        return self.buffer


def ready(*loads):
    return [load.ready() for load in loads]


class Store:
    def __init__(self, target, buffer, sem):
        self.copy, self.ref, self.shape, self.waiting = pltpu.make_async_copy(buffer, target, sem), buffer, buffer.shape, False

    def push(self):
        self.copy.start()
        self.waiting = True

    def finish(self):
        if not self.waiting:
            self.push()
        self.copy.wait()


class Here:
    def __init__(self, ref):
        self.ref = self.buffer = ref
        self.shape = ref.shape

    def ready(self):
        return self.ref

    def push(self):
        pass

    def finish(self):
        pass


def terms_after(first, terms):
    arrays = in_order(first, [array for array, _, _ in terms])
    return [(array, start, blocks) for array, (_, start, blocks) in zip(arrays, terms)]


class Raw:
    def __init__(self, target, sems):
        self.target, self.sems, self.copies = target, sems, []
        self.shape = target.shape

    def push_from(self, source, there):
        copy = pltpu.make_async_copy(source, self.target.at[there], self.sems.at[len(self.copies)])
        copy.start()
        self.copies.append(copy)

    def finish(self):
        for copy in self.copies:
            copy.wait()


def push_halves(core, place, rows_ref, sends, keep):
    half = keep.shape[0]
    part = half // 4
    for k in range(4):
        at = (place ^ k) * part
        send, there = sends[k // 2], pl.ds(k % 2 * part, part)
        send.push_from(rows_ref.at[pl.ds(pl.multiple_of((1 - core) * half + at, 16), part)], there)
        keep.push_from(rows_ref.at[pl.ds(pl.multiple_of(core * half + at, 16), part)], pl.ds(k * part, part))


class Kept:
    def __init__(self, *what):
        self.what = what


class Bare:
    def __init__(self, *what):
        self.what = what


class Fetch:
    def __init__(self, what):
        self.what = what


def call(kernel, outs, scratch, *operands, scalars, micros, vmem):
    fetched = [k for k, operand in enumerate(operands) if isinstance(operand, Fetch)]
    bare_in = [k for k, operand in enumerate(operands) if isinstance(operand, Bare)]
    operands = [
        operand.what if isinstance(operand, Fetch) else operand.what[0] if isinstance(operand, Bare) else operand
        for operand in operands
    ]
    bare_out = [k for k, out in enumerate(outs) if isinstance(out, Bare)]
    outs = [out.what if isinstance(out, Bare) else out for out in outs]
    outs = list(outs) + [Kept(operands[k].shape, operands[k].dtype) for k in fetched]
    kept_in = [isinstance(operand, Kept) for operand in operands]
    kept_out = [isinstance(out, Kept) for out in outs]
    operands = [
        operand if k < scalars
        else pltpu.with_memory_space_constraint(operand.what[0], pltpu.VMEM) if kept
        else pltpu.with_memory_space_constraint(operand, pltpu.HBM)
        for k, (operand, kept) in enumerate(zip(operands, kept_in))
    ]
    outs = [out.what if kept else out for out, kept in zip(outs, kept_out)]
    raw = [len(out) > 2 for out in outs]
    loads = [k for k in range(scalars, len(operands)) if not kept_in[k] and k not in bare_in]
    stores = [k for k in range(len(outs)) if not kept_out[k] and k not in bare_out]
    buffered = [k for k in stores if not raw[k]]
    own_loads = [k for k in loads if k not in fetched]

    def body(*refs):
        n, m = len(operands), len(outs)
        ins, results, rest = list(refs[:n]), list(refs[n : n + m]), list(refs[n + m :])
        in_sems, out_sems = rest.pop(), rest.pop()
        buffers = [rest.pop() for _ in range(len(own_loads) + len(buffered))][::-1]
        targets = dict(zip(own_loads, buffers)) | dict(zip(fetched, results[m - len(fetched) :]))
        results = results[: m - len(fetched)]
        for k in range(scalars, n):
            if kept_in[k]:
                ins[k] = Here(ins[k])
        for place, k in enumerate(loads):
            ins[k] = Load(ins[k], targets[k], in_sems.at[place])
        buffers = buffers[len(own_loads) :]
        for k in range(len(results)):
            if kept_out[k]:
                results[k] = Here(results[k])
        for place, k in enumerate(stores):
            if raw[k]:
                results[k] = Raw(results[k], out_sems.at[place])
            else:
                results[k] = Store(results[k], buffers.pop(0), out_sems.at[place, 0])
        kernel(*ins, *results, *rest)
        for k in fetched:
            ins[k].ready()
        for k in stores:
            results[k].finish()

    spaces = [
        pltpu.SMEM if k < scalars else pltpu.VMEM if kept_in[k] else pltpu.HBM for k in range(len(operands))
    ]
    buffers = [(operands[k].shape, operands[k].dtype) for k in own_loads] + [outs[k][:2] for k in buffered]
    return pl.pallas_call(
        body,
        out_shape=[
            pltpu.VMEM(out[0], out[1]) if kept else pltpu.HBM(out[0], out[1])
            for out, kept in zip(outs, kept_out)
        ],
        in_specs=[pl.BlockSpec(memory_space=space) for space in spaces],
        out_specs=[pl.BlockSpec(memory_space=pltpu.VMEM if kept else pltpu.HBM) for kept in kept_out],
        scratch_shapes=[
            pltpu.SemaphoreType.DMA(space[0]) if space[1] is None else pltpu.VMEM(*space)
            for space in list(scratch) + buffers
        ]
        + [pltpu.SemaphoreType.DMA((max(len(stores), 1), 4)), pltpu.SemaphoreType.DMA((max(len(loads), 1),))],
        compiler_params=pltpu.CompilerParams(vmem_limit_bytes=vmem * MIB),
        cost_estimate=pl.CostEstimate(flops=micros * 10**9, bytes_accessed=micros * 10**6, transcendentals=0),
    )(*operands)


class Group:
    def __init__(self, blk_count, dp_count, bits):
        self.blk_count, self.dp_count, self.bits = blk_count, dp_count, bits
        self.size = 2 ** len(bits)
        place = {"blk": lax.axis_index("blk"), "dp": lax.axis_index("dp")}
        self.digits = [(place[axis] >> (bit.bit_length() - 1)) & 1 for axis, bit in bits]
        self.me = sum(digit << k for k, digit in enumerate(self.digits))

    def pairs(self, mask):
        change = {"blk": 0, "dp": 0}
        for k, (axis, bit) in enumerate(self.bits):
            if mask >> k & 1:
                change[axis] |= bit
        return [
            (blk * self.dp_count + dp, (blk ^ change["blk"]) * self.dp_count + (dp ^ change["dp"]))
            for blk in range(self.blk_count)
            for dp in range(self.dp_count)
        ]

    def send(self, values, mask):
        return lax.ppermute(values, ("blk", "dp"), self.pairs(mask))

    def scatter(self, terms):
        def part(index):
            return [
                (array, first + index * (blocks // self.size), blocks // self.size) for array, first, blocks in terms
            ]

        outs = [total(part(self.me ^ mask)) for mask in range(1, self.size)]
        arrived = [self.send(out, mask + 1) for mask, out in enumerate(outs)]
        return outs, part(self.me) + [whole(array) for array in arrived]

    def pieces(self, held):
        return [held] + [self.send(held, mask) for mask in range(1, self.size)]

    def gather(self, held):
        return self.arrange(self.pieces(held))

    def arrange(self, parts):
        for k, digit in enumerate(self.digits):
            parts = [
                jnp.where(digit == 0, parts[q], parts[q ^ (1 << k)]) for q in range(self.size)
            ]
        return jnp.concatenate(parts, axis=0)


def groups_of(blk_count, dp_count):
    bits, bit = [], 2
    while bit < dp_count:
        bits.append(("dp", bit))
        bit *= 2
    groups = [[("blk", 1)], [("blk", 2), ("dp", 1)]]
    groups += [bits[k : k + 2] for k in range(0, len(bits), 2)]
    return [Group(blk_count, dp_count, group) for group in groups]


def whole(array):
    return array, 0, array.shape[0]


def total(terms):
    spans = [
        array[first : first + blocks] if isinstance(first, int) else lax.dynamic_slice_in_dim(array, first, blocks, 0)
        for array, first, blocks in terms
    ]
    return sum(span.astype(F32) for span in spans).astype(BF)


def in_order(first, then):
    return lax.optimization_barrier((first, then))[1]


def halves_to_scratch(core_ref, place_ref, held, arrived, both_ref):
    held, arrived = ready(held, arrived)
    half = held.shape[0]
    part = half // 4
    for k in range(4):
        at = (place_ref[0] ^ k) * part
        span = slice(k * part, (k + 1) * part)
        both_ref[pl.ds(pl.multiple_of(core_ref[0] * half + at, 16), part), :] = held[span, :]
        both_ref[pl.ds(pl.multiple_of((1 - core_ref[0]) * half + at, 16), part), :] = arrived[span, :]


def early_kernel(
    core_ref, place_ref, held, arrived,
    outer_weight, inner_weight, output_weight, outer_bias, second_gain, second_bias, inner_bias, first_gain, first_bias,
    output_bias,
    both_ref,
):
    halves_to_scratch(core_ref, place_ref, held, arrived, both_ref)
    inner_width, width = outer_weight.shape
    chunks = inner_width // width
    for chunk in range(chunks):
        span = slice(chunk * width, (chunk + 1) * width)
        outer_weight.ref[span, :] = both_ref[span, :].T.astype(F32)
    outer_weight.push()
    for chunk in range(chunks):
        at = inner_width + chunk * width
        inner_weight.ref[:, chunk * width : (chunk + 1) * width] = both_ref[at : at + width, :].astype(F32)
    at = 2 * inner_width
    output_weight.ref[...] = both_ref[at : at + width, :].astype(F32)
    output_weight.push()
    small = both_ref[at + width : at + width + 16, :].astype(F32)

    def vector(out, row):
        out.ref[...] = small[row, :]
        out.push()

    vector(outer_bias, 0)
    vector(second_gain, 1)
    vector(second_bias, 2)
    inner_bias.ref[...] = jnp.concatenate([small[3 + k : 4 + k, :] for k in range(chunks)], axis=1)[0, :]
    inner_bias.push()
    vector(first_gain, 3 + chunks)
    vector(first_bias, 4 + chunks)
    vector(output_bias, 5 + chunks)


def late_kernel(
    core_ref, place_ref, held, arrived,
    query_weight, query_bias, key_weight, key_bias, value_weight, value_bias, relative,
    both_ref,
):
    halves_to_scratch(core_ref, place_ref, held, arrived, both_ref)
    width = query_weight.shape[0]
    rel = relative.shape[0]
    for k, out in enumerate((query_weight, key_weight, value_weight)):
        out.ref[...] = both_ref[k * width : (k + 1) * width, :].astype(F32)
        out.push()
    at = 3 * width
    relative.ref[...] = both_ref[at : at + rel, :].astype(F32)
    small = both_ref[at + rel : at + rel + 16, :].astype(F32)
    query_bias.ref[...] = small[0, :]
    key_bias.ref[...] = small[1, :]
    value_bias.ref[...] = small[2, :]


def on_device(
    blk_count, dp_count,
    tokens, lengths, query_weight, query_bias, key_weight, key_bias, value_weight, value_bias,
    output_weight, output_bias, first_gain, first_bias, inner_weight, inner_bias, outer_weight, outer_bias,
    second_gain, second_bias, relative_table, cotangent,
):
    seq_count, size, width = tokens.shape
    rel = relative_table.shape[0]
    inner_width = inner_weight.shape[1]
    own = tokens[0]
    block = lax.axis_index("blk").astype(jnp.int32).reshape(1)
    groups = groups_of(blk_count, dp_count)
    chips = groups[1:]
    place = chips[0].me.astype(jnp.int32).reshape(1)
    shards = blk_count * dp_count

    def along(values, bit):
        return lax.ppermute(values, "blk", [(i, i ^ bit) for i in range(blk_count)])

    def blocks(rows, share):
        return rows.reshape(shards // share, -1, width)

    def flat(values):
        return values.reshape(-1, width)

    def first_terms(keep, low, high):
        arrived = [groups[0].send(blocks(piece, 4), 1) for piece in (low, high)]
        keep, part = blocks(keep, 2), shards // 8
        return [[(keep, k * part, part), (arrived[k // 2], k % 2 * part, part)] for k in range(4)]

    def first_scatter(parts):
        outs = [total(terms) for terms in parts[1:]]
        return outs, parts[0] + [whole(chips[0].send(out, k + 1)) for k, out in enumerate(outs)]

    core = along(own, 1)
    far = along(own, 2)
    diagonal = along(own, 3)
    full = blk_count * size
    (
        rel_query, rel_key, terms, relative_kept, query_weight, key_weight, query_bias, key_bias, own, value_weight, value_bias,
    ) = call(
        first_kernel,
        [Kept((rel, width), BF), Kept((rel, width), BF), Bare((HEADS // 2, 2 * size, full), F32)],
        [((size, width), BF), ((size, width), BF), ((HEADS // 2, 2 * size, full), F32), ((HEADS // 2,), None)],
        block,
        *map(Fetch, (relative_table, query_weight, key_weight, query_bias, key_bias, own, value_weight, value_bias)),
        scalars=1, micros=9, vmem=14,
    )
    (
        layer_out, grad_first, chances, sent, stats, query_all, key_all, value_all,
        early_send_low, early_send_high, early_keep,
    ) = call(
        forward_kernel,
        [
            ((size, width), F32),
            Kept((size, width), F32),
            Kept((HEADS // 2, 2 * size, full), BF),
            Kept((size + 32, width), BF),
            Kept((size, 128), F32),
            Kept((full, width), BF),
            Kept((full, width), BF),
            Kept((full, width), BF),
            ((EARLY_ROWS // 4, width), BF, "raw"),
            ((EARLY_ROWS // 4, width), BF, "raw"),
            ((EARLY_ROWS // 2, width), BF, "raw"),
        ],
        [
            ((full, width), BF),
            ((2 * size, full), F32),
            ((size, width), F32),
            ((size, 128), F32),
            ((size, inner_width), BF),
            ((size, inner_width), F32),
            ((EARLY_ROWS, width), BF),
            ((HEADS // 2, 2 * size, full), F32),
            ((size, width), F32),
            ((16, width), F32),
            ((1, inner_width), F32),
            ((HEADS // 2,), None),
        ],
        block, lengths, place,
        *map(Kept, (own, core, far, diagonal, rel_query, rel_key)),
        Bare(terms),
        *map(Kept, (query_weight, key_weight, query_bias, key_bias, value_weight, value_bias)),
        output_weight, output_bias, first_gain, first_bias, inner_weight, inner_bias, outer_weight, outer_bias,
        second_gain, second_bias, cotangent[0],
        scalars=3, micros=20, vmem=26,
    )
    early_parts = first_terms(early_keep, early_send_low, early_send_high)
    sent_far = along(sent, 2)
    sent_core = along(sent, 1)
    position_scratch = [((2 * rel, width), BF), ((2 * size, 2 * rel), BF), ((size, width), BF)]
    grad_query, grad_rel_key = call(
        query_kernel,
        [Kept((size, width), BF), Kept((width, rel), F32)],
        position_scratch + [((size, width), BF)],
        block, *map(Kept, (rel_key, query_all, sent, stats, value_all, key_all, chances)),
        scalars=1, micros=8, vmem=10,
    )
    sent_diagonal = along(in_order(grad_query, sent_far), 1)
    key_scratch = (
        [((full, width), BF), ((2 * size, full), F32), ((2 * size, full), BF)] + position_scratch + [((16, full), F32)]
    )
    key_arrays = tuple(
        map(Kept, (rel_query, key_all, rel_key, query_all, value_all, sent, sent_core, sent_far, sent_diagonal))
    )
    sending, early_terms = first_scatter(early_parts)
    grad_tokens, late_send_low, late_send_high, late_keep = call(
        key_kernel,
        [((size, width), F32)] + [((LATE_ROWS // 4, width), BF, "raw")] * 2 + [((LATE_ROWS // 2, width), BF, "raw")],
        [((LATE_ROWS, width), BF), ((size, width), BF), ((size, width), BF), ((width, rel), F32)] + key_scratch,
        in_order(sending, block), lengths, place, *key_arrays,
        *map(Kept, (own, relative_kept, grad_query, grad_rel_key, query_weight, key_weight, value_weight, grad_first)),
        scalars=3, micros=17, vmem=18,
    )
    late_parts = first_terms(late_keep, late_send_low, late_send_high)
    early_terms = terms_after(late_send_low, early_terms)
    for group in chips[1:]:
        sending, early_terms = group.scatter(early_terms)
        late_parts = [terms_after(sending, terms) for terms in late_parts]
    sending, late_terms = first_scatter(late_parts)
    first_arrived = late_terms[1 - chips[0].size][0]
    early_held = total(terms_after(first_arrived, early_terms))
    for group in reversed(chips[2:]):
        early_held = group.gather(early_held)
    early_parts = chips[1].pieces(early_held)
    for group in chips[1:]:
        sending, late_terms = group.scatter(late_terms)
    first_arrived = late_terms[1 - chips[-1].size][0]
    early_pieces = chips[0].pieces(chips[1].arrange(in_order(first_arrived, early_parts)))
    late_held = total(late_terms)
    for group in reversed(chips[2:]):
        late_held = group.gather(late_held)
    late_parts = chips[1].pieces(late_held)
    late_parts, early_first = lax.optimization_barrier((late_parts, early_pieces[1]))
    early_pieces[1] = early_first
    late_held = chips[1].arrange(late_parts)
    early_held = jnp.concatenate(early_pieces, axis=0)
    late_pieces = chips[0].pieces(late_held)
    my_core = groups[0].me.astype(jnp.int32).reshape(1)
    square, vector = ((width, width), F32), ((width,), F32)
    (
        g_outer_weight, g_inner_weight, g_output_weight, g_outer_bias, g_second_gain, g_second_bias, g_inner_bias,
        g_first_gain, g_first_bias, g_output_bias,
    ) = call(
        early_kernel,
        [((inner_width, width), F32), ((width, inner_width), F32), square, vector, vector, vector,
         ((inner_width,), F32), vector, vector, vector],
        [((EARLY_ROWS, width), BF)],
        my_core, place, *(Kept(flat(piece)) for piece in groups[0].pieces(early_held)),
        scalars=2, micros=4, vmem=14,
    )
    late_held = jnp.concatenate(in_order(g_output_bias, late_pieces), axis=0)
    (
        g_query_weight, g_query_bias, g_key_weight, g_key_bias, g_value_weight, g_value_bias, g_relative,
    ) = call(
        late_kernel,
        [square, vector, square, vector, square, vector, ((rel, width), F32)],
        [((LATE_ROWS, width), BF)],
        my_core, place, *(Kept(flat(piece)) for piece in groups[0].pieces(late_held)),
        scalars=2, micros=2, vmem=10,
    )
    return (
        layer_out[None], grad_tokens[None], g_query_weight, g_query_bias, g_key_weight, g_key_bias,
        g_value_weight, g_value_bias, g_output_weight, g_output_bias, g_first_gain, g_first_bias,
        g_inner_weight, g_inner_bias, g_outer_weight, g_outer_bias, g_second_gain, g_second_bias, g_relative,
    )


def solution(mesh):
    blk_count, dp_count = mesh.shape["blk"], mesh.shape["dp"]
    rows = P("dp", "blk", None)
    in_specs = (rows, P("dp")) + (P(),) * 17 + (rows,)
    out_specs = (rows, rows) + (P(),) * 17

    def whole(*arrays):
        return on_device(blk_count, dp_count, *arrays)

    return jax.shard_map(whole, mesh=mesh, in_specs=in_specs, out_specs=out_specs, check_vma=False)
```

profile of v0, /device:TPU:9, one launch (start us, length us, event | category | flops | bytes accessed | tf_op | source)
XLA Modules:
  0.0 120.6 jit_solution(11942289501312942697)
XLA Ops:
  1.4 1.3 %collective-permute-start.1 = (bf16[256,384]{1,0:T(8,128)(2,1)}, bf16[256,384]{1,0:T(8,128)(2,1)S(1)}, u32[]{:S(2)}, u32[]{:S(2)}) collective-permute-start(bf16[256,384]{1,0:T(8,128)(2,1)} %bitcast.41), channel_id=1, source_target_pairs={{0,16},{8,24},{16,0},{24,8},{1,17},{9,25},{17,1},{25,9},{2,18},{10... | collective-permute-start | bytes 589832 | tf_op jit(solution)/shard_map/ppermute | solution.py:864
  3.1 7.9 %shard_map.339 = (bf16[512,384]{1,0:T(8,128)(2,1)S(1)}, bf16[512,384]{1,0:T(8,128)(2,1)S(1)}, f32[3,512,1024]{2,1,0:T(8,128)}, bf16[512,384]{1,0:T(8,128)(2,1)S(...) custom-call(s32[1]{0:T(128)} %bitcast.refs_0_, ...), custom_call_target="tpu_custom_call" | custom-call | flops 8999999488 | bytes 9000000 | tf_op jit(solution)/shard_map/pallas_call | solution.py:692
  12.5 17.3 %shard_map.340 = (f32[256,384]{1,0:T(8,128)}, f32[256,384]{1,0:T(8,128)S(1)}, bf16[3,512,1024]{2,1,0:T(8,128)(2,1)S(1)}, bf16[288,384]{1,0:T(8,128)(2,1)S(1)}, f...) custom-call(s32[1]{0:T(128)} %bitcast.refs_0_, ...), custom_call_target="tpu_custom_call" | custom-call | flops 20000000000 | bytes 20000000 | tf_op jit(solution)/shard_map/pallas_call | solution.py:692
  29.8 1.3 %collective-permute-start.6 = (bf16[288,384]{1,0:T(8,128)(2,1)S(1)}, bf16[288,384]{1,0:T(8,128)(2,1)S(1)}, u32[]{:S(2)}, u32[]{:S(2)}) collective-permute-start(bf16[288,384]{1,0:T(8,128)(2,1)S(1)} %get-tuple-element.114.refs_3_.refs_8_), channel_id=1, source_target_pairs={{0,16},{8,24},{16,0},{24,8},{1,17},{9,25},{17,1},{25,9},{2,18},{10... | collective-permute-start | bytes 663560 | tf_op jit(solution)/shard_map/ppermute | solution.py:864
  32.1 5.5 %shard_map.341 = (bf16[256,384]{1,0:T(8,128)(2,1)S(1)}, f32[384,512]{1,0:T(8,128)S(1)}) custom-call(s32[1]{0:T(128)} %bitcast.refs_0_, bf16[512,384]{1,0:T(8,128)(2,1)S(1)} %get-tuple-element.98.refs_8_.refs_1_.refs_5_, bf16[1024,384]{1,0:T(8,128)(2,1)S(1)} %get-tuple-element.112.refs_2_.refs_6_, bf16[288,384]{1,0:T(8,128)(2,1)S(1)} %get-tuple-element.114.refs_3_.refs_8_, ...), custom_call_target="tpu_custom_call" | custom-call | flops 8000000000 | bytes 8000000 | tf_op jit(solution)/shard_map/pallas_call | solution.py:692
  38.9 2.1 %collective-permute-start.10 = (bf16[4,112,384]{2,1,0:T(8,128)(2,1)}, bf16[4,112,384]{2,1,0:T(8,128)(2,1)}, u32[]{:S(2)}, u32[]{:S(2)}) collective-permute-start(bf16[4,112,384]{2,1,0:T(8,128)(2,1)} %get-tuple-element.192), channel_id=1, source_target_pairs={{0,17},{1,16},{2,19},{3,18},{4,21},{5,20},{6,23},{7,22},{8,25},{9,... | collective-permute-start | bytes 1032200 | tf_op jit(solution)/shard_map/ppermute | solution.py:730
  41.7 15.9 %shard_map.342 = (f32[256,384]{1,0:T(8,128)}, bf16[448,384]{1,0:T(8,128)(2,1)}, bf16[448,384]{1,0:T(8,128)(2,1)}, bf16[896,384]{1,0:T(8,128)(2,1)}) custom-call(s32[1]{0:T(128)} %bitcast.refs_0_, s32[1]{0:T(128)S(6)} %copy.48.refs_1_, s32[1]{0:T(128)} %bitcast.1.refs_2_.refs_1_, bf16[512,384]{1,0:T(8,128)(2,1)S(1)} %get-tuple-element.97.refs_7_.refs_3_, ...), custom_call_target="tpu_custom_call" | custom-call | flops 16999999488 | bytes 17000000 | tf_op jit(solution)/shard_map/pallas_call | solution.py:692
  57.6 1.4 %collective-permute-start.11 = (bf16[8,56,384]{2,1,0:T(8,128)(2,1)}, bf16[8,56,384]{2,1,0:T(8,128)(2,1)S(1)}, u32[]{:S(2)}, u32[]{:S(2)}) collective-permute-start(bf16[8,56,384]{2,1,0:T(8,128)(2,1)} %bitcast.39), channel_id=1, source_target_pairs={{0,8},{1,9},{2,10},{3,11},{4,12},{5,13},{6,14},{7,15},{8,0},{9,1},... | collective-permute-start | bytes 1032200 | tf_op jit(solution)/shard_map/ppermute | solution.py:730
  59.2 1.5 %add_convert_fusion.4 = (bf16[1,112,384]{2,1,0:T(8,128)(2,1)S(1)}, bf16[1,112,384]{2,1,0:T(8,128)(2,1)S(1)}, bf16[1,112,384]{2,1,0:T(8,128)(2,1)S(1)}) fusion(bf16[4,112,384]{2,1,0:T(8,128)(2,1)} %collective-permute-done.10, s32[]{:T(128)S(6)} %select_n.150, bf16[4,112,384]{2,1,0:T(8,128)(2,1)} %collective-permute-done.9, ...), kind=kLoop, calls=%fused_computation.12 | loop fusion | flops 1290240 | bytes 1548324 | tf_op jit(solution)/shard_map/convert_element_type | solution.py:775
  60.9 2.3 %collective-permute-start.18 = (bf16[1,112,384]{2,1,0:T(8,128)(2,1)S(1)}, bf16[1,112,384]{2,1,0:T(8,128)(2,1)S(1)}, u32[]{:S(2)}, u32[]{:S(2)}) collective-permute-start(bf16[1,112,384]{2,1,0:T(8,128)(2,1)S(1)} %get-tuple-element.182), channel_id=1, source_target_pairs={{0,4},{1,5},{2,6},{3,7},{4,0},{5,1},{6,2},{7,3},{8,12},{9,13},{10,... | collective-permute-start | bytes 258056 | tf_op jit(solution)/shard_map/ppermute | solution.py:730
  64.2 1.3 %collective-permute-start.14 = (bf16[4,56,384]{2,1,0:T(8,128)(2,1)S(1)}, bf16[4,56,384]{2,1,0:T(8,128)(2,1)S(1)}, u32[]{:S(2)}, u32[]{:S(2)}) collective-permute-start(bf16[4,56,384]{2,1,0:T(8,128)(2,1)S(1)} %get-tuple-element.190), channel_id=1, source_target_pairs={{0,1},{1,0},{2,3},{3,2},{4,5},{5,4},{6,7},{7,6},{8,9},{9,8},{10,11... | collective-permute-start | bytes 516104 | tf_op jit(solution)/shard_map/ppermute | solution.py:730
  67.3 3.9 %collective-permute-done.19 = bf16[1,112,384]{2,1,0:T(8,128)(2,1)S(1)} collective-permute-done((bf16[1,112,384]{2,1,0:T(8,128)(2,1)S(1)}, bf16[1,112,384]{2,1,0:T(8,128)(2,1)S(1)}, u32[]{:S(2)}, u32[]{:S(2)}) %collective-permute-start.19) | collective-permute-done | bytes 86048 | tf_op jit(solution)/shard_map/ppermute | solution.py:730
  72.4 2.1 %collective-permute-start.21 = (bf16[1,112,384]{2,1,0:T(8,128)(2,1)S(1)}, bf16[1,112,384]{2,1,0:T(8,128)(2,1)S(1)}, u32[]{:S(2)}, u32[]{:S(2)}) collective-permute-start(bf16[1,112,384]{2,1,0:T(8,128)(2,1)S(1)} %add_convert_fusion.3), channel_id=1, source_target_pairs={{0,4},{1,5},{2,6},{3,7},{4,0},{5,1},{6,2},{7,3},{8,12},{9,13},{10,... | collective-permute-start | bytes 258056 | tf_op jit(solution)/shard_map/ppermute | solution.py:730
  77.4 2.3 %collective-permute-done.16 = bf16[1,56,384]{2,1,0:T(8,128)(2,1)S(1)} collective-permute-done((bf16[1,56,384]{2,1,0:T(8,128)(2,1)S(1)}, bf16[1,56,384]{2,1,0:T(8,128)(2,1)S(1)}, u32[]{:S(2)}, u32[]{:S(2)}) %collective-permute-start.16) | collective-permute-done | bytes 43040 | tf_op jit(solution)/shard_map/ppermute | solution.py:730
  79.6 1.3 %collective-permute-start.24 = (bf16[1,56,384]{2,1,0:T(8,128)(2,1)S(1)}, bf16[1,56,384]{2,1,0:T(8,128)(2,1)S(1)}, u32[]{:S(2)}, u32[]{:S(2)}) collective-permute-start(bf16[1,56,384]{2,1,0:T(8,128)(2,1)S(1)} %get-tuple-element.185), channel_id=1, source_target_pairs={{0,6},{1,7},{2,4},{3,5},{4,2},{5,3},{6,0},{7,1},{8,14},{9,15},{10,... | collective-permute-start | bytes 129032 | tf_op jit(solution)/shard_map/ppermute | solution.py:730
  81.0 2.3 %collective-permute-done.22 = bf16[1,112,384]{2,1,0:T(8,128)(2,1)S(1)} collective-permute-done((bf16[1,112,384]{2,1,0:T(8,128)(2,1)S(1)}, bf16[1,112,384]{2,1,0:T(8,128)(2,1)S(1)}, u32[]{:S(2)}, u32[]{:S(2)}) %collective-permute-start.22) | collective-permute-done | bytes 86048 | tf_op jit(solution)/shard_map/ppermute | solution.py:730
  87.3 2.1 %collective-permute-start.26 = (bf16[1,56,384]{2,1,0:T(8,128)(2,1)S(1)}, bf16[1,56,384]{2,1,0:T(8,128)(2,1)S(1)}, u32[]{:S(2)}, u32[]{:S(2)}) collective-permute-start(bf16[1,56,384]{2,1,0:T(8,128)(2,1)S(1)} %add_convert_fusion.7), channel_id=1, source_target_pairs={{0,4},{1,5},{2,6},{3,7},{4,0},{5,1},{6,2},{7,3},{8,12},{9,13},{10,... | collective-permute-start | bytes 129032 | tf_op jit(solution)/shard_map/ppermute | solution.py:730
  91.4 2.3 %collective-permute-done.27 = bf16[1,56,384]{2,1,0:T(8,128)(2,1)S(1)} collective-permute-done((bf16[1,56,384]{2,1,0:T(8,128)(2,1)S(1)}, bf16[1,56,384]{2,1,0:T(8,128)(2,1)S(1)}, u32[]{:S(2)}, u32[]{:S(2)}) %collective-permute-start.27) | collective-permute-done | bytes 43040 | tf_op jit(solution)/shard_map/ppermute | solution.py:730
  93.8 4.4 %collective-permute-done.30 = bf16[4,112,384]{2,1,0:T(8,128)(2,1)S(1)} collective-permute-done((bf16[4,112,384]{2,1,0:T(8,128)(2,1)S(1)}, bf16[4,112,384]{2,1,0:T(8,128)(2,1)S(1)}, u32[]{:S(2)}, u32[]{:S(2)}) %collective-permute-start.30) | collective-permute-done | bytes 344096 | tf_op jit(solution)/shard_map/ppermute | solution.py:730
  98.3 4.6 %collective-permute-start.31 = (bf16[16,112,384]{2,1,0:T(8,128)(2,1)S(1)}, bf16[16,112,384]{2,1,0:T(8,128)(2,1)S(1)}, u32[]{:S(2)}, u32[]{:S(2)}) collective-permute-start(bf16[16,112,384]{2,1,0:T(8,128)(2,1)S(1)} %constant_dynamic-update-slice_fusion), channel_id=1, source_target_pairs={{0,8},{1,9},{2,10},{3,11},{4,12},{5,13},{6,14},{7,15},{8,0},{9,1},... | collective-permute-start | bytes 4128776 | tf_op jit(solution)/shard_map/ppermute | solution.py:730
  105.7 3.8 %shard_map.343 = (f32[1536,384]{1,0:T(8,128)}, f32[384,1536]{1,0:T(8,128)}, f32[384,384]{1,0:T(8,128)}, f32[384]{0:T(512)}, f32[384]{0:T(512)}, /*index=5*/f32[3...) custom-call(s32[1]{0:T(128)} %bitcast.11.refs_0_, s32[1]{0:T(128)} %bitcast.1.refs_2_.refs_1_, ...), custom_call_target="tpu_custom_call" | custom-call | flops 4000000000 | bytes 4000000 | tf_op jit(solution)/shard_map/pallas_call | solution.py:692
  109.5 4.0 %collective-permute-done.34 = bf16[4,56,384]{2,1,0:T(8,128)(2,1)S(1)} collective-permute-done((bf16[4,56,384]{2,1,0:T(8,128)(2,1)S(1)}, bf16[4,56,384]{2,1,0:T(8,128)(2,1)S(1)}, u32[]{:S(2)}, u32[]{:S(2)}) %collective-permute-start.34) | collective-permute-done | bytes 172064 | tf_op jit(solution)/shard_map/ppermute | solution.py:730
  114.9 1.8 %collective-permute-done.35 = bf16[16,56,384]{2,1,0:T(8,128)(2,1)S(1)} collective-permute-done((bf16[16,56,384]{2,1,0:T(8,128)(2,1)S(1)}, bf16[16,56,384]{2,1,0:T(8,128)(2,1)S(1)}, u32[]{:S(2)}, u32[]{:S(2)}) %collective-permute-start.35) | collective-permute-done | bytes 688160 | tf_op jit(solution)/shard_map/ppermute | solution.py:730
  116.6 3.8 %shard_map.344 = (f32[384,384]{1,0:T(8,128)}, f32[384]{0:T(512)}, f32[384,384]{1,0:T(8,128)}, f32[384]{0:T(512)}, f32[384,384]{1,0:T(8,128)}, /*index=5*/f32[384]{0:T(512)}, f32[512,384]{1,0:T(8,128)}) custom-call(s32[1]{0:T(128)} %bitcast.11.refs_0_, s32[1]{0:T(128)} %bitcast.1.refs_2_.refs_1_, bf16[896,384]{1,0:T(8,128)(2,1)S(1)} %bitcast.23, ...), custom_call_target="tpu_custom_call" | custom-call | flops 2000000000 | bytes 2000000 | tf_op jit(solution)/shard_map/pallas_call | solution.py:692
  (85 shorter events, 22.3 us)
Async XLA Ops:
  0.7 11.0 %collective-permute-start = (bf16[256,384]{1,0:T(8,128)(2,1)}, bf16[256,384]{1,0:T(8,128)(2,1)S(1)}, u32[]{:S(2)}, u32[]{:S(2)}) collective-permute-start(bf16[256,384]{1,0:T(8,128)(2,1)} %bitcast.40), channel_id=1, source_target_pairs={{0,8},{8,0},{16,24},{24,16},{1,9},{9,1},{17,25},{25,17},{2,10},{10... | collective-permute-start | bytes 589832 | tf_op jit(solution)/shard_map/ppermute | solution.py:864
  1.4 10.3 %collective-permute-start.1 = (bf16[256,384]{1,0:T(8,128)(2,1)}, bf16[256,384]{1,0:T(8,128)(2,1)S(1)}, u32[]{:S(2)}, u32[]{:S(2)}) collective-permute-start(bf16[256,384]{1,0:T(8,128)(2,1)} %bitcast.41), channel_id=1, source_target_pairs={{0,16},{8,24},{16,0},{24,8},{1,17},{9,25},{17,1},{25,9},{2,18},{10... | collective-permute-start | bytes 589832 | tf_op jit(solution)/shard_map/ppermute | solution.py:864
  2.7 9.8 %collective-permute-start.2 = (bf16[256,384]{1,0:T(8,128)(2,1)}, bf16[256,384]{1,0:T(8,128)(2,1)S(1)}, u32[]{:S(2)}, u32[]{:S(2)}) collective-permute-start(bf16[256,384]{1,0:T(8,128)(2,1)} %bitcast.42), channel_id=1, source_target_pairs={{0,24},{8,16},{16,8},{24,0},{1,25},{9,17},{17,9},{25,1},{2,26},{10... | collective-permute-start | bytes 589832 | tf_op jit(solution)/shard_map/ppermute | solution.py:864
  29.8 7.9 %collective-permute-start.6 = (bf16[288,384]{1,0:T(8,128)(2,1)S(1)}, bf16[288,384]{1,0:T(8,128)(2,1)S(1)}, u32[]{:S(2)}, u32[]{:S(2)}) collective-permute-start(bf16[288,384]{1,0:T(8,128)(2,1)S(1)} %get-tuple-element.114.refs_3_.refs_8_), channel_id=1, source_target_pairs={{0,16},{8,24},{16,0},{24,8},{1,17},{9,25},{17,1},{25,9},{2,18},{10... | collective-permute-start | bytes 663560 | tf_op jit(solution)/shard_map/ppermute | solution.py:864
  31.1 10.6 %collective-permute-start.5 = (bf16[288,384]{1,0:T(8,128)(2,1)S(1)}, bf16[288,384]{1,0:T(8,128)(2,1)S(1)}, u32[]{:S(2)}, u32[]{:S(2)}) collective-permute-start(bf16[288,384]{1,0:T(8,128)(2,1)S(1)} %get-tuple-element.114.refs_3_.refs_8_), channel_id=1, source_target_pairs={{0,8},{8,0},{16,24},{24,16},{1,9},{9,1},{17,25},{25,17},{2,10},{10... | collective-permute-start | bytes 663560 | tf_op jit(solution)/shard_map/ppermute | solution.py:864
  31.6 9.5 %collective-permute-start.3 = (bf16[8,112,384]{2,1,0:T(8,128)(2,1)}, bf16[8,112,384]{2,1,0:T(8,128)(2,1)S(1)}, u32[]{:S(2)}, u32[]{:S(2)}) collective-permute-start(bf16[8,112,384]{2,1,0:T(8,128)(2,1)} %bitcast.36), channel_id=1, source_target_pairs={{0,8},{1,9},{2,10},{3,11},{4,12},{5,13},{6,14},{7,15},{8,0},{9,1},... | collective-permute-start | bytes 2064392 | tf_op jit(solution)/shard_map/ppermute | solution.py:730
  38.9 20.3 %collective-permute-start.10 = (bf16[4,112,384]{2,1,0:T(8,128)(2,1)}, bf16[4,112,384]{2,1,0:T(8,128)(2,1)}, u32[]{:S(2)}, u32[]{:S(2)}) collective-permute-start(bf16[4,112,384]{2,1,0:T(8,128)(2,1)} %get-tuple-element.192), channel_id=1, source_target_pairs={{0,17},{1,16},{2,19},{3,18},{4,21},{5,20},{6,23},{7,22},{8,25},{9,... | collective-permute-start | bytes 1032200 | tf_op jit(solution)/shard_map/ppermute | solution.py:730
  40.9 18.2 %collective-permute-start.9 = (bf16[4,112,384]{2,1,0:T(8,128)(2,1)}, bf16[4,112,384]{2,1,0:T(8,128)(2,1)}, u32[]{:S(2)}, u32[]{:S(2)}) collective-permute-start(bf16[4,112,384]{2,1,0:T(8,128)(2,1)} %get-tuple-element.193), channel_id=1, source_target_pairs={{0,1},{1,0},{2,3},{3,2},{4,5},{5,4},{6,7},{7,6},{8,9},{9,8},{10,11... | collective-permute-start | bytes 1032200 | tf_op jit(solution)/shard_map/ppermute | solution.py:730
  41.3 17.9 %collective-permute-start.8 = (bf16[4,112,384]{2,1,0:T(8,128)(2,1)S(1)}, bf16[4,112,384]{2,1,0:T(8,128)(2,1)}, u32[]{:S(2)}, u32[]{:S(2)}) collective-permute-start(bf16[4,112,384]{2,1,0:T(8,128)(2,1)S(1)} %fusion.2), channel_id=1, source_target_pairs={{0,16},{1,17},{2,18},{3,19},{4,20},{5,21},{6,22},{7,23},{8,24},{9,... | collective-permute-start | bytes 1032200 | tf_op jit(solution)/shard_map/ppermute | solution.py:730
  63.2 8.0 %collective-permute-start.19 = (bf16[1,112,384]{2,1,0:T(8,128)(2,1)S(1)}, bf16[1,112,384]{2,1,0:T(8,128)(2,1)S(1)}, u32[]{:S(2)}, u32[]{:S(2)}) collective-permute-start(bf16[1,112,384]{2,1,0:T(8,128)(2,1)S(1)} %get-tuple-element.181), channel_id=1, source_target_pairs={{0,6},{1,7},{2,4},{3,5},{4,2},{5,3},{6,0},{7,1},{8,14},{9,15},{10,... | collective-permute-start | bytes 258056 | tf_op jit(solution)/shard_map/ppermute | solution.py:730
  63.4 7.8 %collective-permute-start.12 = (bf16[4,56,384]{2,1,0:T(8,128)(2,1)S(1)}, bf16[4,56,384]{2,1,0:T(8,128)(2,1)S(1)}, u32[]{:S(2)}, u32[]{:S(2)}) collective-permute-start(bf16[4,56,384]{2,1,0:T(8,128)(2,1)S(1)} %add_convert_fusion.2), channel_id=1, source_target_pairs={{0,16},{1,17},{2,18},{3,19},{4,20},{5,21},{6,22},{7,23},{8,24},{9,... | collective-permute-start | bytes 516104 | tf_op jit(solution)/shard_map/ppermute | solution.py:730
  64.2 10.8 %collective-permute-start.14 = (bf16[4,56,384]{2,1,0:T(8,128)(2,1)S(1)}, bf16[4,56,384]{2,1,0:T(8,128)(2,1)S(1)}, u32[]{:S(2)}, u32[]{:S(2)}) collective-permute-start(bf16[4,56,384]{2,1,0:T(8,128)(2,1)S(1)} %get-tuple-element.190), channel_id=1, source_target_pairs={{0,1},{1,0},{2,3},{3,2},{4,5},{5,4},{6,7},{7,6},{8,9},{9,8},{10,11... | collective-permute-start | bytes 516104 | tf_op jit(solution)/shard_map/ppermute | solution.py:730
  65.5 9.5 %collective-permute-start.15 = (bf16[4,56,384]{2,1,0:T(8,128)(2,1)S(1)}, bf16[4,56,384]{2,1,0:T(8,128)(2,1)S(1)}, u32[]{:S(2)}, u32[]{:S(2)}) collective-permute-start(bf16[4,56,384]{2,1,0:T(8,128)(2,1)S(1)} %get-tuple-element.191), channel_id=1, source_target_pairs={{0,17},{1,16},{2,19},{3,18},{4,21},{5,20},{6,23},{7,22},{8,25},{9,... | collective-permute-start | bytes 516104 | tf_op jit(solution)/shard_map/ppermute | solution.py:730
  72.3 8.6 %collective-permute-start.20 = (bf16[1,112,384]{2,1,0:T(8,128)(2,1)S(1)}, bf16[1,112,384]{2,1,0:T(8,128)(2,1)S(1)}, u32[]{:S(2)}, u32[]{:S(2)}) collective-permute-start(bf16[1,112,384]{2,1,0:T(8,128)(2,1)S(1)} %add_convert_fusion.3), channel_id=1, source_target_pairs={{0,2},{1,3},{2,0},{3,1},{4,6},{5,7},{6,4},{7,5},{8,10},{9,11},{10,... | collective-permute-start | bytes 258056 | tf_op jit(solution)/shard_map/ppermute | solution.py:730
  72.4 8.6 %collective-permute-start.21 = (bf16[1,112,384]{2,1,0:T(8,128)(2,1)S(1)}, bf16[1,112,384]{2,1,0:T(8,128)(2,1)S(1)}, u32[]{:S(2)}, u32[]{:S(2)}) collective-permute-start(bf16[1,112,384]{2,1,0:T(8,128)(2,1)S(1)} %add_convert_fusion.3), channel_id=1, source_target_pairs={{0,4},{1,5},{2,6},{3,7},{4,0},{5,1},{6,2},{7,3},{8,12},{9,13},{10,... | collective-permute-start | bytes 258056 | tf_op jit(solution)/shard_map/ppermute | solution.py:730
  74.5 8.8 %collective-permute-start.22 = (bf16[1,112,384]{2,1,0:T(8,128)(2,1)S(1)}, bf16[1,112,384]{2,1,0:T(8,128)(2,1)S(1)}, u32[]{:S(2)}, u32[]{:S(2)}) collective-permute-start(bf16[1,112,384]{2,1,0:T(8,128)(2,1)S(1)} %add_convert_fusion.3), channel_id=1, source_target_pairs={{0,6},{1,7},{2,4},{3,5},{4,2},{5,3},{6,0},{7,1},{8,14},{9,15},{10,... | collective-permute-start | bytes 258056 | tf_op jit(solution)/shard_map/ppermute | solution.py:730
  76.2 10.1 %collective-permute-start.23 = (bf16[1,56,384]{2,1,0:T(8,128)(2,1)S(1)}, bf16[1,56,384]{2,1,0:T(8,128)(2,1)S(1)}, u32[]{:S(2)}, u32[]{:S(2)}) collective-permute-start(bf16[1,56,384]{2,1,0:T(8,128)(2,1)S(1)} %get-tuple-element.184), channel_id=1, source_target_pairs={{0,4},{1,5},{2,6},{3,7},{4,0},{5,1},{6,2},{7,3},{8,12},{9,13},{10,... | collective-permute-start | bytes 129032 | tf_op jit(solution)/shard_map/ppermute | solution.py:730
  79.6 6.7 %collective-permute-start.24 = (bf16[1,56,384]{2,1,0:T(8,128)(2,1)S(1)}, bf16[1,56,384]{2,1,0:T(8,128)(2,1)S(1)}, u32[]{:S(2)}, u32[]{:S(2)}) collective-permute-start(bf16[1,56,384]{2,1,0:T(8,128)(2,1)S(1)} %get-tuple-element.185), channel_id=1, source_target_pairs={{0,6},{1,7},{2,4},{3,5},{4,2},{5,3},{6,0},{7,1},{8,14},{9,15},{10,... | collective-permute-start | bytes 129032 | tf_op jit(solution)/shard_map/ppermute | solution.py:730
  83.7 10.0 %collective-permute-start.28 = (bf16[4,112,384]{2,1,0:T(8,128)(2,1)S(1)}, bf16[4,112,384]{2,1,0:T(8,128)(2,1)S(1)}, u32[]{:S(2)}, u32[]{:S(2)}) collective-permute-start(bf16[4,112,384]{2,1,0:T(8,128)(2,1)S(1)} %pad_maximum_fusion), channel_id=1, source_target_pairs={{0,16},{1,17},{2,18},{3,19},{4,20},{5,21},{6,22},{7,23},{8,24},{9,... | collective-permute-start | bytes 1032200 | tf_op jit(solution)/shard_map/ppermute | solution.py:730
  84.3 9.4 %collective-permute-start.29 = (bf16[4,112,384]{2,1,0:T(8,128)(2,1)S(1)}, bf16[4,112,384]{2,1,0:T(8,128)(2,1)S(1)}, u32[]{:S(2)}, u32[]{:S(2)}) collective-permute-start(bf16[4,112,384]{2,1,0:T(8,128)(2,1)S(1)} %pad_maximum_fusion), channel_id=1, source_target_pairs={{0,1},{1,0},{2,3},{3,2},{4,5},{5,4},{6,7},{7,6},{8,9},{9,8},{10,11... | collective-permute-start | bytes 1032200 | tf_op jit(solution)/shard_map/ppermute | solution.py:730
  85.6 12.7 %collective-permute-start.30 = (bf16[4,112,384]{2,1,0:T(8,128)(2,1)S(1)}, bf16[4,112,384]{2,1,0:T(8,128)(2,1)S(1)}, u32[]{:S(2)}, u32[]{:S(2)}) collective-permute-start(bf16[4,112,384]{2,1,0:T(8,128)(2,1)S(1)} %pad_maximum_fusion), channel_id=1, source_target_pairs={{0,17},{1,16},{2,19},{3,18},{4,21},{5,20},{6,23},{7,22},{8,25},{9,... | collective-permute-start | bytes 1032200 | tf_op jit(solution)/shard_map/ppermute | solution.py:730
  98.3 7.4 %collective-permute-start.31 = (bf16[16,112,384]{2,1,0:T(8,128)(2,1)S(1)}, bf16[16,112,384]{2,1,0:T(8,128)(2,1)S(1)}, u32[]{:S(2)}, u32[]{:S(2)}) collective-permute-start(bf16[16,112,384]{2,1,0:T(8,128)(2,1)S(1)} %constant_dynamic-update-slice_fusion), channel_id=1, source_target_pairs={{0,8},{1,9},{2,10},{3,11},{4,12},{5,13},{6,14},{7,15},{8,0},{9,1},... | collective-permute-start | bytes 4128776 | tf_op jit(solution)/shard_map/ppermute | solution.py:730
  102.9 6.6 %collective-permute-start.32 = (bf16[4,56,384]{2,1,0:T(8,128)(2,1)S(1)}, bf16[4,56,384]{2,1,0:T(8,128)(2,1)S(1)}, u32[]{:S(2)}, u32[]{:S(2)}) collective-permute-start(bf16[4,56,384]{2,1,0:T(8,128)(2,1)S(1)} %pad_maximum_fusion.1), channel_id=1, source_target_pairs={{0,16},{1,17},{2,18},{3,19},{4,20},{5,21},{6,22},{7,23},{8,24},{9,... | collective-permute-start | bytes 516104 | tf_op jit(solution)/shard_map/ppermute | solution.py:730
  104.9 8.7 %collective-permute-start.34 = (bf16[4,56,384]{2,1,0:T(8,128)(2,1)S(1)}, bf16[4,56,384]{2,1,0:T(8,128)(2,1)S(1)}, u32[]{:S(2)}, u32[]{:S(2)}) collective-permute-start(bf16[4,56,384]{2,1,0:T(8,128)(2,1)S(1)} %pad_maximum_fusion.1), channel_id=1, source_target_pairs={{0,17},{1,16},{2,19},{3,18},{4,21},{5,20},{6,23},{7,22},{8,25},{9,... | collective-permute-start | bytes 516104 | tf_op jit(solution)/shard_map/ppermute | solution.py:730
  (16 other events, 84.9 us)
where the time goes:
time: 122 us; the launch traced here: 121 us
  Pallas kernels  54.3 us (45%)
  starting transfers between devices  35 us (29%)
  waiting for transfers between devices  23.9 us (20%)
  other arithmetic  5.19 us (4%)
  between operations  1.76 us (1%)
    pallas_call x6, Pallas kernels, call(): pl.pallas_call(body, out_shape=[pltpu.VMEM(out[0], out[1]) if kept else p...  54.3 us
    ppermute x30, starting transfers between devices, send(): return lax.ppermute(values, ('blk', 'dp'), self.pairs(mask))  30.7 us
    ppermute x30, waiting for transfers between devices, send(): return lax.ppermute(values, ('blk', 'dp'), self.pairs(mask))  23.2 us
    convert_element_type x8, other arithmetic, total(): return sum((span.astype(F32) for span in spans)).astype(BF)  4.82 us
    ppermute x6, starting transfers between devices, along(): return lax.ppermute(values, 'blk', [(i, i ^ bit) for i in range(blk_count)])  4.34 us
  transfers between devices with their start and end apart: 36, of which 10 were waited for; matrix products, arithmetic and copies ran while one was open for 4% of the time, Pallas kernels for 27%

commit v1 on v0

--- a/solution.py
+++ b/solution.py
@@ -1,3 +1,4 @@
+import functools
 import math
 
 import jax
@@ -367,6 +368,8 @@
 
     for chunk in range(chunks):
         back(chunk, 0)
+    early_sends = (early_send_low, early_send_high)
+    push_half(0, block % 2, place_ref[0], grads_out, early_sends, early_keep)
     grad_normed = sums_ref[...].astype(BF).astype(F32)
     grad_first = norm_backward(grad_normed * as_row(first_gain), first_hat, first_rate)
     first_store.ref[...] = grad_first
@@ -378,7 +381,7 @@
     ):
         small_ref[3 + chunks + k : 4 + chunks + k, :] = values
     grads_out[small_at : small_at + 16, :] = small_ref[...].astype(BF)
-    push_halves(block % 2, place_ref[0], grads_out, (early_send_low, early_send_high), early_keep)
+    push_half(1, block % 2, place_ref[0], grads_out, early_sends, early_keep)
     grad_mixture = nt(grad_branch, output_weight[...]).astype(BF)
     sent_out[:size, :] = grad_mixture
     along = grad_mixture.astype(F32) * mixture_ref[...]
@@ -513,6 +516,8 @@
     grads_out[0:model_width, :] = (tn(tokens, grad_query[...]) + tt(table, query_low)).astype(BF)
     grads_out[model_width : 2 * model_width, :] = (tn(tokens, grad_key) + tt(table, key_low)).astype(BF)
     grads_out[2 * model_width : 3 * model_width, :] = tn(tokens, grad_value).astype(BF)
+    late_sends = (late_send_low, late_send_high)
+    push_half(0, block % 2, place_ref[0], grads_out, late_sends, late_keep)
     table_at = 3 * model_width
     query_weight, key_weight, value_weight, grad_first = ready(query_weight, key_weight, value_weight, grad_first)
     grads_out[table_at : table_at + rel, :] = (
@@ -534,7 +539,7 @@
         jnp.zeros((13, model_width), F32),
     ]
     grads_out[small_at : small_at + 16, :] = jnp.concatenate(small, axis=0).astype(BF)
-    push_halves(block % 2, place_ref[0], grads_out, (late_send_low, late_send_high), late_keep)
+    push_half(1, block % 2, place_ref[0], grads_out, late_sends, late_keep)
     tokens_store.ref[...] = (
         nt(grad_query[...], query_weight[...])
         + nt(grad_key, key_weight[...])
@@ -595,27 +600,35 @@
 
 class Raw:
     def __init__(self, target, sems):
-        self.target, self.sems, self.copies = target, sems, []
+        self.target, self.sems = target, sems
         self.shape = target.shape
 
-    def push_from(self, source, there):
-        copy = pltpu.make_async_copy(source, self.target.at[there], self.sems.at[len(self.copies)])
-        copy.start()
-        self.copies.append(copy)
+    def push_from(self, source, k, part):
+        pltpu.make_async_copy(source, self.target.at[pl.ds(k * part, part)], self.sems.at[k]).start()
+        self.part = part
 
     def finish(self):
-        for copy in self.copies:
-            copy.wait()
-
-
-def push_halves(core, place, rows_ref, sends, keep):
+        for k in range(self.shape[0] // self.part):
+            there = self.target.at[pl.ds(k * self.part, self.part)]
+            pltpu.make_async_copy(there, there, self.sems.at[k]).wait()
+
+
+def push_half(which, core, place, rows_ref, sends, keep):
     half = keep.shape[0]
     part = half // 4
-    for k in range(4):
-        at = (place ^ k) * part
-        send, there = sends[k // 2], pl.ds(k % 2 * part, part)
-        send.push_from(rows_ref.at[pl.ds(pl.multiple_of((1 - core) * half + at, 16), part)], there)
-        keep.push_from(rows_ref.at[pl.ds(pl.multiple_of(core * half + at, 16), part)], pl.ds(k * part, part))
+
+    def source(k):
+        return rows_ref.at[pl.ds(pl.multiple_of(which * half + (place ^ k) * part, 16), part)]
+
+    @pl.when(core == which)
+    def _():
+        for k in range(4):
+            keep.push_from(source(k), k, part)
+
+    @pl.when(core != which)
+    def _():
+        for k in range(4):
+            sends[k // 2].push_from(source(k), k % 2, part)
 
 
 class Kept:
@@ -825,23 +838,65 @@
     vector(output_bias, 5 + chunks)
 
 
-def late_kernel(
-    core_ref, place_ref, held, arrived,
-    query_weight, query_bias, key_weight, key_bias, value_weight, value_bias, relative,
-    both_ref,
-):
-    halves_to_scratch(core_ref, place_ref, held, arrived, both_ref)
-    width = query_weight.shape[0]
+def late_kernel(mine, shapes, core_ref, place_ref, held, *rest):
+    outs, (rows_ref, wide_ref, vector_ref, sems) = rest[-11:-4], rest[-4:]
+    query_weight, query_bias, key_weight, key_bias, value_weight, value_bias, relative = outs
+    half, width = rows_ref.shape
+    part = half // 4
     rel = relative.shape[0]
-    for k, out in enumerate((query_weight, key_weight, value_weight)):
-        out.ref[...] = both_ref[k * width : (k + 1) * width, :].astype(F32)
-        out.push()
-    at = 3 * width
-    relative.ref[...] = both_ref[at : at + rel, :].astype(F32)
-    small = both_ref[at + rel : at + rel + 16, :].astype(F32)
-    query_bias.ref[...] = small[0, :]
-    key_bias.ref[...] = small[1, :]
-    value_bias.ref[...] = small[2, :]
+    for k in range(4):
+        at = pl.multiple_of((place_ref[0] ^ k) * part, 16)
+        rows_ref[pl.ds(at, part), :] = held[k * part : (k + 1) * part, :]
+    split = half - 2 * width
+    which = core_ref[0] if mine else 1 - core_ref[0]
+
+    def copy(spans):
+        copies = []
+        for k, (at, rows, out, start) in enumerate(spans):
+            wide_ref[at : at + rows, :] = rows_ref[at : at + rows, :].astype(F32)
+            one = pltpu.make_async_copy(wide_ref.at[pl.ds(at, rows)], out.at[pl.ds(start, rows)], sems.at[k])
+            one.start()
+            copies.append(one)
+        return copies
+
+    @pl.when(which == 0)
+    def _():
+        spans = ((0, width, query_weight, 0), (width, width, key_weight, 0), (2 * width, split, value_weight, 0))
+        for one in copy(spans):
+            one.wait()
+
+    @pl.when(which == 1)
+    def _():
+        rest_rows = width - split
+        copies = copy(((rest_rows, rel, relative, 0), (0, rest_rows, value_weight, split)))
+        small = rows_ref[rest_rows + rel : rest_rows + rel + 16, :].astype(F32)
+        for k, out in enumerate((query_bias, key_bias, value_bias)):
+            vector_ref[k, :] = small[k, :]
+            one = pltpu.make_async_copy(vector_ref.at[k], out, sems.at[2 + k])
+            one.start()
+            copies.append(one)
+        for one in copies:
+            one.wait()
+
+
+def late_call(mine, shapes, core, place, held, *before):
+    hbm, smem = pl.BlockSpec(memory_space=pltpu.HBM), pl.BlockSpec(memory_space=pltpu.SMEM)
+    width = held.shape[1]
+    return pl.pallas_call(
+        functools.partial(late_kernel, mine, shapes),
+        out_shape=[pltpu.HBM(shape, F32) for shape in shapes],
+        in_specs=[smem, smem, pl.BlockSpec(memory_space=pltpu.VMEM)] + [hbm] * len(before),
+        out_specs=[hbm] * len(shapes),
+        scratch_shapes=[
+            pltpu.VMEM(held.shape, BF),
+            pltpu.VMEM(held.shape, F32),
+            pltpu.VMEM((8, width), F32),
+            pltpu.SemaphoreType.DMA((5,)),
+        ],
+        input_output_aliases={3 + k: k for k in range(len(before))},
+        compiler_params=pltpu.CompilerParams(vmem_limit_bytes=10 * MIB),
+        cost_estimate=pl.CostEstimate(flops=2 * 10**9, bytes_accessed=2 * 10**6, transcendentals=0),
+    )(core, place, pltpu.with_memory_space_constraint(held, pltpu.VMEM), *before)
 
 
 def on_device(
@@ -964,22 +1019,22 @@
     for group in chips[1:]:
         sending, early_terms = group.scatter(early_terms)
         late_parts = [terms_after(sending, terms) for terms in late_parts]
-    sending, late_terms = first_scatter(late_parts)
-    first_arrived = late_terms[1 - chips[0].size][0]
-    early_held = total(terms_after(first_arrived, early_terms))
+    sending_xy, late_terms = first_scatter(late_parts)
+    arrived = [array for array, _, _ in late_terms[1 - chips[0].size :]]
+    early_held = total(early_terms)
     for group in reversed(chips[2:]):
         early_held = group.gather(early_held)
     early_parts = chips[1].pieces(early_held)
     for group in chips[1:]:
-        sending, late_terms = group.scatter(late_terms)
-    first_arrived = late_terms[1 - chips[-1].size][0]
-    early_pieces = chips[0].pieces(chips[1].arrange(in_order(first_arrived, early_parts)))
+        sending_z, late_terms = group.scatter(late_terms)
+    z_arrived = [array for array, _, _ in late_terms[1 - chips[-1].size :]]
+    early_parts = in_order(z_arrived[0], early_parts)
+    early_pieces = chips[0].pieces(chips[1].arrange(early_parts))
     late_held = total(late_terms)
     for group in reversed(chips[2:]):
         late_held = group.gather(late_held)
     late_parts = chips[1].pieces(late_held)
-    late_parts, early_first = lax.optimization_barrier((late_parts, early_pieces[1]))
-    early_pieces[1] = early_first
+    late_parts, early_pieces[1] = lax.optimization_barrier((late_parts, early_pieces[1]))
     late_held = chips[1].arrange(late_parts)
     early_held = jnp.concatenate(early_pieces, axis=0)
     late_pieces = chips[0].pieces(late_held)
@@ -997,15 +1052,12 @@
         scalars=2, micros=4, vmem=14,
     )
     late_held = jnp.concatenate(in_order(g_output_bias, late_pieces), axis=0)
+    own_half, other_half = (flat(piece) for piece in groups[0].pieces(late_held))
+    shapes = [square[0], vector[0]] * 3 + [(rel, width)]
+    late_grads = late_call(True, shapes, my_core, place, own_half)
     (
         g_query_weight, g_query_bias, g_key_weight, g_key_bias, g_value_weight, g_value_bias, g_relative,
-    ) = call(
-        late_kernel,
-        [square, vector, square, vector, square, vector, ((rel, width), F32)],
-        [((LATE_ROWS, width), BF)],
-        my_core, place, *(Kept(flat(piece)) for piece in groups[0].pieces(late_held)),
-        scalars=2, micros=2, vmem=10,
-    )
+    ) = late_call(False, shapes, my_core, place, other_half, *late_grads)
     return (
         layer_out[None], grad_tokens[None], g_query_weight, g_query_bias, g_key_weight, g_key_bias,
         g_value_weight, g_value_bias, g_output_weight, g_output_bias, g_first_gain, g_first_bias,

time: 122 us -> 118 us (0.967); the launches traced: 121 us -> 118 us
  Pallas kernels: 54.3 us -> 52.2 us
    pallas_call x6 -> x5, Pallas kernels: 54.3 us -> 49.8 us  [call(): pl.pallas_call(body, out_shape=[pltpu.VMEM(out[0], out[1]) if kept else p...]
    pallas_call x0 -> x2, Pallas kernels: none -> 2.38 us  [late_call(): pl.pallas_call(functools.partial(late_kernel, mine, shapes), out_shape=[p...]
  transfers between devices with their start and end apart: 36 -> 36, of which waited for: 10 -> 9; matrix products, arithmetic and copies ran while one was open for 4% -> 5% of each run, Pallas kernels for 27% -> 29%
where the time goes in v1:
time: 118 us
  Pallas kernels  52.2 us (44%)
  starting transfers between devices  35 us (30%)
  waiting for transfers between devices  23.4 us (20%)
  other arithmetic  5.19 us (4%)
  between operations  1.77 us (2%)
    pallas_call x5, Pallas kernels, call(): pl.pallas_call(body, out_shape=[pltpu.VMEM(out[0], out[1]) if kept else p...  49.8 us
    ppermute x30, starting transfers between devices, send(): return lax.ppermute(values, ('blk', 'dp'), self.pairs(mask))  30.6 us
    ppermute x30, waiting for transfers between devices, send(): return lax.ppermute(values, ('blk', 'dp'), self.pairs(mask))  22.6 us
    convert_element_type x8, other arithmetic, total(): return sum((span.astype(F32) for span in spans)).astype(BF)  4.82 us
    ppermute x6, starting transfers between devices, along(): return lax.ppermute(values, 'blk', [(i, i ^ bit) for i in range(blk_count)])  4.35 us
    pallas_call x2, Pallas kernels, late_call(): pl.pallas_call(functools.partial(late_kernel, mine, shapes), out_shape=[p...  2.38 us
  transfers between devices with their start and end apart: 36, of which 9 were waited for; matrix products, arithmetic and copies ran while one was open for 5% of the time, Pallas kernels for 29%

profile of v1, /device:TPU:9, one launch (start us, length us, event | category | flops | bytes accessed | tf_op | source)
XLA Modules:
  0.0 117.8 jit_solution(14664925456913891053)
XLA Ops:
  1.4 1.3 %collective-permute-start.1 = (bf16[256,384]{1,0:T(8,128)(2,1)}, bf16[256,384]{1,0:T(8,128)(2,1)S(1)}, u32[]{:S(2)}, u32[]{:S(2)}) collective-permute-start(bf16[256,384]{1,0:T(8,128)(2,1)} %bitcast.41), channel_id=1, source_target_pairs={{0,16},{8,24},{16,0},{24,8},{1,17},{9,25},{17,1},{25,9},{2,18},{10... | collective-permute-start | bytes 589832 | tf_op jit(solution)/shard_map/ppermute | solution.py:919
  3.1 7.9 %shard_map.339 = (bf16[512,384]{1,0:T(8,128)(2,1)S(1)}, bf16[512,384]{1,0:T(8,128)(2,1)S(1)}, f32[3,512,1024]{2,1,0:T(8,128)}, bf16[512,384]{1,0:T(8,128)(2,1)S(...) custom-call(s32[1]{0:T(128)} %bitcast.refs_0_, ...), custom_call_target="tpu_custom_call" | custom-call | flops 8999999488 | bytes 9000000 | tf_op jit(solution)/shard_map/pallas_call | solution.py:705
  12.5 16.9 %shard_map.340 = (f32[256,384]{1,0:T(8,128)}, f32[256,384]{1,0:T(8,128)S(1)}, bf16[3,512,1024]{2,1,0:T(8,128)(2,1)S(1)}, bf16[288,384]{1,0:T(8,128)(2,1)S(1)}, f...) custom-call(s32[1]{0:T(128)} %bitcast.refs_0_, ...), custom_call_target="tpu_custom_call" | custom-call | flops 20000000000 | bytes 20000000 | tf_op jit(solution)/shard_map/pallas_call | solution.py:705
  29.3 1.3 %collective-permute-start.6 = (bf16[288,384]{1,0:T(8,128)(2,1)S(1)}, bf16[288,384]{1,0:T(8,128)(2,1)S(1)}, u32[]{:S(2)}, u32[]{:S(2)}) collective-permute-start(bf16[288,384]{1,0:T(8,128)(2,1)S(1)} %get-tuple-element.113.refs_3_.refs_8_), channel_id=1, source_target_pairs={{0,16},{8,24},{16,0},{24,8},{1,17},{9,25},{17,1},{25,9},{2,18},{10... | collective-permute-start | bytes 663560 | tf_op jit(solution)/shard_map/ppermute | solution.py:919
  31.7 5.5 %shard_map.341 = (bf16[256,384]{1,0:T(8,128)(2,1)S(1)}, f32[384,512]{1,0:T(8,128)S(1)}) custom-call(s32[1]{0:T(128)} %bitcast.refs_0_, bf16[512,384]{1,0:T(8,128)(2,1)S(1)} %get-tuple-element.97.refs_8_.refs_1_.refs_5_, bf16[1024,384]{1,0:T(8,128)(2,1)S(1)} %get-tuple-element.111.refs_2_.refs_6_, bf16[288,384]{1,0:T(8,128)(2,1)S(1)} %get-tuple-element.113.refs_3_.refs_8_, ...), custom_call_target="tpu_custom_call" | custom-call | flops 8000000000 | bytes 8000000 | tf_op jit(solution)/shard_map/pallas_call | solution.py:705
  38.4 2.1 %collective-permute-start.10 = (bf16[4,112,384]{2,1,0:T(8,128)(2,1)}, bf16[4,112,384]{2,1,0:T(8,128)(2,1)}, u32[]{:S(2)}, u32[]{:S(2)}) collective-permute-start(bf16[4,112,384]{2,1,0:T(8,128)(2,1)} %get-tuple-element.190), channel_id=1, source_target_pairs={{0,17},{1,16},{2,19},{3,18},{4,21},{5,20},{6,23},{7,22},{8,25},{9,... | collective-permute-start | bytes 1032200 | tf_op jit(solution)/shard_map/ppermute | solution.py:743
  41.2 15.7 %shard_map.342 = (f32[256,384]{1,0:T(8,128)}, bf16[448,384]{1,0:T(8,128)(2,1)}, bf16[448,384]{1,0:T(8,128)(2,1)}, bf16[896,384]{1,0:T(8,128)(2,1)}) custom-call(s32[1]{0:T(128)} %bitcast.refs_0_, s32[1]{0:T(128)S(6)} %copy.62.refs_1_, s32[1]{0:T(128)} %bitcast.1.refs_2_.refs_1_.place_ref, bf16[512,384]{1,0:T(8,128)(2,1)S(1)} %get-tuple-element.96.refs_7_.refs_3_, ...), custom_call_target="tpu_custom_call" | custom-call | flops 16999999488 | bytes 17000000 | tf_op jit(solution)/shard_map/pallas_call | solution.py:705
  57.0 1.4 %collective-permute-start.11 = (bf16[8,56,384]{2,1,0:T(8,128)(2,1)}, bf16[8,56,384]{2,1,0:T(8,128)(2,1)S(1)}, u32[]{:S(2)}, u32[]{:S(2)}) collective-permute-start(bf16[8,56,384]{2,1,0:T(8,128)(2,1)} %bitcast.39), channel_id=1, source_target_pairs={{0,8},{1,9},{2,10},{3,11},{4,12},{5,13},{6,14},{7,15},{8,0},{9,1},... | collective-permute-start | bytes 1032200 | tf_op jit(solution)/shard_map/ppermute | solution.py:743
  58.5 1.5 %add_convert_fusion.4 = (bf16[1,112,384]{2,1,0:T(8,128)(2,1)S(1)}, bf16[1,112,384]{2,1,0:T(8,128)(2,1)S(1)}, bf16[1,112,384]{2,1,0:T(8,128)(2,1)S(1)}) fusion(bf16[4,112,384]{2,1,0:T(8,128)(2,1)} %collective-permute-done.10, s32[]{:T(128)S(6)} %select_n.150, bf16[4,112,384]{2,1,0:T(8,128)(2,1)} %collective-permute-done.9, ...), kind=kLoop, calls=%fused_computation.12 | loop fusion | flops 1290240 | bytes 1548324 | tf_op jit(solution)/shard_map/convert_element_type | solution.py:788
  60.2 2.3 %collective-permute-start.18 = (bf16[1,112,384]{2,1,0:T(8,128)(2,1)S(1)}, bf16[1,112,384]{2,1,0:T(8,128)(2,1)S(1)}, u32[]{:S(2)}, u32[]{:S(2)}) collective-permute-start(bf16[1,112,384]{2,1,0:T(8,128)(2,1)S(1)} %get-tuple-element.180), channel_id=1, source_target_pairs={{0,4},{1,5},{2,6},{3,7},{4,0},{5,1},{6,2},{7,3},{8,12},{9,13},{10,... | collective-permute-start | bytes 258056 | tf_op jit(solution)/shard_map/ppermute | solution.py:743
  63.6 1.3 %collective-permute-start.14 = (bf16[4,56,384]{2,1,0:T(8,128)(2,1)S(1)}, bf16[4,56,384]{2,1,0:T(8,128)(2,1)S(1)}, u32[]{:S(2)}, u32[]{:S(2)}) collective-permute-start(bf16[4,56,384]{2,1,0:T(8,128)(2,1)S(1)} %get-tuple-element.188), channel_id=1, source_target_pairs={{0,1},{1,0},{2,3},{3,2},{4,5},{5,4},{6,7},{7,6},{8,9},{9,8},{10,11... | collective-permute-start | bytes 516104 | tf_op jit(solution)/shard_map/ppermute | solution.py:743
  66.6 3.9 %collective-permute-done.19 = bf16[1,112,384]{2,1,0:T(8,128)(2,1)S(1)} collective-permute-done((bf16[1,112,384]{2,1,0:T(8,128)(2,1)S(1)}, bf16[1,112,384]{2,1,0:T(8,128)(2,1)S(1)}, u32[]{:S(2)}, u32[]{:S(2)}) %collective-permute-start.19) | collective-permute-done | bytes 86048 | tf_op jit(solution)/shard_map/ppermute | solution.py:743
  71.7 2.1 %collective-permute-start.21 = (bf16[1,112,384]{2,1,0:T(8,128)(2,1)S(1)}, bf16[1,112,384]{2,1,0:T(8,128)(2,1)S(1)}, u32[]{:S(2)}, u32[]{:S(2)}) collective-permute-start(bf16[1,112,384]{2,1,0:T(8,128)(2,1)S(1)} %add_convert_fusion.3), channel_id=1, source_target_pairs={{0,4},{1,5},{2,6},{3,7},{4,0},{5,1},{6,2},{7,3},{8,12},{9,13},{10,... | collective-permute-start | bytes 258056 | tf_op jit(solution)/shard_map/ppermute | solution.py:743
  77.2 5.9 %collective-permute-done.22 = bf16[1,112,384]{2,1,0:T(8,128)(2,1)S(1)} collective-permute-done((bf16[1,112,384]{2,1,0:T(8,128)(2,1)S(1)}, bf16[1,112,384]{2,1,0:T(8,128)(2,1)S(1)}, u32[]{:S(2)}, u32[]{:S(2)}) %collective-permute-start.22) | collective-permute-done | bytes 86048 | tf_op jit(solution)/shard_map/ppermute | solution.py:743
  84.1 1.2 %collective-permute-start.29 = (bf16[4,112,384]{2,1,0:T(8,128)(2,1)S(1)}, bf16[4,112,384]{2,1,0:T(8,128)(2,1)S(1)}, u32[]{:S(2)}, u32[]{:S(2)}) collective-permute-start(bf16[4,112,384]{2,1,0:T(8,128)(2,1)S(1)} %pad_maximum_fusion), channel_id=1, source_target_pairs={{0,1},{1,0},{2,3},{3,2},{4,5},{5,4},{6,7},{7,6},{8,9},{9,8},{10,11... | collective-permute-start | bytes 1032200 | tf_op jit(solution)/shard_map/ppermute | solution.py:743
  87.1 2.4 %collective-permute-start.26 = (bf16[1,56,384]{2,1,0:T(8,128)(2,1)S(1)}, bf16[1,56,384]{2,1,0:T(8,128)(2,1)S(1)}, u32[]{:S(2)}, u32[]{:S(2)}) collective-permute-start(bf16[1,56,384]{2,1,0:T(8,128)(2,1)S(1)} %add_convert_fusion.7), channel_id=1, source_target_pairs={{0,4},{1,5},{2,6},{3,7},{4,0},{5,1},{6,2},{7,3},{8,12},{9,13},{10,... | collective-permute-start | bytes 129032 | tf_op jit(solution)/shard_map/ppermute | solution.py:743
  90.3 1.2 %collective-permute-start.27 = (bf16[1,56,384]{2,1,0:T(8,128)(2,1)S(1)}, bf16[1,56,384]{2,1,0:T(8,128)(2,1)S(1)}, u32[]{:S(2)}, u32[]{:S(2)}) collective-permute-start(bf16[1,56,384]{2,1,0:T(8,128)(2,1)S(1)} %add_convert_fusion.7), channel_id=1, source_target_pairs={{0,6},{1,7},{2,4},{3,5},{4,2},{5,3},{6,0},{7,1},{8,14},{9,15},{10,... | collective-permute-start | bytes 129032 | tf_op jit(solution)/shard_map/ppermute | solution.py:743
  91.5 1.9 %collective-permute-done.27 = bf16[1,56,384]{2,1,0:T(8,128)(2,1)S(1)} collective-permute-done((bf16[1,56,384]{2,1,0:T(8,128)(2,1)S(1)}, bf16[1,56,384]{2,1,0:T(8,128)(2,1)S(1)}, u32[]{:S(2)}, u32[]{:S(2)}) %collective-permute-start.27) | collective-permute-done | bytes 43040 | tf_op jit(solution)/shard_map/ppermute | solution.py:743
  93.6 4.5 %collective-permute-done.30 = bf16[4,112,384]{2,1,0:T(8,128)(2,1)S(1)} collective-permute-done((bf16[4,112,384]{2,1,0:T(8,128)(2,1)S(1)}, bf16[4,112,384]{2,1,0:T(8,128)(2,1)S(1)}, u32[]{:S(2)}, u32[]{:S(2)}) %collective-permute-start.30) | collective-permute-done | bytes 344096 | tf_op jit(solution)/shard_map/ppermute | solution.py:743
  98.1 4.6 %collective-permute-start.31 = (bf16[16,112,384]{2,1,0:T(8,128)(2,1)S(1)}, bf16[16,112,384]{2,1,0:T(8,128)(2,1)S(1)}, u32[]{:S(2)}, u32[]{:S(2)}) collective-permute-start(bf16[16,112,384]{2,1,0:T(8,128)(2,1)S(1)} %constant_dynamic-update-slice_fusion), channel_id=1, source_target_pairs={{0,8},{1,9},{2,10},{3,11},{4,12},{5,13},{6,14},{7,15},{8,0},{9,1},... | collective-permute-start | bytes 4128776 | tf_op jit(solution)/shard_map/ppermute | solution.py:743
  103.4 1.2 %collective-permute-start.33 = (bf16[4,56,384]{2,1,0:T(8,128)(2,1)S(1)}, bf16[4,56,384]{2,1,0:T(8,128)(2,1)S(1)}, u32[]{:S(2)}, u32[]{:S(2)}) collective-permute-start(bf16[4,56,384]{2,1,0:T(8,128)(2,1)S(1)} %pad_maximum_fusion.1), channel_id=1, source_target_pairs={{0,1},{1,0},{2,3},{3,2},{4,5},{5,4},{6,7},{7,6},{8,9},{9,8},{10,11... | collective-permute-start | bytes 516104 | tf_op jit(solution)/shard_map/ppermute | solution.py:743
  105.5 3.8 %shard_map.343 = (f32[1536,384]{1,0:T(8,128)}, f32[384,1536]{1,0:T(8,128)}, f32[384,384]{1,0:T(8,128)}, f32[384]{0:T(512)}, f32[384]{0:T(512)}, /*index=5*/f32[3...) custom-call(s32[1]{0:T(128)} %bitcast.11.refs_0_.core_ref, s32[1]{0:T(128)} %bitcast.1.refs_2_.refs_1_.place_ref, ...), custom_call_target="tpu_custom_call" | custom-call | flops 4000000000 | bytes 4000000 | tf_op jit(solution)/shard_map/pallas_call | solution.py:705
  109.3 4.0 %collective-permute-done.34 = bf16[4,56,384]{2,1,0:T(8,128)(2,1)S(1)} collective-permute-done((bf16[4,56,384]{2,1,0:T(8,128)(2,1)S(1)}, bf16[4,56,384]{2,1,0:T(8,128)(2,1)S(1)}, u32[]{:S(2)}, u32[]{:S(2)}) %collective-permute-start.34) | collective-permute-done | bytes 172064 | tf_op jit(solution)/shard_map/ppermute | solution.py:743
  116.5 1.2 %shard_map.345 = (f32[384,384]{1,0:T(8,128)}, f32[384]{0:T(512)}, f32[384,384]{1,0:T(8,128)}, f32[384]{0:T(512)}, f32[384,384]{1,0:T(8,128)}, /*index=5*/f32[384]{0:T(512)}, f32[512,384]{1,0:T(8,128)}) custom-call(s32[1]{0:T(128)} %bitcast.11.refs_0_.core_ref, ...), custom_call_target="tpu_custom_call", output_to_operand_aliasing={{0}: (3, {}), {1}: (4, {}), {2}: (5, {}), {3}: (6, {}), {4}... | custom-call | flops 2000000000 | bytes 2000000 | tf_op jit(solution)/shard_map/pallas_call | solution.py:885
  (86 shorter events, 20.9 us)
Async XLA Ops:
  0.7 11.0 %collective-permute-start = (bf16[256,384]{1,0:T(8,128)(2,1)}, bf16[256,384]{1,0:T(8,128)(2,1)S(1)}, u32[]{:S(2)}, u32[]{:S(2)}) collective-permute-start(bf16[256,384]{1,0:T(8,128)(2,1)} %bitcast.40), channel_id=1, source_target_pairs={{0,8},{8,0},{16,24},{24,16},{1,9},{9,1},{17,25},{25,17},{2,10},{10... | collective-permute-start | bytes 589832 | tf_op jit(solution)/shard_map/ppermute | solution.py:919
  1.4 10.3 %collective-permute-start.1 = (bf16[256,384]{1,0:T(8,128)(2,1)}, bf16[256,384]{1,0:T(8,128)(2,1)S(1)}, u32[]{:S(2)}, u32[]{:S(2)}) collective-permute-start(bf16[256,384]{1,0:T(8,128)(2,1)} %bitcast.41), channel_id=1, source_target_pairs={{0,16},{8,24},{16,0},{24,8},{1,17},{9,25},{17,1},{25,9},{2,18},{10... | collective-permute-start | bytes 589832 | tf_op jit(solution)/shard_map/ppermute | solution.py:919
  2.7 9.8 %collective-permute-start.2 = (bf16[256,384]{1,0:T(8,128)(2,1)}, bf16[256,384]{1,0:T(8,128)(2,1)S(1)}, u32[]{:S(2)}, u32[]{:S(2)}) collective-permute-start(bf16[256,384]{1,0:T(8,128)(2,1)} %bitcast.42), channel_id=1, source_target_pairs={{0,24},{8,16},{16,8},{24,0},{1,25},{9,17},{17,9},{25,1},{2,26},{10... | collective-permute-start | bytes 589832 | tf_op jit(solution)/shard_map/ppermute | solution.py:919
  29.3 7.9 %collective-permute-start.6 = (bf16[288,384]{1,0:T(8,128)(2,1)S(1)}, bf16[288,384]{1,0:T(8,128)(2,1)S(1)}, u32[]{:S(2)}, u32[]{:S(2)}) collective-permute-start(bf16[288,384]{1,0:T(8,128)(2,1)S(1)} %get-tuple-element.113.refs_3_.refs_8_), channel_id=1, source_target_pairs={{0,16},{8,24},{16,0},{24,8},{1,17},{9,25},{17,1},{25,9},{2,18},{10... | collective-permute-start | bytes 663560 | tf_op jit(solution)/shard_map/ppermute | solution.py:919
  30.7 10.5 %collective-permute-start.5 = (bf16[288,384]{1,0:T(8,128)(2,1)S(1)}, bf16[288,384]{1,0:T(8,128)(2,1)S(1)}, u32[]{:S(2)}, u32[]{:S(2)}) collective-permute-start(bf16[288,384]{1,0:T(8,128)(2,1)S(1)} %get-tuple-element.113.refs_3_.refs_8_), channel_id=1, source_target_pairs={{0,8},{8,0},{16,24},{24,16},{1,9},{9,1},{17,25},{25,17},{2,10},{10... | collective-permute-start | bytes 663560 | tf_op jit(solution)/shard_map/ppermute | solution.py:919
  31.2 9.6 %collective-permute-start.3 = (bf16[8,112,384]{2,1,0:T(8,128)(2,1)}, bf16[8,112,384]{2,1,0:T(8,128)(2,1)S(1)}, u32[]{:S(2)}, u32[]{:S(2)}) collective-permute-start(bf16[8,112,384]{2,1,0:T(8,128)(2,1)} %bitcast.36), channel_id=1, source_target_pairs={{0,8},{1,9},{2,10},{3,11},{4,12},{5,13},{6,14},{7,15},{8,0},{9,1},... | collective-permute-start | bytes 2064392 | tf_op jit(solution)/shard_map/ppermute | solution.py:743
  38.4 20.1 %collective-permute-start.10 = (bf16[4,112,384]{2,1,0:T(8,128)(2,1)}, bf16[4,112,384]{2,1,0:T(8,128)(2,1)}, u32[]{:S(2)}, u32[]{:S(2)}) collective-permute-start(bf16[4,112,384]{2,1,0:T(8,128)(2,1)} %get-tuple-element.190), channel_id=1, source_target_pairs={{0,17},{1,16},{2,19},{3,18},{4,21},{5,20},{6,23},{7,22},{8,25},{9,... | collective-permute-start | bytes 1032200 | tf_op jit(solution)/shard_map/ppermute | solution.py:743
  40.5 18.0 %collective-permute-start.9 = (bf16[4,112,384]{2,1,0:T(8,128)(2,1)}, bf16[4,112,384]{2,1,0:T(8,128)(2,1)}, u32[]{:S(2)}, u32[]{:S(2)}) collective-permute-start(bf16[4,112,384]{2,1,0:T(8,128)(2,1)} %get-tuple-element.191), channel_id=1, source_target_pairs={{0,1},{1,0},{2,3},{3,2},{4,5},{5,4},{6,7},{7,6},{8,9},{9,8},{10,11... | collective-permute-start | bytes 1032200 | tf_op jit(solution)/shard_map/ppermute | solution.py:743
  40.8 17.7 %collective-permute-start.8 = (bf16[4,112,384]{2,1,0:T(8,128)(2,1)S(1)}, bf16[4,112,384]{2,1,0:T(8,128)(2,1)}, u32[]{:S(2)}, u32[]{:S(2)}) collective-permute-start(bf16[4,112,384]{2,1,0:T(8,128)(2,1)S(1)} %fusion.2), channel_id=1, source_target_pairs={{0,16},{1,17},{2,18},{3,19},{4,20},{5,21},{6,22},{7,23},{8,24},{9,... | collective-permute-start | bytes 1032200 | tf_op jit(solution)/shard_map/ppermute | solution.py:743
  60.2 6.4 %collective-permute-start.18 = (bf16[1,112,384]{2,1,0:T(8,128)(2,1)S(1)}, bf16[1,112,384]{2,1,0:T(8,128)(2,1)S(1)}, u32[]{:S(2)}, u32[]{:S(2)}) collective-permute-start(bf16[1,112,384]{2,1,0:T(8,128)(2,1)S(1)} %get-tuple-element.180), channel_id=1, source_target_pairs={{0,4},{1,5},{2,6},{3,7},{4,0},{5,1},{6,2},{7,3},{8,12},{9,13},{10,... | collective-permute-start | bytes 258056 | tf_op jit(solution)/shard_map/ppermute | solution.py:743
  62.5 8.0 %collective-permute-start.19 = (bf16[1,112,384]{2,1,0:T(8,128)(2,1)S(1)}, bf16[1,112,384]{2,1,0:T(8,128)(2,1)S(1)}, u32[]{:S(2)}, u32[]{:S(2)}) collective-permute-start(bf16[1,112,384]{2,1,0:T(8,128)(2,1)S(1)} %get-tuple-element.179), channel_id=1, source_target_pairs={{0,6},{1,7},{2,4},{3,5},{4,2},{5,3},{6,0},{7,1},{8,14},{9,15},{10,... | collective-permute-start | bytes 258056 | tf_op jit(solution)/shard_map/ppermute | solution.py:743
  62.8 11.1 %collective-permute-start.12 = (bf16[4,56,384]{2,1,0:T(8,128)(2,1)S(1)}, bf16[4,56,384]{2,1,0:T(8,128)(2,1)S(1)}, u32[]{:S(2)}, u32[]{:S(2)}) collective-permute-start(bf16[4,56,384]{2,1,0:T(8,128)(2,1)S(1)} %add_convert_fusion.2), channel_id=1, source_target_pairs={{0,16},{1,17},{2,18},{3,19},{4,20},{5,21},{6,22},{7,23},{8,24},{9,... | collective-permute-start | bytes 516104 | tf_op jit(solution)/shard_map/ppermute | solution.py:743
  63.6 10.8 %collective-permute-start.14 = (bf16[4,56,384]{2,1,0:T(8,128)(2,1)S(1)}, bf16[4,56,384]{2,1,0:T(8,128)(2,1)S(1)}, u32[]{:S(2)}, u32[]{:S(2)}) collective-permute-start(bf16[4,56,384]{2,1,0:T(8,128)(2,1)S(1)} %get-tuple-element.188), channel_id=1, source_target_pairs={{0,1},{1,0},{2,3},{3,2},{4,5},{5,4},{6,7},{7,6},{8,9},{9,8},{10,11... | collective-permute-start | bytes 516104 | tf_op jit(solution)/shard_map/ppermute | solution.py:743
  64.8 9.5 %collective-permute-start.15 = (bf16[4,56,384]{2,1,0:T(8,128)(2,1)S(1)}, bf16[4,56,384]{2,1,0:T(8,128)(2,1)S(1)}, u32[]{:S(2)}, u32[]{:S(2)}) collective-permute-start(bf16[4,56,384]{2,1,0:T(8,128)(2,1)S(1)} %get-tuple-element.189), channel_id=1, source_target_pairs={{0,17},{1,16},{2,19},{3,18},{4,21},{5,20},{6,23},{7,22},{8,25},{9,... | collective-permute-start | bytes 516104 | tf_op jit(solution)/shard_map/ppermute | solution.py:743
  73.8 9.3 %collective-permute-start.22 = (bf16[1,112,384]{2,1,0:T(8,128)(2,1)S(1)}, bf16[1,112,384]{2,1,0:T(8,128)(2,1)S(1)}, u32[]{:S(2)}, u32[]{:S(2)}) collective-permute-start(bf16[1,112,384]{2,1,0:T(8,128)(2,1)S(1)} %add_convert_fusion.3), channel_id=1, source_target_pairs={{0,6},{1,7},{2,4},{3,5},{4,2},{5,3},{6,0},{7,1},{8,14},{9,15},{10,... | collective-permute-start | bytes 258056 | tf_op jit(solution)/shard_map/ppermute | solution.py:743
  74.5 8.6 %collective-permute-start.16 = (bf16[1,56,384]{2,1,0:T(8,128)(2,1)S(1)}, bf16[1,56,384]{2,1,0:T(8,128)(2,1)S(1)}, u32[]{:S(2)}, u32[]{:S(2)}) collective-permute-start(bf16[1,56,384]{2,1,0:T(8,128)(2,1)S(1)} %get-tuple-element.184), channel_id=1, source_target_pairs={{0,2},{1,3},{2,0},{3,1},{4,6},{5,7},{6,4},{7,5},{8,10},{9,11},{10,... | collective-permute-start | bytes 129032 | tf_op jit(solution)/shard_map/ppermute | solution.py:743
  75.6 10.6 %collective-permute-start.23 = (bf16[1,56,384]{2,1,0:T(8,128)(2,1)S(1)}, bf16[1,56,384]{2,1,0:T(8,128)(2,1)S(1)}, u32[]{:S(2)}, u32[]{:S(2)}) collective-permute-start(bf16[1,56,384]{2,1,0:T(8,128)(2,1)S(1)} %get-tuple-element.182), channel_id=1, source_target_pairs={{0,4},{1,5},{2,6},{3,7},{4,0},{5,1},{6,2},{7,3},{8,12},{9,13},{10,... | collective-permute-start | bytes 129032 | tf_op jit(solution)/shard_map/ppermute | solution.py:743
  76.7 9.5 %collective-permute-start.24 = (bf16[1,56,384]{2,1,0:T(8,128)(2,1)S(1)}, bf16[1,56,384]{2,1,0:T(8,128)(2,1)S(1)}, u32[]{:S(2)}, u32[]{:S(2)}) collective-permute-start(bf16[1,56,384]{2,1,0:T(8,128)(2,1)S(1)} %get-tuple-element.183), channel_id=1, source_target_pairs={{0,6},{1,7},{2,4},{3,5},{4,2},{5,3},{6,0},{7,1},{8,14},{9,15},{10,... | collective-permute-start | bytes 129032 | tf_op jit(solution)/shard_map/ppermute | solution.py:743
  83.5 10.0 %collective-permute-start.28 = (bf16[4,112,384]{2,1,0:T(8,128)(2,1)S(1)}, bf16[4,112,384]{2,1,0:T(8,128)(2,1)S(1)}, u32[]{:S(2)}, u32[]{:S(2)}) collective-permute-start(bf16[4,112,384]{2,1,0:T(8,128)(2,1)S(1)} %pad_maximum_fusion), channel_id=1, source_target_pairs={{0,16},{1,17},{2,18},{3,19},{4,20},{5,21},{6,22},{7,23},{8,24},{9,... | collective-permute-start | bytes 1032200 | tf_op jit(solution)/shard_map/ppermute | solution.py:743
  84.1 9.4 %collective-permute-start.29 = (bf16[4,112,384]{2,1,0:T(8,128)(2,1)S(1)}, bf16[4,112,384]{2,1,0:T(8,128)(2,1)S(1)}, u32[]{:S(2)}, u32[]{:S(2)}) collective-permute-start(bf16[4,112,384]{2,1,0:T(8,128)(2,1)S(1)} %pad_maximum_fusion), channel_id=1, source_target_pairs={{0,1},{1,0},{2,3},{3,2},{4,5},{5,4},{6,7},{7,6},{8,9},{9,8},{10,11... | collective-permute-start | bytes 1032200 | tf_op jit(solution)/shard_map/ppermute | solution.py:743
  85.4 12.7 %collective-permute-start.30 = (bf16[4,112,384]{2,1,0:T(8,128)(2,1)S(1)}, bf16[4,112,384]{2,1,0:T(8,128)(2,1)S(1)}, u32[]{:S(2)}, u32[]{:S(2)}) collective-permute-start(bf16[4,112,384]{2,1,0:T(8,128)(2,1)S(1)} %pad_maximum_fusion), channel_id=1, source_target_pairs={{0,17},{1,16},{2,19},{3,18},{4,21},{5,20},{6,23},{7,22},{8,25},{9,... | collective-permute-start | bytes 1032200 | tf_op jit(solution)/shard_map/ppermute | solution.py:743
  98.1 7.4 %collective-permute-start.31 = (bf16[16,112,384]{2,1,0:T(8,128)(2,1)S(1)}, bf16[16,112,384]{2,1,0:T(8,128)(2,1)S(1)}, u32[]{:S(2)}, u32[]{:S(2)}) collective-permute-start(bf16[16,112,384]{2,1,0:T(8,128)(2,1)S(1)} %constant_dynamic-update-slice_fusion), channel_id=1, source_target_pairs={{0,8},{1,9},{2,10},{3,11},{4,12},{5,13},{6,14},{7,15},{8,0},{9,1},... | collective-permute-start | bytes 4128776 | tf_op jit(solution)/shard_map/ppermute | solution.py:743
  102.8 6.6 %collective-permute-start.32 = (bf16[4,56,384]{2,1,0:T(8,128)(2,1)S(1)}, bf16[4,56,384]{2,1,0:T(8,128)(2,1)S(1)}, u32[]{:S(2)}, u32[]{:S(2)}) collective-permute-start(bf16[4,56,384]{2,1,0:T(8,128)(2,1)S(1)} %pad_maximum_fusion.1), channel_id=1, source_target_pairs={{0,16},{1,17},{2,18},{3,19},{4,20},{5,21},{6,22},{7,23},{8,24},{9,... | collective-permute-start | bytes 516104 | tf_op jit(solution)/shard_map/ppermute | solution.py:743
  104.7 8.7 %collective-permute-start.34 = (bf16[4,56,384]{2,1,0:T(8,128)(2,1)S(1)}, bf16[4,56,384]{2,1,0:T(8,128)(2,1)S(1)}, u32[]{:S(2)}, u32[]{:S(2)}) collective-permute-start(bf16[4,56,384]{2,1,0:T(8,128)(2,1)S(1)} %pad_maximum_fusion.1), channel_id=1, source_target_pairs={{0,17},{1,16},{2,19},{3,18},{4,21},{5,20},{6,23},{7,22},{8,25},{9,... | collective-permute-start | bytes 516104 | tf_op jit(solution)/shard_map/ppermute | solution.py:743
  (16 other events, 87.9 us)

commit v2 on v1

--- a/solution.py
+++ b/solution.py
@@ -14,6 +14,7 @@
 LOG2E = math.log2(math.e)
 EPS = 1e-07
 MIB = 1024 * 1024
+QUERY_SPLIT = 1
 EARLY_ROWS = 3584
 LATE_ROWS = 1792
 
@@ -91,7 +92,7 @@
     for side in range(2):
         rows = slice(side * size, (side + 1) * size)
         s_ref[rows, : 3 * size] = pltpu.roll(source[rows], shift, 1, stride=1, stride_axis=0)[:, : 3 * size]
-    s_ref[:, 3 * size :] = wide(jnp.where(block < 2, last, first), size)
+    s_ref[:, 3 * size :] = wide(jnp.where(block < 2, last, first), s_ref.shape[1] - 3 * size)
 
 
 def other_terms(block, s_ref, others, tables, shift, slots):
@@ -256,6 +257,11 @@
     chances_out, sent_out = chances_store.ref, sent_store.ref
     for pair in range(HEADS // 2):
         slab_copy(terms, terms_ref, sems, pair).start()
+    for load in (
+        output_weight, output_bias, first_gain, first_bias, inner_weight, inner_bias, outer_weight, outer_bias,
+        second_gain, second_bias, cotangent,
+    ):
+        load.begin()
     own, core, far, diagonal, rel_query_out = ready(own, core, far, diagonal, rel_query)
     query_weight, key_weight, query_bias, key_bias = ready(query_weight, key_weight, query_bias, key_bias)
     value_weight, value_bias = ready(value_weight, value_bias)
@@ -274,7 +280,8 @@
         columns = pair_columns(pair)
         query_own = stacked(query_out[size : 2 * size, columns])
         slab_copy(terms, terms_ref, sems, pair).wait()
-        s_ref[...] = terms_ref[pair]
+        s_ref[:, : 3 * size] = terms_ref[pair, :, : 3 * size]
+        s_ref[:, 3 * size :] = wide(terms_ref[pair, :, 3 * size : 3 * size + 1], size)
         other_terms(
             block,
             s_ref,
@@ -409,12 +416,12 @@
 
 
 def query_kernel(
-    block_ref, rel_key, query_all, sent, stats, value_all, key_all, chances_load,
+    first, last, block_ref, rel_key, query_all, sent, stats, value_all, key_all, chances_load,
     query_store, rel_key_grad_store,
-    ext_ref, wall_ref, back_ref, rows_ref,
+    ext_ref, wall_ref, back_ref,
 ):
     block = block_ref[0]
-    size, model_width = query_store.shape
+    size, model_width = query_store.shape[0], query_all.shape[1]
     scale = 1.0 / math.sqrt(3.0 * (model_width // HEADS))
     flip = reversal(size)
     chances = chances_load.buffer
@@ -437,19 +444,19 @@
         row_grad, table = position_backward(
             block, grad_scores, flip, key_all[:, columns], ext_ref[:, columns], back_ref[:, columns], wall_ref, 3 * size
         )
-        rows_ref[:, columns] = (row_grad * scale).astype(BF)
-        rel_key_grad_store.ref[columns, :] = table_grad(table, scale)
+        there = pair_columns(pair - first)
+        query_store.ref[:, there] = nn(flip, (row_grad * scale).astype(BF)).astype(BF)
+        rel_key_grad_store.ref[there, :] = table_grad(table, scale)
         return carry
 
-    lax.fori_loop(0, HEADS // 2, pair_step, 0)
-    query_store.ref[...] = nn(flip, rows_ref[...]).astype(BF)
+    lax.fori_loop(first, last, pair_step, 0)
 
 
 def key_kernel(
     block_ref, length_ref, place_ref, rel_query, key_all, rel_key, query_all, value_all,
     sent_own, sent_core, sent_far, sent_diagonal,
-    own, relative, grad_query, grad_rel_key, query_weight, key_weight, value_weight, grad_first,
-    tokens_store, late_send_low, late_send_high, late_keep,
+    own, relative, grad_query_low, grad_rel_key_low, grad_query_high, grad_rel_key_high, query_weight, key_weight,
+    value_weight, grad_first, tokens_store, late_send_low, late_send_high, late_keep,
     grads_out, key_rows_ref, value_rows_ref, rel_grad_ref,
     sent_ref, s_ref, grad_ref, ext_ref, wall_ref, back_ref, stat_ref,
 ):
@@ -503,17 +510,21 @@
         return carry
 
     lax.fori_loop(0, HEADS // 2, pair_step, 0)
-    own, relative, grad_query, grad_rel_key = ready(own, relative, grad_query, grad_rel_key)
+    own, relative, *grads = ready(
+        own, relative, grad_query_low, grad_rel_key_low, grad_query_high, grad_rel_key_high
+    )
+    grad_query = jnp.concatenate([grads[0][...], grads[2][...]], axis=1)
+    grad_rel_key = jnp.concatenate([grads[1][...], grads[3][...]], axis=0)
     rel = relative.shape[0]
     grad_key = nn(flip, key_rows_ref[...]).astype(BF)
     grad_value = value_rows_ref[...]
     rel_query_grad = rel_grad_ref[...]
-    rel_key_grad = grad_rel_key[...]
+    rel_key_grad = grad_rel_key
     query_low = rel_query_grad.astype(BF)
     key_low = nn(rel_key_grad.astype(BF), reversal(rel)).astype(BF)
     tokens = own[...]
     table = relative[...]
-    grads_out[0:model_width, :] = (tn(tokens, grad_query[...]) + tt(table, query_low)).astype(BF)
+    grads_out[0:model_width, :] = (tn(tokens, grad_query) + tt(table, query_low)).astype(BF)
     grads_out[model_width : 2 * model_width, :] = (tn(tokens, grad_key) + tt(table, key_low)).astype(BF)
     grads_out[2 * model_width : 3 * model_width, :] = tn(tokens, grad_value).astype(BF)
     late_sends = (late_send_low, late_send_high)
@@ -533,7 +544,7 @@
         return (nt(ones, high) + nt(ones, low))[0:1, :]
 
     small = [
-        column_sum(grad_query[...]) + lane_sums(rel_query_grad),
+        column_sum(grad_query) + lane_sums(rel_query_grad),
         column_sum(grad_key) + lane_sums(rel_key_grad),
         column_sum(grad_value),
         jnp.zeros((13, model_width), F32),
@@ -541,7 +552,7 @@
     grads_out[small_at : small_at + 16, :] = jnp.concatenate(small, axis=0).astype(BF)
     push_half(1, block % 2, place_ref[0], grads_out, late_sends, late_keep)
     tokens_store.ref[...] = (
-        nt(grad_query[...], query_weight[...])
+        nt(grad_query, query_weight[...])
         + nt(grad_key, key_weight[...])
         + nt(grad_value, value_weight[...])
         + grad_first[...]
@@ -551,6 +562,8 @@
 class Load:
     def __init__(self, source, buffer, sem):
         self.copy, self.buffer, self.waiting = pltpu.make_async_copy(source, buffer, sem), buffer, True
+
+    def begin(self):
         self.copy.start()
 
     def ready(self):
@@ -646,7 +659,7 @@
         self.what = what
 
 
-def call(kernel, outs, scratch, *operands, scalars, micros, vmem):
+def call(kernel, outs, scratch, *operands, scalars, micros, vmem, later=False):
     fetched = [k for k, operand in enumerate(operands) if isinstance(operand, Fetch)]
     bare_in = [k for k, operand in enumerate(operands) if isinstance(operand, Bare)]
     operands = [
@@ -683,6 +696,8 @@
                 ins[k] = Here(ins[k])
         for place, k in enumerate(loads):
             ins[k] = Load(ins[k], targets[k], in_sems.at[place])
+            if not later:
+                ins[k].begin()
         buffers = buffers[len(own_loads) :]
         for k in range(len(results)):
             if kept_out[k]:
@@ -937,12 +952,13 @@
     far = along(own, 2)
     diagonal = along(own, 3)
     full = blk_count * size
+    slabs = (HEADS // 2, 2 * size, 3 * size + 128)
     (
         rel_query, rel_key, terms, relative_kept, query_weight, key_weight, query_bias, key_bias, own, value_weight, value_bias,
     ) = call(
         first_kernel,
-        [Kept((rel, width), BF), Kept((rel, width), BF), Bare((HEADS // 2, 2 * size, full), F32)],
-        [((size, width), BF), ((size, width), BF), ((HEADS // 2, 2 * size, full), F32), ((HEADS // 2,), None)],
+        [Kept((rel, width), BF), Kept((rel, width), BF), Bare(slabs, F32)],
+        [((size, width), BF), ((size, width), BF), (slabs, F32), ((HEADS // 2,), None)],
         block,
         *map(Fetch, (relative_table, query_weight, key_weight, query_bias, key_bias, own, value_weight, value_bias)),
         scalars=1, micros=9, vmem=14,
@@ -973,7 +989,7 @@
             ((size, inner_width), BF),
             ((size, inner_width), F32),
             ((EARLY_ROWS, width), BF),
-            ((HEADS // 2, 2 * size, full), F32),
+            (slabs, F32),
             ((size, width), F32),
             ((16, width), F32),
             ((1, inner_width), F32),
@@ -985,33 +1001,40 @@
         *map(Kept, (query_weight, key_weight, query_bias, key_bias, value_weight, value_bias)),
         output_weight, output_bias, first_gain, first_bias, inner_weight, inner_bias, outer_weight, outer_bias,
         second_gain, second_bias, cotangent[0],
-        scalars=3, micros=20, vmem=26,
+        scalars=3, micros=20, vmem=26, later=True,
     )
     early_parts = first_terms(early_keep, early_send_low, early_send_high)
     sent_far = along(sent, 2)
     sent_core = along(sent, 1)
     position_scratch = [((2 * rel, width), BF), ((2 * size, 2 * rel), BF), ((size, width), BF)]
-    grad_query, grad_rel_key = call(
-        query_kernel,
-        [Kept((size, width), BF), Kept((width, rel), F32)],
-        position_scratch + [((size, width), BF)],
-        block, *map(Kept, (rel_key, query_all, sent, stats, value_all, key_all, chances)),
-        scalars=1, micros=8, vmem=10,
-    )
-    sent_diagonal = along(in_order(grad_query, sent_far), 1)
+    query_arrays = tuple(map(Kept, (rel_key, query_all, sent, stats, value_all, key_all, chances)))
+
+    def query_call(first, last, block_then):
+        columns = (last - first) * 128
+        return call(
+            functools.partial(query_kernel, first, last),
+            [Kept((size, columns), BF), Kept((columns, rel), F32)],
+            position_scratch,
+            block_then, *query_arrays,
+            scalars=1, micros=2 * (last - first) + 1, vmem=10,
+        )
+
+    query_grads = query_call(0, QUERY_SPLIT, block)
+    sending, early_terms = first_scatter([terms_after(query_grads[0], terms) for terms in early_parts])
+    query_grads += query_call(QUERY_SPLIT, HEADS // 2, in_order(sending, block))
+    sent_diagonal = along(in_order(query_grads[2], sent_far), 1)
     key_scratch = (
         [((full, width), BF), ((2 * size, full), F32), ((2 * size, full), BF)] + position_scratch + [((16, full), F32)]
     )
     key_arrays = tuple(
         map(Kept, (rel_query, key_all, rel_key, query_all, value_all, sent, sent_core, sent_far, sent_diagonal))
     )
-    sending, early_terms = first_scatter(early_parts)
     grad_tokens, late_send_low, late_send_high, late_keep = call(
         key_kernel,
         [((size, width), F32)] + [((LATE_ROWS // 4, width), BF, "raw")] * 2 + [((LATE_ROWS // 2, width), BF, "raw")],
         [((LATE_ROWS, width), BF), ((size, width), BF), ((size, width), BF), ((width, rel), F32)] + key_scratch,
-        in_order(sending, block), lengths, place, *key_arrays,
-        *map(Kept, (own, relative_kept, grad_query, grad_rel_key, query_weight, key_weight, value_weight, grad_first)),
+        block, lengths, place, *key_arrays,
+        *map(Kept, (own, relative_kept, *query_grads, query_weight, key_weight, value_weight, grad_first)),
         scalars=3, micros=17, vmem=18,
     )
     late_parts = first_terms(late_keep, late_send_low, late_send_high)

time: 118 us -> 118 us (level)
    pallas_call x5 -> x6, Pallas kernels: 49.8 us -> 49.4 us  [call(): pl.pallas_call(body, out_shape=[pltpu.VMEM(out[0], out[1]) if kept else p...]
where the time goes in v2:
time: 118 us; the launch traced here: 117 us
  Pallas kernels  51.7 us (44%)
  starting transfers between devices  34.9 us (30%)
  waiting for transfers between devices  23.4 us (20%)
  other arithmetic  5.17 us (4%)
  between operations  1.77 us (2%)
    pallas_call x6, Pallas kernels, call(): pl.pallas_call(body, out_shape=[pltpu.VMEM(out[0], out[1]) if kept else p...  49.4 us
    ppermute x30, starting transfers between devices, send(): return lax.ppermute(values, ('blk', 'dp'), self.pairs(mask))  30.6 us
    ppermute x30, waiting for transfers between devices, send(): return lax.ppermute(values, ('blk', 'dp'), self.pairs(mask))  22.5 us
    convert_element_type x8, other arithmetic, total(): return sum((span.astype(F32) for span in spans)).astype(BF)  4.8 us
    ppermute x6, starting transfers between devices, along(): return lax.ppermute(values, 'blk', [(i, i ^ bit) for i in range(blk_count)])  4.29 us
    pallas_call x2, Pallas kernels, late_call(): pl.pallas_call(functools.partial(late_kernel, mine, shapes), out_shape=[p...  2.38 us
  transfers between devices with their start and end apart: 36, of which 9 were waited for; matrix products, arithmetic and copies ran while one was open for 5% of the time, Pallas kernels for 29%

profile of v2, /device:TPU:9, one launch (start us, length us, event | category | flops | bytes accessed | tf_op | source)
XLA Modules:
  0.0 117.3 jit_solution(6503777938447827363)
XLA Ops:
  1.4 1.3 %collective-permute-start.1 = (bf16[256,384]{1,0:T(8,128)(2,1)}, bf16[256,384]{1,0:T(8,128)(2,1)S(1)}, u32[]{:S(2)}, u32[]{:S(2)}) collective-permute-start(bf16[256,384]{1,0:T(8,128)(2,1)} %bitcast.34), channel_id=1, source_target_pairs={{0,16},{8,24},{16,0},{24,8},{1,17},{9,25},{17,1},{25,9},{2,18},{10... | collective-permute-start | bytes 589832 | tf_op jit(solution)/shard_map/ppermute | solution.py:934
  3.1 7.8 %shard_map.339 = (bf16[512,384]{1,0:T(8,128)(2,1)S(1)}, bf16[512,384]{1,0:T(8,128)(2,1)S(1)}, f32[3,512,896]{2,1,0:T(8,128)}, bf16[512,384]{1,0:T(8,128)(2,1)S(1...) custom-call(s32[1]{0:T(128)} %bitcast.refs_0_, ...), custom_call_target="tpu_custom_call" | custom-call | flops 8999999488 | bytes 9000000 | tf_op jit(solution)/shard_map/pallas_call | solution.py:720
  12.5 16.6 %shard_map.340 = (f32[256,384]{1,0:T(8,128)}, f32[256,384]{1,0:T(8,128)S(1)}, bf16[3,512,1024]{2,1,0:T(8,128)(2,1)S(1)}, bf16[288,384]{1,0:T(8,128)(2,1)S(1)}, f...) custom-call(s32[1]{0:T(128)} %bitcast.refs_0_, ...), custom_call_target="tpu_custom_call" | custom-call | flops 20000000000 | bytes 20000000 | tf_op jit(solution)/shard_map/pallas_call | solution.py:720
  29.7 1.2 %collective-permute-start.4 = (bf16[288,384]{1,0:T(8,128)(2,1)S(1)}, bf16[288,384]{1,0:T(8,128)(2,1)S(1)}, u32[]{:S(2)}, u32[]{:S(2)}) collective-permute-start(bf16[288,384]{1,0:T(8,128)(2,1)S(1)} %get-tuple-element.115.refs_3_.refs_8_), channel_id=1, source_target_pairs={{0,16},{8,24},{16,0},{24,8},{1,17},{9,25},{17,1},{25,9},{2,18},{10... | collective-permute-start | bytes 663560 | tf_op jit(solution)/shard_map/ppermute | solution.py:934
  31.4 1.7 %shard_map.341 = (bf16[256,128]{1,0:T(8,128)(2,1)S(1)}, f32[128,512]{1,0:T(8,128)S(1)}) custom-call(s32[1]{0:T(128)} %bitcast.refs_0_, bf16[512,384]{1,0:T(8,128)(2,1)S(1)} %get-tuple-element.103.refs_8_.refs_1_.refs_5_, bf16[1024,384]{1,0:T(8,128)(2,1)S(1)} %get-tuple-element.113.refs_2_.refs_6_, bf16[288,384]{1,0:T(8,128)(2,1)S(1)} %get-tuple-element.115.refs_3_.refs_8_, ...), custom_call_target="tpu_custom_call" | custom-call | flops 3000000000 | bytes 3000000 | tf_op jit(solution)/shard_map/pallas_call | solution.py:720
  34.3 3.7 %shard_map.342 = (bf16[256,256]{1,0:T(8,128)(2,1)S(1)}, f32[256,512]{1,0:T(8,128)S(1)}) custom-call(s32[1]{0:T(128)} %bitcast.refs_0_, bf16[512,384]{1,0:T(8,128)(2,1)S(1)} %get-tuple-element.103.refs_8_.refs_1_.refs_5_, bf16[1024,384]{1,0:T(8,128)(2,1)S(1)} %get-tuple-element.113.refs_2_.refs_6_, bf16[288,384]{1,0:T(8,128)(2,1)S(1)} %get-tuple-element.115.refs_3_.refs_8_, ...), custom_call_target="tpu_custom_call" | custom-call | flops 5000000000 | bytes 5000000 | tf_op jit(solution)/shard_map/pallas_call | solution.py:720
  38.1 1.9 %collective-permute-start.10 = (bf16[4,112,384]{2,1,0:T(8,128)(2,1)}, bf16[4,112,384]{2,1,0:T(8,128)(2,1)}, u32[]{:S(2)}, u32[]{:S(2)}) collective-permute-start(bf16[4,112,384]{2,1,0:T(8,128)(2,1)} %get-tuple-element.194), channel_id=1, source_target_pairs={{0,17},{1,16},{2,19},{3,18},{4,21},{5,20},{6,23},{7,22},{8,25},{9,... | collective-permute-start | bytes 1032200 | tf_op jit(solution)/shard_map/ppermute | solution.py:758
  40.8 15.7 %shard_map.343 = (f32[256,384]{1,0:T(8,128)}, bf16[448,384]{1,0:T(8,128)(2,1)}, bf16[448,384]{1,0:T(8,128)(2,1)}, bf16[896,384]{1,0:T(8,128)(2,1)}) custom-call(s32[1]{0:T(128)} %bitcast.refs_0_, s32[1]{0:T(128)S(6)} %copy.62.refs_1_, s32[1]{0:T(128)} %bitcast.1.refs_2_.refs_1_.place_ref, bf16[512,384]{1,0:T(8,128)(2,1)S(1)} %get-tuple-element.102.refs_7_.refs_3_, ...), custom_call_target="tpu_custom_call" | custom-call | flops 16999999488 | bytes 17000000 | tf_op jit(solution)/shard_map/pallas_call | solution.py:720
  56.5 1.3 %collective-permute-start.11 = (bf16[8,56,384]{2,1,0:T(8,128)(2,1)}, bf16[8,56,384]{2,1,0:T(8,128)(2,1)S(1)}, u32[]{:S(2)}, u32[]{:S(2)}) collective-permute-start(bf16[8,56,384]{2,1,0:T(8,128)(2,1)} %bitcast.32), channel_id=1, source_target_pairs={{0,8},{1,9},{2,10},{3,11},{4,12},{5,13},{6,14},{7,15},{8,0},{9,1},... | collective-permute-start | bytes 1032200 | tf_op jit(solution)/shard_map/ppermute | solution.py:758
  58.0 1.5 %add_convert_fusion.7 = (bf16[1,112,384]{2,1,0:T(8,128)(2,1)S(1)}, bf16[1,112,384]{2,1,0:T(8,128)(2,1)S(1)}, bf16[1,112,384]{2,1,0:T(8,128)(2,1)S(1)}) fusion(bf16[4,112,384]{2,1,0:T(8,128)(2,1)} %collective-permute-done.10, s32[]{:T(128)S(6)} %select_n.150, bf16[4,112,384]{2,1,0:T(8,128)(2,1)} %collective-permute-done.9, ...), kind=kLoop, calls=%fused_computation.9 | loop fusion | flops 1290240 | bytes 1548324 | tf_op jit(solution)/shard_map/convert_element_type | solution.py:803
  59.7 2.3 %collective-permute-start.18 = (bf16[1,112,384]{2,1,0:T(8,128)(2,1)S(1)}, bf16[1,112,384]{2,1,0:T(8,128)(2,1)S(1)}, u32[]{:S(2)}, u32[]{:S(2)}) collective-permute-start(bf16[1,112,384]{2,1,0:T(8,128)(2,1)S(1)} %get-tuple-element.192), channel_id=1, source_target_pairs={{0,4},{1,5},{2,6},{3,7},{4,0},{5,1},{6,2},{7,3},{8,12},{9,13},{10,... | collective-permute-start | bytes 258056 | tf_op jit(solution)/shard_map/ppermute | solution.py:758
  63.3 1.3 %collective-permute-start.14 = (bf16[4,56,384]{2,1,0:T(8,128)(2,1)S(1)}, bf16[4,56,384]{2,1,0:T(8,128)(2,1)S(1)}, u32[]{:S(2)}, u32[]{:S(2)}) collective-permute-start(bf16[4,56,384]{2,1,0:T(8,128)(2,1)S(1)} %get-tuple-element.199), channel_id=1, source_target_pairs={{0,1},{1,0},{2,3},{3,2},{4,5},{5,4},{6,7},{7,6},{8,9},{9,8},{10,11... | collective-permute-start | bytes 516104 | tf_op jit(solution)/shard_map/ppermute | solution.py:758
  66.2 3.9 %collective-permute-done.19 = bf16[1,112,384]{2,1,0:T(8,128)(2,1)S(1)} collective-permute-done((bf16[1,112,384]{2,1,0:T(8,128)(2,1)S(1)}, bf16[1,112,384]{2,1,0:T(8,128)(2,1)S(1)}, u32[]{:S(2)}, u32[]{:S(2)}) %collective-permute-start.19) | collective-permute-done | bytes 86048 | tf_op jit(solution)/shard_map/ppermute | solution.py:758
  71.3 2.1 %collective-permute-start.21 = (bf16[1,112,384]{2,1,0:T(8,128)(2,1)S(1)}, bf16[1,112,384]{2,1,0:T(8,128)(2,1)S(1)}, u32[]{:S(2)}, u32[]{:S(2)}) collective-permute-start(bf16[1,112,384]{2,1,0:T(8,128)(2,1)S(1)} %add_convert_fusion.6), channel_id=1, source_target_pairs={{0,4},{1,5},{2,6},{3,7},{4,0},{5,1},{6,2},{7,3},{8,12},{9,13},{10,... | collective-permute-start | bytes 258056 | tf_op jit(solution)/shard_map/ppermute | solution.py:758
  76.8 5.9 %collective-permute-done.22 = bf16[1,112,384]{2,1,0:T(8,128)(2,1)S(1)} collective-permute-done((bf16[1,112,384]{2,1,0:T(8,128)(2,1)S(1)}, bf16[1,112,384]{2,1,0:T(8,128)(2,1)S(1)}, u32[]{:S(2)}, u32[]{:S(2)}) %collective-permute-start.22) | collective-permute-done | bytes 86048 | tf_op jit(solution)/shard_map/ppermute | solution.py:758
  86.6 2.4 %collective-permute-start.26 = (bf16[1,56,384]{2,1,0:T(8,128)(2,1)S(1)}, bf16[1,56,384]{2,1,0:T(8,128)(2,1)S(1)}, u32[]{:S(2)}, u32[]{:S(2)}) collective-permute-start(bf16[1,56,384]{2,1,0:T(8,128)(2,1)S(1)} %add_convert_fusion.10), channel_id=1, source_target_pairs={{0,4},{1,5},{2,6},{3,7},{4,0},{5,1},{6,2},{7,3},{8,12},{9,13},{10,... | collective-permute-start | bytes 129032 | tf_op jit(solution)/shard_map/ppermute | solution.py:758
  89.8 1.3 %collective-permute-start.27 = (bf16[1,56,384]{2,1,0:T(8,128)(2,1)S(1)}, bf16[1,56,384]{2,1,0:T(8,128)(2,1)S(1)}, u32[]{:S(2)}, u32[]{:S(2)}) collective-permute-start(bf16[1,56,384]{2,1,0:T(8,128)(2,1)S(1)} %add_convert_fusion.10), channel_id=1, source_target_pairs={{0,6},{1,7},{2,4},{3,5},{4,2},{5,3},{6,0},{7,1},{8,14},{9,15},{10,... | collective-permute-start | bytes 129032 | tf_op jit(solution)/shard_map/ppermute | solution.py:758
  91.1 1.9 %collective-permute-done.27 = bf16[1,56,384]{2,1,0:T(8,128)(2,1)S(1)} collective-permute-done((bf16[1,56,384]{2,1,0:T(8,128)(2,1)S(1)}, bf16[1,56,384]{2,1,0:T(8,128)(2,1)S(1)}, u32[]{:S(2)}, u32[]{:S(2)}) %collective-permute-start.27) | collective-permute-done | bytes 43040 | tf_op jit(solution)/shard_map/ppermute | solution.py:758
  93.1 4.4 %collective-permute-done.30 = bf16[4,112,384]{2,1,0:T(8,128)(2,1)S(1)} collective-permute-done((bf16[4,112,384]{2,1,0:T(8,128)(2,1)S(1)}, bf16[4,112,384]{2,1,0:T(8,128)(2,1)S(1)}, u32[]{:S(2)}, u32[]{:S(2)}) %collective-permute-start.30) | collective-permute-done | bytes 344096 | tf_op jit(solution)/shard_map/ppermute | solution.py:758
  97.6 4.6 %collective-permute-start.31 = (bf16[16,112,384]{2,1,0:T(8,128)(2,1)S(1)}, bf16[16,112,384]{2,1,0:T(8,128)(2,1)S(1)}, u32[]{:S(2)}, u32[]{:S(2)}) collective-permute-start(bf16[16,112,384]{2,1,0:T(8,128)(2,1)S(1)} %constant_dynamic-update-slice_fusion), channel_id=1, source_target_pairs={{0,8},{1,9},{2,10},{3,11},{4,12},{5,13},{6,14},{7,15},{8,0},{9,1},... | collective-permute-start | bytes 4128776 | tf_op jit(solution)/shard_map/ppermute | solution.py:758
  103.2 1.2 %collective-permute-start.33 = (bf16[4,56,384]{2,1,0:T(8,128)(2,1)S(1)}, bf16[4,56,384]{2,1,0:T(8,128)(2,1)S(1)}, u32[]{:S(2)}, u32[]{:S(2)}) collective-permute-start(bf16[4,56,384]{2,1,0:T(8,128)(2,1)S(1)} %pad_maximum_fusion.1), channel_id=1, source_target_pairs={{0,1},{1,0},{2,3},{3,2},{4,5},{5,4},{6,7},{7,6},{8,9},{9,8},{10,11... | collective-permute-start | bytes 516104 | tf_op jit(solution)/shard_map/ppermute | solution.py:758
  105.0 3.8 %shard_map.344 = (f32[1536,384]{1,0:T(8,128)}, f32[384,1536]{1,0:T(8,128)}, f32[384,384]{1,0:T(8,128)}, f32[384]{0:T(512)}, f32[384]{0:T(512)}, /*index=5*/f32[3...) custom-call(s32[1]{0:T(128)} %bitcast.9.refs_0_.core_ref, s32[1]{0:T(128)} %bitcast.1.refs_2_.refs_1_.place_ref, ...), custom_call_target="tpu_custom_call" | custom-call | flops 4000000000 | bytes 4000000 | tf_op jit(solution)/shard_map/pallas_call | solution.py:720
  108.9 4.0 %collective-permute-done.34 = bf16[4,56,384]{2,1,0:T(8,128)(2,1)S(1)} collective-permute-done((bf16[4,56,384]{2,1,0:T(8,128)(2,1)S(1)}, bf16[4,56,384]{2,1,0:T(8,128)(2,1)S(1)}, u32[]{:S(2)}, u32[]{:S(2)}) %collective-permute-start.34) | collective-permute-done | bytes 172064 | tf_op jit(solution)/shard_map/ppermute | solution.py:758
  116.0 1.2 %shard_map.346 = (f32[384,384]{1,0:T(8,128)}, f32[384]{0:T(512)}, f32[384,384]{1,0:T(8,128)}, f32[384]{0:T(512)}, f32[384,384]{1,0:T(8,128)}, /*index=5*/f32[384]{0:T(512)}, f32[512,384]{1,0:T(8,128)}) custom-call(s32[1]{0:T(128)} %bitcast.9.refs_0_.core_ref, ...), custom_call_target="tpu_custom_call", output_to_operand_aliasing={{0}: (3, {}), {1}: (4, {}), {2}: (5, {}), {3}: (6, {}), {4}... | custom-call | flops 2000000000 | bytes 2000000 | tf_op jit(solution)/shard_map/pallas_call | solution.py:900
  (86 shorter events, 22.4 us)
Async XLA Ops:
  0.7 10.9 %collective-permute-start = (bf16[256,384]{1,0:T(8,128)(2,1)}, bf16[256,384]{1,0:T(8,128)(2,1)S(1)}, u32[]{:S(2)}, u32[]{:S(2)}) collective-permute-start(bf16[256,384]{1,0:T(8,128)(2,1)} %bitcast.33), channel_id=1, source_target_pairs={{0,8},{8,0},{16,24},{24,16},{1,9},{9,1},{17,25},{25,17},{2,10},{10... | collective-permute-start | bytes 589832 | tf_op jit(solution)/shard_map/ppermute | solution.py:934
  1.4 10.2 %collective-permute-start.1 = (bf16[256,384]{1,0:T(8,128)(2,1)}, bf16[256,384]{1,0:T(8,128)(2,1)S(1)}, u32[]{:S(2)}, u32[]{:S(2)}) collective-permute-start(bf16[256,384]{1,0:T(8,128)(2,1)} %bitcast.34), channel_id=1, source_target_pairs={{0,16},{8,24},{16,0},{24,8},{1,17},{9,25},{17,1},{25,9},{2,18},{10... | collective-permute-start | bytes 589832 | tf_op jit(solution)/shard_map/ppermute | solution.py:934
  2.7 9.8 %collective-permute-start.2 = (bf16[256,384]{1,0:T(8,128)(2,1)}, bf16[256,384]{1,0:T(8,128)(2,1)S(1)}, u32[]{:S(2)}, u32[]{:S(2)}) collective-permute-start(bf16[256,384]{1,0:T(8,128)(2,1)} %bitcast.35), channel_id=1, source_target_pairs={{0,24},{8,16},{16,8},{24,0},{1,25},{9,17},{17,9},{25,1},{2,26},{10... | collective-permute-start | bytes 589832 | tf_op jit(solution)/shard_map/ppermute | solution.py:934
  29.7 8.3 %collective-permute-start.4 = (bf16[288,384]{1,0:T(8,128)(2,1)S(1)}, bf16[288,384]{1,0:T(8,128)(2,1)S(1)}, u32[]{:S(2)}, u32[]{:S(2)}) collective-permute-start(bf16[288,384]{1,0:T(8,128)(2,1)S(1)} %get-tuple-element.115.refs_3_.refs_8_), channel_id=1, source_target_pairs={{0,16},{8,24},{16,0},{24,8},{1,17},{9,25},{17,1},{25,9},{2,18},{10... | collective-permute-start | bytes 663560 | tf_op jit(solution)/shard_map/ppermute | solution.py:934
  30.9 9.9 %collective-permute-start.3 = (bf16[288,384]{1,0:T(8,128)(2,1)S(1)}, bf16[288,384]{1,0:T(8,128)(2,1)S(1)}, u32[]{:S(2)}, u32[]{:S(2)}) collective-permute-start(bf16[288,384]{1,0:T(8,128)(2,1)S(1)} %get-tuple-element.115.refs_3_.refs_8_), channel_id=1, source_target_pairs={{0,8},{8,0},{16,24},{24,16},{1,9},{9,1},{17,25},{25,17},{2,10},{10... | collective-permute-start | bytes 663560 | tf_op jit(solution)/shard_map/ppermute | solution.py:934
  38.1 19.9 %collective-permute-start.10 = (bf16[4,112,384]{2,1,0:T(8,128)(2,1)}, bf16[4,112,384]{2,1,0:T(8,128)(2,1)}, u32[]{:S(2)}, u32[]{:S(2)}) collective-permute-start(bf16[4,112,384]{2,1,0:T(8,128)(2,1)} %get-tuple-element.194), channel_id=1, source_target_pairs={{0,17},{1,16},{2,19},{3,18},{4,21},{5,20},{6,23},{7,22},{8,25},{9,... | collective-permute-start | bytes 1032200 | tf_op jit(solution)/shard_map/ppermute | solution.py:758
  40.0 18.0 %collective-permute-start.9 = (bf16[4,112,384]{2,1,0:T(8,128)(2,1)}, bf16[4,112,384]{2,1,0:T(8,128)(2,1)}, u32[]{:S(2)}, u32[]{:S(2)}) collective-permute-start(bf16[4,112,384]{2,1,0:T(8,128)(2,1)} %get-tuple-element.195), channel_id=1, source_target_pairs={{0,1},{1,0},{2,3},{3,2},{4,5},{5,4},{6,7},{7,6},{8,9},{9,8},{10,11... | collective-permute-start | bytes 1032200 | tf_op jit(solution)/shard_map/ppermute | solution.py:758
  40.3 17.8 %collective-permute-start.8 = (bf16[4,112,384]{2,1,0:T(8,128)(2,1)S(1)}, bf16[4,112,384]{2,1,0:T(8,128)(2,1)}, u32[]{:S(2)}, u32[]{:S(2)}) collective-permute-start(bf16[4,112,384]{2,1,0:T(8,128)(2,1)S(1)} %add_convert_fusion.2), channel_id=1, source_target_pairs={{0,16},{1,17},{2,18},{3,19},{4,20},{5,21},{6,22},{7,23},{8,24},{9,... | collective-permute-start | bytes 1032200 | tf_op jit(solution)/shard_map/ppermute | solution.py:758
  56.5 5.7 %collective-permute-start.11 = (bf16[8,56,384]{2,1,0:T(8,128)(2,1)}, bf16[8,56,384]{2,1,0:T(8,128)(2,1)S(1)}, u32[]{:S(2)}, u32[]{:S(2)}) collective-permute-start(bf16[8,56,384]{2,1,0:T(8,128)(2,1)} %bitcast.32), channel_id=1, source_target_pairs={{0,8},{1,9},{2,10},{3,11},{4,12},{5,13},{6,14},{7,15},{8,0},{9,1},... | collective-permute-start | bytes 1032200 | tf_op jit(solution)/shard_map/ppermute | solution.py:758
  59.7 6.4 %collective-permute-start.18 = (bf16[1,112,384]{2,1,0:T(8,128)(2,1)S(1)}, bf16[1,112,384]{2,1,0:T(8,128)(2,1)S(1)}, u32[]{:S(2)}, u32[]{:S(2)}) collective-permute-start(bf16[1,112,384]{2,1,0:T(8,128)(2,1)S(1)} %get-tuple-element.192), channel_id=1, source_target_pairs={{0,4},{1,5},{2,6},{3,7},{4,0},{5,1},{6,2},{7,3},{8,12},{9,13},{10,... | collective-permute-start | bytes 258056 | tf_op jit(solution)/shard_map/ppermute | solution.py:758
  62.1 8.0 %collective-permute-start.19 = (bf16[1,112,384]{2,1,0:T(8,128)(2,1)S(1)}, bf16[1,112,384]{2,1,0:T(8,128)(2,1)S(1)}, u32[]{:S(2)}, u32[]{:S(2)}) collective-permute-start(bf16[1,112,384]{2,1,0:T(8,128)(2,1)S(1)} %get-tuple-element.191), channel_id=1, source_target_pairs={{0,6},{1,7},{2,4},{3,5},{4,2},{5,3},{6,0},{7,1},{8,14},{9,15},{10,... | collective-permute-start | bytes 258056 | tf_op jit(solution)/shard_map/ppermute | solution.py:758
  62.3 11.1 %collective-permute-start.12 = (bf16[4,56,384]{2,1,0:T(8,128)(2,1)S(1)}, bf16[4,56,384]{2,1,0:T(8,128)(2,1)S(1)}, u32[]{:S(2)}, u32[]{:S(2)}) collective-permute-start(bf16[4,56,384]{2,1,0:T(8,128)(2,1)S(1)} %add_convert_fusion.5), channel_id=1, source_target_pairs={{0,16},{1,17},{2,18},{3,19},{4,20},{5,21},{6,22},{7,23},{8,24},{9,... | collective-permute-start | bytes 516104 | tf_op jit(solution)/shard_map/ppermute | solution.py:758
  63.3 10.6 %collective-permute-start.14 = (bf16[4,56,384]{2,1,0:T(8,128)(2,1)S(1)}, bf16[4,56,384]{2,1,0:T(8,128)(2,1)S(1)}, u32[]{:S(2)}, u32[]{:S(2)}) collective-permute-start(bf16[4,56,384]{2,1,0:T(8,128)(2,1)S(1)} %get-tuple-element.199), channel_id=1, source_target_pairs={{0,1},{1,0},{2,3},{3,2},{4,5},{5,4},{6,7},{7,6},{8,9},{9,8},{10,11... | collective-permute-start | bytes 516104 | tf_op jit(solution)/shard_map/ppermute | solution.py:758
  64.6 9.3 %collective-permute-start.15 = (bf16[4,56,384]{2,1,0:T(8,128)(2,1)S(1)}, bf16[4,56,384]{2,1,0:T(8,128)(2,1)S(1)}, u32[]{:S(2)}, u32[]{:S(2)}) collective-permute-start(bf16[4,56,384]{2,1,0:T(8,128)(2,1)S(1)} %get-tuple-element.200), channel_id=1, source_target_pairs={{0,17},{1,16},{2,19},{3,18},{4,21},{5,20},{6,23},{7,22},{8,25},{9,... | collective-permute-start | bytes 516104 | tf_op jit(solution)/shard_map/ppermute | solution.py:758
  73.4 9.3 %collective-permute-start.22 = (bf16[1,112,384]{2,1,0:T(8,128)(2,1)S(1)}, bf16[1,112,384]{2,1,0:T(8,128)(2,1)S(1)}, u32[]{:S(2)}, u32[]{:S(2)}) collective-permute-start(bf16[1,112,384]{2,1,0:T(8,128)(2,1)S(1)} %add_convert_fusion.6), channel_id=1, source_target_pairs={{0,6},{1,7},{2,4},{3,5},{4,2},{5,3},{6,0},{7,1},{8,14},{9,15},{10,... | collective-permute-start | bytes 258056 | tf_op jit(solution)/shard_map/ppermute | solution.py:758
  74.0 8.6 %collective-permute-start.16 = (bf16[1,56,384]{2,1,0:T(8,128)(2,1)S(1)}, bf16[1,56,384]{2,1,0:T(8,128)(2,1)S(1)}, u32[]{:S(2)}, u32[]{:S(2)}) collective-permute-start(bf16[1,56,384]{2,1,0:T(8,128)(2,1)S(1)} %get-tuple-element.198), channel_id=1, source_target_pairs={{0,2},{1,3},{2,0},{3,1},{4,6},{5,7},{6,4},{7,5},{8,10},{9,11},{10,... | collective-permute-start | bytes 129032 | tf_op jit(solution)/shard_map/ppermute | solution.py:758
  75.1 10.6 %collective-permute-start.23 = (bf16[1,56,384]{2,1,0:T(8,128)(2,1)S(1)}, bf16[1,56,384]{2,1,0:T(8,128)(2,1)S(1)}, u32[]{:S(2)}, u32[]{:S(2)}) collective-permute-start(bf16[1,56,384]{2,1,0:T(8,128)(2,1)S(1)} %get-tuple-element.196), channel_id=1, source_target_pairs={{0,4},{1,5},{2,6},{3,7},{4,0},{5,1},{6,2},{7,3},{8,12},{9,13},{10,... | collective-permute-start | bytes 129032 | tf_op jit(solution)/shard_map/ppermute | solution.py:758
  76.2 9.5 %collective-permute-start.24 = (bf16[1,56,384]{2,1,0:T(8,128)(2,1)S(1)}, bf16[1,56,384]{2,1,0:T(8,128)(2,1)S(1)}, u32[]{:S(2)}, u32[]{:S(2)}) collective-permute-start(bf16[1,56,384]{2,1,0:T(8,128)(2,1)S(1)} %get-tuple-element.197), channel_id=1, source_target_pairs={{0,6},{1,7},{2,4},{3,5},{4,2},{5,3},{6,0},{7,1},{8,14},{9,15},{10,... | collective-permute-start | bytes 129032 | tf_op jit(solution)/shard_map/ppermute | solution.py:758
  83.0 10.0 %collective-permute-start.28 = (bf16[4,112,384]{2,1,0:T(8,128)(2,1)S(1)}, bf16[4,112,384]{2,1,0:T(8,128)(2,1)S(1)}, u32[]{:S(2)}, u32[]{:S(2)}) collective-permute-start(bf16[4,112,384]{2,1,0:T(8,128)(2,1)S(1)} %pad_maximum_fusion), channel_id=1, source_target_pairs={{0,16},{1,17},{2,18},{3,19},{4,20},{5,21},{6,22},{7,23},{8,24},{9,... | collective-permute-start | bytes 1032200 | tf_op jit(solution)/shard_map/ppermute | solution.py:758
  83.9 9.1 %collective-permute-start.29 = (bf16[4,112,384]{2,1,0:T(8,128)(2,1)S(1)}, bf16[4,112,384]{2,1,0:T(8,128)(2,1)S(1)}, u32[]{:S(2)}, u32[]{:S(2)}) collective-permute-start(bf16[4,112,384]{2,1,0:T(8,128)(2,1)S(1)} %pad_maximum_fusion), channel_id=1, source_target_pairs={{0,1},{1,0},{2,3},{3,2},{4,5},{5,4},{6,7},{7,6},{8,9},{9,8},{10,11... | collective-permute-start | bytes 1032200 | tf_op jit(solution)/shard_map/ppermute | solution.py:758
  85.1 12.4 %collective-permute-start.30 = (bf16[4,112,384]{2,1,0:T(8,128)(2,1)S(1)}, bf16[4,112,384]{2,1,0:T(8,128)(2,1)S(1)}, u32[]{:S(2)}, u32[]{:S(2)}) collective-permute-start(bf16[4,112,384]{2,1,0:T(8,128)(2,1)S(1)} %pad_maximum_fusion), channel_id=1, source_target_pairs={{0,17},{1,16},{2,19},{3,18},{4,21},{5,20},{6,23},{7,22},{8,25},{9,... | collective-permute-start | bytes 1032200 | tf_op jit(solution)/shard_map/ppermute | solution.py:758
  97.6 7.4 %collective-permute-start.31 = (bf16[16,112,384]{2,1,0:T(8,128)(2,1)S(1)}, bf16[16,112,384]{2,1,0:T(8,128)(2,1)S(1)}, u32[]{:S(2)}, u32[]{:S(2)}) collective-permute-start(bf16[16,112,384]{2,1,0:T(8,128)(2,1)S(1)} %constant_dynamic-update-slice_fusion), channel_id=1, source_target_pairs={{0,8},{1,9},{2,10},{3,11},{4,12},{5,13},{6,14},{7,15},{8,0},{9,1},... | collective-permute-start | bytes 4128776 | tf_op jit(solution)/shard_map/ppermute | solution.py:758
  102.3 6.6 %collective-permute-start.32 = (bf16[4,56,384]{2,1,0:T(8,128)(2,1)S(1)}, bf16[4,56,384]{2,1,0:T(8,128)(2,1)S(1)}, u32[]{:S(2)}, u32[]{:S(2)}) collective-permute-start(bf16[4,56,384]{2,1,0:T(8,128)(2,1)S(1)} %pad_maximum_fusion.1), channel_id=1, source_target_pairs={{0,16},{1,17},{2,18},{3,19},{4,20},{5,21},{6,22},{7,23},{8,24},{9,... | collective-permute-start | bytes 516104 | tf_op jit(solution)/shard_map/ppermute | solution.py:758
  104.4 8.4 %collective-permute-start.34 = (bf16[4,56,384]{2,1,0:T(8,128)(2,1)S(1)}, bf16[4,56,384]{2,1,0:T(8,128)(2,1)S(1)}, u32[]{:S(2)}, u32[]{:S(2)}) collective-permute-start(bf16[4,56,384]{2,1,0:T(8,128)(2,1)S(1)} %pad_maximum_fusion.1), channel_id=1, source_target_pairs={{0,17},{1,16},{2,19},{3,18},{4,21},{5,20},{6,23},{7,22},{8,25},{9,... | collective-permute-start | bytes 516104 | tf_op jit(solution)/shard_map/ppermute | solution.py:758
  (16 other events, 79.0 us)

commit v3 on v2

--- a/solution.py
+++ b/solution.py
@@ -449,7 +449,8 @@
         rel_key_grad_store.ref[there, :] = table_grad(table, scale)
         return carry
 
-    lax.fori_loop(first, last, pair_step, 0)
+    for pair in range(first, last):
+        pair_step(pair, 0)
 
 
 def key_kernel(

time: 118 us -> 117 us (level)
  no operation moved by 1% of the time
where the time goes in v3:
time: 117 us
  Pallas kernels  51.4 us (44%)
  starting transfers between devices  34.9 us (30%)
  waiting for transfers between devices  23.4 us (20%)
  other arithmetic  5.17 us (4%)
  between operations  1.78 us (2%)
    pallas_call x6, Pallas kernels, call(): pl.pallas_call(body, out_shape=[pltpu.VMEM(out[0], out[1]) if kept else p...  49.1 us
    ppermute x30, starting transfers between devices, send(): return lax.ppermute(values, ('blk', 'dp'), self.pairs(mask))  30.5 us
    ppermute x30, waiting for transfers between devices, send(): return lax.ppermute(values, ('blk', 'dp'), self.pairs(mask))  22.5 us
    convert_element_type x8, other arithmetic, total(): return sum((span.astype(F32) for span in spans)).astype(BF)  4.8 us
    ppermute x6, starting transfers between devices, along(): return lax.ppermute(values, 'blk', [(i, i ^ bit) for i in range(blk_count)])  4.41 us
    pallas_call x2, Pallas kernels, late_call(): pl.pallas_call(functools.partial(late_kernel, mine, shapes), out_shape=[p...  2.38 us
  transfers between devices with their start and end apart: 36, of which 9 were waited for; matrix products, arithmetic and copies ran while one was open for 5% of the time, Pallas kernels for 29%

profile of v3, /device:TPU:9, one launch (start us, length us, event | category | flops | bytes accessed | tf_op | source)
XLA Modules:
  0.0 117.1 jit_solution(4259301073726585505)
XLA Ops:
  1.4 1.3 %collective-permute-start.1 = (bf16[256,384]{1,0:T(8,128)(2,1)}, bf16[256,384]{1,0:T(8,128)(2,1)S(1)}, u32[]{:S(2)}, u32[]{:S(2)}) collective-permute-start(bf16[256,384]{1,0:T(8,128)(2,1)} %bitcast.34), channel_id=1, source_target_pairs={{0,16},{8,24},{16,0},{24,8},{1,17},{9,25},{17,1},{25,9},{2,18},{10... | collective-permute-start | bytes 589832 | tf_op jit(solution)/shard_map/ppermute | solution.py:935
  3.1 7.8 %shard_map.339 = (bf16[512,384]{1,0:T(8,128)(2,1)S(1)}, bf16[512,384]{1,0:T(8,128)(2,1)S(1)}, f32[3,512,896]{2,1,0:T(8,128)}, bf16[512,384]{1,0:T(8,128)(2,1)S(1...) custom-call(s32[1]{0:T(128)} %bitcast.refs_0_, ...), custom_call_target="tpu_custom_call" | custom-call | flops 8999999488 | bytes 9000000 | tf_op jit(solution)/shard_map/pallas_call | solution.py:721
  12.5 16.8 %shard_map.340 = (f32[256,384]{1,0:T(8,128)}, f32[256,384]{1,0:T(8,128)S(1)}, bf16[3,512,1024]{2,1,0:T(8,128)(2,1)S(1)}, bf16[288,384]{1,0:T(8,128)(2,1)S(1)}, f...) custom-call(s32[1]{0:T(128)} %bitcast.refs_0_, ...), custom_call_target="tpu_custom_call" | custom-call | flops 20000000000 | bytes 20000000 | tf_op jit(solution)/shard_map/pallas_call | solution.py:721
  29.8 1.2 %collective-permute-start.4 = (bf16[288,384]{1,0:T(8,128)(2,1)S(1)}, bf16[288,384]{1,0:T(8,128)(2,1)S(1)}, u32[]{:S(2)}, u32[]{:S(2)}) collective-permute-start(bf16[288,384]{1,0:T(8,128)(2,1)S(1)} %get-tuple-element.115.refs_3_.refs_8_), channel_id=1, source_target_pairs={{0,16},{8,24},{16,0},{24,8},{1,17},{9,25},{17,1},{25,9},{2,18},{10... | collective-permute-start | bytes 663560 | tf_op jit(solution)/shard_map/ppermute | solution.py:935
  31.6 1.7 %shard_map.341 = (bf16[256,128]{1,0:T(8,128)(2,1)S(1)}, f32[128,512]{1,0:T(8,128)S(1)}) custom-call(s32[1]{0:T(128)} %bitcast.refs_0_, bf16[512,384]{1,0:T(8,128)(2,1)S(1)} %get-tuple-element.103.refs_8_.refs_1_.refs_5_, bf16[1024,384]{1,0:T(8,128)(2,1)S(1)} %get-tuple-element.113.refs_2_.refs_6_, bf16[288,384]{1,0:T(8,128)(2,1)S(1)} %get-tuple-element.115.refs_3_.refs_8_, ...), custom_call_target="tpu_custom_call" | custom-call | flops 3000000000 | bytes 3000000 | tf_op jit(solution)/shard_map/pallas_call | solution.py:721
  34.4 3.0 %shard_map.342 = (bf16[256,256]{1,0:T(8,128)(2,1)S(1)}, f32[256,512]{1,0:T(8,128)S(1)}) custom-call(s32[1]{0:T(128)} %bitcast.refs_0_, bf16[512,384]{1,0:T(8,128)(2,1)S(1)} %get-tuple-element.103.refs_8_.refs_1_.refs_5_, bf16[1024,384]{1,0:T(8,128)(2,1)S(1)} %get-tuple-element.113.refs_2_.refs_6_, bf16[288,384]{1,0:T(8,128)(2,1)S(1)} %get-tuple-element.115.refs_3_.refs_8_, ...), custom_call_target="tpu_custom_call" | custom-call | flops 5000000000 | bytes 5000000 | tf_op jit(solution)/shard_map/pallas_call | solution.py:721
  37.7 2.2 %collective-permute-start.10 = (bf16[4,112,384]{2,1,0:T(8,128)(2,1)}, bf16[4,112,384]{2,1,0:T(8,128)(2,1)}, u32[]{:S(2)}, u32[]{:S(2)}) collective-permute-start(bf16[4,112,384]{2,1,0:T(8,128)(2,1)} %get-tuple-element.194), channel_id=1, source_target_pairs={{0,17},{1,16},{2,19},{3,18},{4,21},{5,20},{6,23},{7,22},{8,25},{9,... | collective-permute-start | bytes 1032200 | tf_op jit(solution)/shard_map/ppermute | solution.py:759
  40.3 15.9 %shard_map.343 = (f32[256,384]{1,0:T(8,128)}, bf16[448,384]{1,0:T(8,128)(2,1)}, bf16[448,384]{1,0:T(8,128)(2,1)}, bf16[896,384]{1,0:T(8,128)(2,1)}) custom-call(s32[1]{0:T(128)} %bitcast.refs_0_, s32[1]{0:T(128)S(6)} %copy.62.refs_1_, s32[1]{0:T(128)} %bitcast.1.refs_2_.refs_1_.place_ref, bf16[512,384]{1,0:T(8,128)(2,1)S(1)} %get-tuple-element.102.refs_7_.refs_3_, ...), custom_call_target="tpu_custom_call" | custom-call | flops 16999999488 | bytes 17000000 | tf_op jit(solution)/shard_map/pallas_call | solution.py:721
  56.3 1.3 %collective-permute-start.11 = (bf16[8,56,384]{2,1,0:T(8,128)(2,1)}, bf16[8,56,384]{2,1,0:T(8,128)(2,1)S(1)}, u32[]{:S(2)}, u32[]{:S(2)}) collective-permute-start(bf16[8,56,384]{2,1,0:T(8,128)(2,1)} %bitcast.32), channel_id=1, source_target_pairs={{0,8},{1,9},{2,10},{3,11},{4,12},{5,13},{6,14},{7,15},{8,0},{9,1},... | collective-permute-start | bytes 1032200 | tf_op jit(solution)/shard_map/ppermute | solution.py:759
  57.7 1.5 %add_convert_fusion.7 = (bf16[1,112,384]{2,1,0:T(8,128)(2,1)S(1)}, bf16[1,112,384]{2,1,0:T(8,128)(2,1)S(1)}, bf16[1,112,384]{2,1,0:T(8,128)(2,1)S(1)}) fusion(bf16[4,112,384]{2,1,0:T(8,128)(2,1)} %collective-permute-done.10, s32[]{:T(128)S(6)} %select_n.150, bf16[4,112,384]{2,1,0:T(8,128)(2,1)} %collective-permute-done.9, ...), kind=kLoop, calls=%fused_computation.9 | loop fusion | flops 1290240 | bytes 1548324 | tf_op jit(solution)/shard_map/convert_element_type | solution.py:804
  59.4 2.3 %collective-permute-start.18 = (bf16[1,112,384]{2,1,0:T(8,128)(2,1)S(1)}, bf16[1,112,384]{2,1,0:T(8,128)(2,1)S(1)}, u32[]{:S(2)}, u32[]{:S(2)}) collective-permute-start(bf16[1,112,384]{2,1,0:T(8,128)(2,1)S(1)} %get-tuple-element.192), channel_id=1, source_target_pairs={{0,4},{1,5},{2,6},{3,7},{4,0},{5,1},{6,2},{7,3},{8,12},{9,13},{10,... | collective-permute-start | bytes 258056 | tf_op jit(solution)/shard_map/ppermute | solution.py:759
  63.0 1.3 %collective-permute-start.14 = (bf16[4,56,384]{2,1,0:T(8,128)(2,1)S(1)}, bf16[4,56,384]{2,1,0:T(8,128)(2,1)S(1)}, u32[]{:S(2)}, u32[]{:S(2)}) collective-permute-start(bf16[4,56,384]{2,1,0:T(8,128)(2,1)S(1)} %get-tuple-element.199), channel_id=1, source_target_pairs={{0,1},{1,0},{2,3},{3,2},{4,5},{5,4},{6,7},{7,6},{8,9},{9,8},{10,11... | collective-permute-start | bytes 516104 | tf_op jit(solution)/shard_map/ppermute | solution.py:759
  65.8 3.9 %collective-permute-done.19 = bf16[1,112,384]{2,1,0:T(8,128)(2,1)S(1)} collective-permute-done((bf16[1,112,384]{2,1,0:T(8,128)(2,1)S(1)}, bf16[1,112,384]{2,1,0:T(8,128)(2,1)S(1)}, u32[]{:S(2)}, u32[]{:S(2)}) %collective-permute-start.19) | collective-permute-done | bytes 86048 | tf_op jit(solution)/shard_map/ppermute | solution.py:759
  71.0 2.1 %collective-permute-start.21 = (bf16[1,112,384]{2,1,0:T(8,128)(2,1)S(1)}, bf16[1,112,384]{2,1,0:T(8,128)(2,1)S(1)}, u32[]{:S(2)}, u32[]{:S(2)}) collective-permute-start(bf16[1,112,384]{2,1,0:T(8,128)(2,1)S(1)} %add_convert_fusion.6), channel_id=1, source_target_pairs={{0,4},{1,5},{2,6},{3,7},{4,0},{5,1},{6,2},{7,3},{8,12},{9,13},{10,... | collective-permute-start | bytes 258056 | tf_op jit(solution)/shard_map/ppermute | solution.py:759
  76.5 5.9 %collective-permute-done.22 = bf16[1,112,384]{2,1,0:T(8,128)(2,1)S(1)} collective-permute-done((bf16[1,112,384]{2,1,0:T(8,128)(2,1)S(1)}, bf16[1,112,384]{2,1,0:T(8,128)(2,1)S(1)}, u32[]{:S(2)}, u32[]{:S(2)}) %collective-permute-start.22) | collective-permute-done | bytes 86048 | tf_op jit(solution)/shard_map/ppermute | solution.py:759
  86.3 2.4 %collective-permute-start.26 = (bf16[1,56,384]{2,1,0:T(8,128)(2,1)S(1)}, bf16[1,56,384]{2,1,0:T(8,128)(2,1)S(1)}, u32[]{:S(2)}, u32[]{:S(2)}) collective-permute-start(bf16[1,56,384]{2,1,0:T(8,128)(2,1)S(1)} %add_convert_fusion.10), channel_id=1, source_target_pairs={{0,4},{1,5},{2,6},{3,7},{4,0},{5,1},{6,2},{7,3},{8,12},{9,13},{10,... | collective-permute-start | bytes 129032 | tf_op jit(solution)/shard_map/ppermute | solution.py:759
  89.5 1.3 %collective-permute-start.27 = (bf16[1,56,384]{2,1,0:T(8,128)(2,1)S(1)}, bf16[1,56,384]{2,1,0:T(8,128)(2,1)S(1)}, u32[]{:S(2)}, u32[]{:S(2)}) collective-permute-start(bf16[1,56,384]{2,1,0:T(8,128)(2,1)S(1)} %add_convert_fusion.10), channel_id=1, source_target_pairs={{0,6},{1,7},{2,4},{3,5},{4,2},{5,3},{6,0},{7,1},{8,14},{9,15},{10,... | collective-permute-start | bytes 129032 | tf_op jit(solution)/shard_map/ppermute | solution.py:759
  90.8 1.9 %collective-permute-done.27 = bf16[1,56,384]{2,1,0:T(8,128)(2,1)S(1)} collective-permute-done((bf16[1,56,384]{2,1,0:T(8,128)(2,1)S(1)}, bf16[1,56,384]{2,1,0:T(8,128)(2,1)S(1)}, u32[]{:S(2)}, u32[]{:S(2)}) %collective-permute-start.27) | collective-permute-done | bytes 43040 | tf_op jit(solution)/shard_map/ppermute | solution.py:759
  92.8 4.4 %collective-permute-done.30 = bf16[4,112,384]{2,1,0:T(8,128)(2,1)S(1)} collective-permute-done((bf16[4,112,384]{2,1,0:T(8,128)(2,1)S(1)}, bf16[4,112,384]{2,1,0:T(8,128)(2,1)S(1)}, u32[]{:S(2)}, u32[]{:S(2)}) %collective-permute-start.30) | collective-permute-done | bytes 344096 | tf_op jit(solution)/shard_map/ppermute | solution.py:759
  97.3 4.6 %collective-permute-start.31 = (bf16[16,112,384]{2,1,0:T(8,128)(2,1)S(1)}, bf16[16,112,384]{2,1,0:T(8,128)(2,1)S(1)}, u32[]{:S(2)}, u32[]{:S(2)}) collective-permute-start(bf16[16,112,384]{2,1,0:T(8,128)(2,1)S(1)} %constant_dynamic-update-slice_fusion), channel_id=1, source_target_pairs={{0,8},{1,9},{2,10},{3,11},{4,12},{5,13},{6,14},{7,15},{8,0},{9,1},... | collective-permute-start | bytes 4128776 | tf_op jit(solution)/shard_map/ppermute | solution.py:759
  102.9 1.2 %collective-permute-start.33 = (bf16[4,56,384]{2,1,0:T(8,128)(2,1)S(1)}, bf16[4,56,384]{2,1,0:T(8,128)(2,1)S(1)}, u32[]{:S(2)}, u32[]{:S(2)}) collective-permute-start(bf16[4,56,384]{2,1,0:T(8,128)(2,1)S(1)} %pad_maximum_fusion.1), channel_id=1, source_target_pairs={{0,1},{1,0},{2,3},{3,2},{4,5},{5,4},{6,7},{7,6},{8,9},{9,8},{10,11... | collective-permute-start | bytes 516104 | tf_op jit(solution)/shard_map/ppermute | solution.py:759
  104.7 3.8 %shard_map.344 = (f32[1536,384]{1,0:T(8,128)}, f32[384,1536]{1,0:T(8,128)}, f32[384,384]{1,0:T(8,128)}, f32[384]{0:T(512)}, f32[384]{0:T(512)}, /*index=5*/f32[3...) custom-call(s32[1]{0:T(128)} %bitcast.9.refs_0_.core_ref, s32[1]{0:T(128)} %bitcast.1.refs_2_.refs_1_.place_ref, ...), custom_call_target="tpu_custom_call" | custom-call | flops 4000000000 | bytes 4000000 | tf_op jit(solution)/shard_map/pallas_call | solution.py:721
  108.6 4.0 %collective-permute-done.34 = bf16[4,56,384]{2,1,0:T(8,128)(2,1)S(1)} collective-permute-done((bf16[4,56,384]{2,1,0:T(8,128)(2,1)S(1)}, bf16[4,56,384]{2,1,0:T(8,128)(2,1)S(1)}, u32[]{:S(2)}, u32[]{:S(2)}) %collective-permute-start.34) | collective-permute-done | bytes 172064 | tf_op jit(solution)/shard_map/ppermute | solution.py:759
  115.7 1.2 %shard_map.346 = (f32[384,384]{1,0:T(8,128)}, f32[384]{0:T(512)}, f32[384,384]{1,0:T(8,128)}, f32[384]{0:T(512)}, f32[384,384]{1,0:T(8,128)}, /*index=5*/f32[384]{0:T(512)}, f32[512,384]{1,0:T(8,128)}) custom-call(s32[1]{0:T(128)} %bitcast.9.refs_0_.core_ref, ...), custom_call_target="tpu_custom_call", output_to_operand_aliasing={{0}: (3, {}), {1}: (4, {}), {2}: (5, {}), {3}: (6, {}), {4}... | custom-call | flops 2000000000 | bytes 2000000 | tf_op jit(solution)/shard_map/pallas_call | solution.py:901
  (86 shorter events, 22.2 us)
Async XLA Ops:
  0.7 10.9 %collective-permute-start = (bf16[256,384]{1,0:T(8,128)(2,1)}, bf16[256,384]{1,0:T(8,128)(2,1)S(1)}, u32[]{:S(2)}, u32[]{:S(2)}) collective-permute-start(bf16[256,384]{1,0:T(8,128)(2,1)} %bitcast.33), channel_id=1, source_target_pairs={{0,8},{8,0},{16,24},{24,16},{1,9},{9,1},{17,25},{25,17},{2,10},{10... | collective-permute-start | bytes 589832 | tf_op jit(solution)/shard_map/ppermute | solution.py:935
  1.4 10.2 %collective-permute-start.1 = (bf16[256,384]{1,0:T(8,128)(2,1)}, bf16[256,384]{1,0:T(8,128)(2,1)S(1)}, u32[]{:S(2)}, u32[]{:S(2)}) collective-permute-start(bf16[256,384]{1,0:T(8,128)(2,1)} %bitcast.34), channel_id=1, source_target_pairs={{0,16},{8,24},{16,0},{24,8},{1,17},{9,25},{17,1},{25,9},{2,18},{10... | collective-permute-start | bytes 589832 | tf_op jit(solution)/shard_map/ppermute | solution.py:935
  2.7 9.8 %collective-permute-start.2 = (bf16[256,384]{1,0:T(8,128)(2,1)}, bf16[256,384]{1,0:T(8,128)(2,1)S(1)}, u32[]{:S(2)}, u32[]{:S(2)}) collective-permute-start(bf16[256,384]{1,0:T(8,128)(2,1)} %bitcast.35), channel_id=1, source_target_pairs={{0,24},{8,16},{16,8},{24,0},{1,25},{9,17},{17,9},{25,1},{2,26},{10... | collective-permute-start | bytes 589832 | tf_op jit(solution)/shard_map/ppermute | solution.py:935
  29.8 7.6 %collective-permute-start.4 = (bf16[288,384]{1,0:T(8,128)(2,1)S(1)}, bf16[288,384]{1,0:T(8,128)(2,1)S(1)}, u32[]{:S(2)}, u32[]{:S(2)}) collective-permute-start(bf16[288,384]{1,0:T(8,128)(2,1)S(1)} %get-tuple-element.115.refs_3_.refs_8_), channel_id=1, source_target_pairs={{0,16},{8,24},{16,0},{24,8},{1,17},{9,25},{17,1},{25,9},{2,18},{10... | collective-permute-start | bytes 663560 | tf_op jit(solution)/shard_map/ppermute | solution.py:935
  31.1 9.3 %collective-permute-start.3 = (bf16[288,384]{1,0:T(8,128)(2,1)S(1)}, bf16[288,384]{1,0:T(8,128)(2,1)S(1)}, u32[]{:S(2)}, u32[]{:S(2)}) collective-permute-start(bf16[288,384]{1,0:T(8,128)(2,1)S(1)} %get-tuple-element.115.refs_3_.refs_8_), channel_id=1, source_target_pairs={{0,8},{8,0},{16,24},{24,16},{1,9},{9,1},{17,25},{25,17},{2,10},{10... | collective-permute-start | bytes 663560 | tf_op jit(solution)/shard_map/ppermute | solution.py:935
  37.7 20.0 %collective-permute-start.10 = (bf16[4,112,384]{2,1,0:T(8,128)(2,1)}, bf16[4,112,384]{2,1,0:T(8,128)(2,1)}, u32[]{:S(2)}, u32[]{:S(2)}) collective-permute-start(bf16[4,112,384]{2,1,0:T(8,128)(2,1)} %get-tuple-element.194), channel_id=1, source_target_pairs={{0,17},{1,16},{2,19},{3,18},{4,21},{5,20},{6,23},{7,22},{8,25},{9,... | collective-permute-start | bytes 1032200 | tf_op jit(solution)/shard_map/ppermute | solution.py:759
  39.8 17.9 %collective-permute-start.9 = (bf16[4,112,384]{2,1,0:T(8,128)(2,1)}, bf16[4,112,384]{2,1,0:T(8,128)(2,1)}, u32[]{:S(2)}, u32[]{:S(2)}) collective-permute-start(bf16[4,112,384]{2,1,0:T(8,128)(2,1)} %get-tuple-element.195), channel_id=1, source_target_pairs={{0,1},{1,0},{2,3},{3,2},{4,5},{5,4},{6,7},{7,6},{8,9},{9,8},{10,11... | collective-permute-start | bytes 1032200 | tf_op jit(solution)/shard_map/ppermute | solution.py:759
  40.1 17.6 %collective-permute-start.8 = (bf16[4,112,384]{2,1,0:T(8,128)(2,1)S(1)}, bf16[4,112,384]{2,1,0:T(8,128)(2,1)}, u32[]{:S(2)}, u32[]{:S(2)}) collective-permute-start(bf16[4,112,384]{2,1,0:T(8,128)(2,1)S(1)} %add_convert_fusion.2), channel_id=1, source_target_pairs={{0,16},{1,17},{2,18},{3,19},{4,20},{5,21},{6,22},{7,23},{8,24},{9,... | collective-permute-start | bytes 1032200 | tf_op jit(solution)/shard_map/ppermute | solution.py:759
  59.4 6.4 %collective-permute-start.18 = (bf16[1,112,384]{2,1,0:T(8,128)(2,1)S(1)}, bf16[1,112,384]{2,1,0:T(8,128)(2,1)S(1)}, u32[]{:S(2)}, u32[]{:S(2)}) collective-permute-start(bf16[1,112,384]{2,1,0:T(8,128)(2,1)S(1)} %get-tuple-element.192), channel_id=1, source_target_pairs={{0,4},{1,5},{2,6},{3,7},{4,0},{5,1},{6,2},{7,3},{8,12},{9,13},{10,... | collective-permute-start | bytes 258056 | tf_op jit(solution)/shard_map/ppermute | solution.py:759
  61.7 8.0 %collective-permute-start.19 = (bf16[1,112,384]{2,1,0:T(8,128)(2,1)S(1)}, bf16[1,112,384]{2,1,0:T(8,128)(2,1)S(1)}, u32[]{:S(2)}, u32[]{:S(2)}) collective-permute-start(bf16[1,112,384]{2,1,0:T(8,128)(2,1)S(1)} %get-tuple-element.191), channel_id=1, source_target_pairs={{0,6},{1,7},{2,4},{3,5},{4,2},{5,3},{6,0},{7,1},{8,14},{9,15},{10,... | collective-permute-start | bytes 258056 | tf_op jit(solution)/shard_map/ppermute | solution.py:759
  62.0 11.1 %collective-permute-start.12 = (bf16[4,56,384]{2,1,0:T(8,128)(2,1)S(1)}, bf16[4,56,384]{2,1,0:T(8,128)(2,1)S(1)}, u32[]{:S(2)}, u32[]{:S(2)}) collective-permute-start(bf16[4,56,384]{2,1,0:T(8,128)(2,1)S(1)} %add_convert_fusion.5), channel_id=1, source_target_pairs={{0,16},{1,17},{2,18},{3,19},{4,20},{5,21},{6,22},{7,23},{8,24},{9,... | collective-permute-start | bytes 516104 | tf_op jit(solution)/shard_map/ppermute | solution.py:759
  63.0 10.6 %collective-permute-start.14 = (bf16[4,56,384]{2,1,0:T(8,128)(2,1)S(1)}, bf16[4,56,384]{2,1,0:T(8,128)(2,1)S(1)}, u32[]{:S(2)}, u32[]{:S(2)}) collective-permute-start(bf16[4,56,384]{2,1,0:T(8,128)(2,1)S(1)} %get-tuple-element.199), channel_id=1, source_target_pairs={{0,1},{1,0},{2,3},{3,2},{4,5},{5,4},{6,7},{7,6},{8,9},{9,8},{10,11... | collective-permute-start | bytes 516104 | tf_op jit(solution)/shard_map/ppermute | solution.py:759
  64.3 9.3 %collective-permute-start.15 = (bf16[4,56,384]{2,1,0:T(8,128)(2,1)S(1)}, bf16[4,56,384]{2,1,0:T(8,128)(2,1)S(1)}, u32[]{:S(2)}, u32[]{:S(2)}) collective-permute-start(bf16[4,56,384]{2,1,0:T(8,128)(2,1)S(1)} %get-tuple-element.200), channel_id=1, source_target_pairs={{0,17},{1,16},{2,19},{3,18},{4,21},{5,20},{6,23},{7,22},{8,25},{9,... | collective-permute-start | bytes 516104 | tf_op jit(solution)/shard_map/ppermute | solution.py:759
  73.1 9.3 %collective-permute-start.22 = (bf16[1,112,384]{2,1,0:T(8,128)(2,1)S(1)}, bf16[1,112,384]{2,1,0:T(8,128)(2,1)S(1)}, u32[]{:S(2)}, u32[]{:S(2)}) collective-permute-start(bf16[1,112,384]{2,1,0:T(8,128)(2,1)S(1)} %add_convert_fusion.6), channel_id=1, source_target_pairs={{0,6},{1,7},{2,4},{3,5},{4,2},{5,3},{6,0},{7,1},{8,14},{9,15},{10,... | collective-permute-start | bytes 258056 | tf_op jit(solution)/shard_map/ppermute | solution.py:759
  73.7 8.6 %collective-permute-start.16 = (bf16[1,56,384]{2,1,0:T(8,128)(2,1)S(1)}, bf16[1,56,384]{2,1,0:T(8,128)(2,1)S(1)}, u32[]{:S(2)}, u32[]{:S(2)}) collective-permute-start(bf16[1,56,384]{2,1,0:T(8,128)(2,1)S(1)} %get-tuple-element.198), channel_id=1, source_target_pairs={{0,2},{1,3},{2,0},{3,1},{4,6},{5,7},{6,4},{7,5},{8,10},{9,11},{10,... | collective-permute-start | bytes 129032 | tf_op jit(solution)/shard_map/ppermute | solution.py:759
  74.8 10.6 %collective-permute-start.23 = (bf16[1,56,384]{2,1,0:T(8,128)(2,1)S(1)}, bf16[1,56,384]{2,1,0:T(8,128)(2,1)S(1)}, u32[]{:S(2)}, u32[]{:S(2)}) collective-permute-start(bf16[1,56,384]{2,1,0:T(8,128)(2,1)S(1)} %get-tuple-element.196), channel_id=1, source_target_pairs={{0,4},{1,5},{2,6},{3,7},{4,0},{5,1},{6,2},{7,3},{8,12},{9,13},{10,... | collective-permute-start | bytes 129032 | tf_op jit(solution)/shard_map/ppermute | solution.py:759
  75.9 9.5 %collective-permute-start.24 = (bf16[1,56,384]{2,1,0:T(8,128)(2,1)S(1)}, bf16[1,56,384]{2,1,0:T(8,128)(2,1)S(1)}, u32[]{:S(2)}, u32[]{:S(2)}) collective-permute-start(bf16[1,56,384]{2,1,0:T(8,128)(2,1)S(1)} %get-tuple-element.197), channel_id=1, source_target_pairs={{0,6},{1,7},{2,4},{3,5},{4,2},{5,3},{6,0},{7,1},{8,14},{9,15},{10,... | collective-permute-start | bytes 129032 | tf_op jit(solution)/shard_map/ppermute | solution.py:759
  82.7 10.0 %collective-permute-start.28 = (bf16[4,112,384]{2,1,0:T(8,128)(2,1)S(1)}, bf16[4,112,384]{2,1,0:T(8,128)(2,1)S(1)}, u32[]{:S(2)}, u32[]{:S(2)}) collective-permute-start(bf16[4,112,384]{2,1,0:T(8,128)(2,1)S(1)} %pad_maximum_fusion), channel_id=1, source_target_pairs={{0,16},{1,17},{2,18},{3,19},{4,20},{5,21},{6,22},{7,23},{8,24},{9,... | collective-permute-start | bytes 1032200 | tf_op jit(solution)/shard_map/ppermute | solution.py:759
  83.6 9.1 %collective-permute-start.29 = (bf16[4,112,384]{2,1,0:T(8,128)(2,1)S(1)}, bf16[4,112,384]{2,1,0:T(8,128)(2,1)S(1)}, u32[]{:S(2)}, u32[]{:S(2)}) collective-permute-start(bf16[4,112,384]{2,1,0:T(8,128)(2,1)S(1)} %pad_maximum_fusion), channel_id=1, source_target_pairs={{0,1},{1,0},{2,3},{3,2},{4,5},{5,4},{6,7},{7,6},{8,9},{9,8},{10,11... | collective-permute-start | bytes 1032200 | tf_op jit(solution)/shard_map/ppermute | solution.py:759
  84.8 12.4 %collective-permute-start.30 = (bf16[4,112,384]{2,1,0:T(8,128)(2,1)S(1)}, bf16[4,112,384]{2,1,0:T(8,128)(2,1)S(1)}, u32[]{:S(2)}, u32[]{:S(2)}) collective-permute-start(bf16[4,112,384]{2,1,0:T(8,128)(2,1)S(1)} %pad_maximum_fusion), channel_id=1, source_target_pairs={{0,17},{1,16},{2,19},{3,18},{4,21},{5,20},{6,23},{7,22},{8,25},{9,... | collective-permute-start | bytes 1032200 | tf_op jit(solution)/shard_map/ppermute | solution.py:759
  97.3 7.4 %collective-permute-start.31 = (bf16[16,112,384]{2,1,0:T(8,128)(2,1)S(1)}, bf16[16,112,384]{2,1,0:T(8,128)(2,1)S(1)}, u32[]{:S(2)}, u32[]{:S(2)}) collective-permute-start(bf16[16,112,384]{2,1,0:T(8,128)(2,1)S(1)} %constant_dynamic-update-slice_fusion), channel_id=1, source_target_pairs={{0,8},{1,9},{2,10},{3,11},{4,12},{5,13},{6,14},{7,15},{8,0},{9,1},... | collective-permute-start | bytes 4128776 | tf_op jit(solution)/shard_map/ppermute | solution.py:759
  102.0 6.6 %collective-permute-start.32 = (bf16[4,56,384]{2,1,0:T(8,128)(2,1)S(1)}, bf16[4,56,384]{2,1,0:T(8,128)(2,1)S(1)}, u32[]{:S(2)}, u32[]{:S(2)}) collective-permute-start(bf16[4,56,384]{2,1,0:T(8,128)(2,1)S(1)} %pad_maximum_fusion.1), channel_id=1, source_target_pairs={{0,16},{1,17},{2,18},{3,19},{4,20},{5,21},{6,22},{7,23},{8,24},{9,... | collective-permute-start | bytes 516104 | tf_op jit(solution)/shard_map/ppermute | solution.py:759
  102.9 5.7 %collective-permute-start.33 = (bf16[4,56,384]{2,1,0:T(8,128)(2,1)S(1)}, bf16[4,56,384]{2,1,0:T(8,128)(2,1)S(1)}, u32[]{:S(2)}, u32[]{:S(2)}) collective-permute-start(bf16[4,56,384]{2,1,0:T(8,128)(2,1)S(1)} %pad_maximum_fusion.1), channel_id=1, source_target_pairs={{0,1},{1,0},{2,3},{3,2},{4,5},{5,4},{6,7},{7,6},{8,9},{9,8},{10,11... | collective-permute-start | bytes 516104 | tf_op jit(solution)/shard_map/ppermute | solution.py:759
  104.1 8.4 %collective-permute-start.34 = (bf16[4,56,384]{2,1,0:T(8,128)(2,1)S(1)}, bf16[4,56,384]{2,1,0:T(8,128)(2,1)S(1)}, u32[]{:S(2)}, u32[]{:S(2)}) collective-permute-start(bf16[4,56,384]{2,1,0:T(8,128)(2,1)S(1)} %pad_maximum_fusion.1), channel_id=1, source_target_pairs={{0,17},{1,16},{2,19},{3,18},{4,21},{5,20},{6,23},{7,22},{8,25},{9,... | collective-permute-start | bytes 516104 | tf_op jit(solution)/shard_map/ppermute | solution.py:759
  (16 other events, 79.0 us)
